TPU v7x, 128 devices: a whole 4x4x4 slice. The times are simulated.
128 devices in a mesh: wide: 16 (over y, z_hi, core), local: 8 (over x, z_lo).
Axes of the slice: x: 4, y: 4, z: 4 (z_hi: 2, z_lo: 2; z = z_hi * 2 + z_lo), core: 2. Of those that a mesh axis runs over, the one named last changes fastest.
Arguments:
- grad_out: bfloat16 [16384, 2080], P(('wide', 'local')), may hold values from -6 to 6
- expert_id: int32 [16384], P(('wide', 'local')), may hold values from 0 to 15, as said below
- slot: int32 [16384], P(('wide', 'local')), may hold values from -1 to 7, as said below
- gate_prob: float32 [16384], P(('wide', 'local')), may hold values from 0.1 to 1
- saved_inputs: bfloat16 [16, 16, 64, 2080], P('wide', None, 'local'), may hold values from -6 to 6
- w_in: bfloat16 [16, 2080, 6144], P('wide', None, 'local'), may hold values from -0.125 to 0.125
- w_out: bfloat16 [16, 6144, 2080], P('wide', 'local'), may hold values from -0.078125 to 0.078125
Outputs:
- grad_tokens: bfloat16 [16384, 2080], P(('wide', 'local'))
- grad_in_weight: bfloat16 [16, 2080, 6144], P('wide', None, 'local')
- grad_out_weight: bfloat16 [16, 6144, 2080], P('wide', 'local')
Inputs may be any that keep to these rules, and one draw needn't show every extreme that they name: `expert_id`: the expert each token chose. `slot`: the position of a token among the tokens of its device that chose the same expert, in token order, or -1 where that position is 8 or more. In every draw one expert, common to all devices, fills all 8 of its slots from every device.
All inputs are finite; a program needn't handle non-finite values.
Results may differ from a plain program's by a relative error of at most 0.014.
Values may be sent and summed in bfloat16 or wider, within the bound.
No kernel may reach another device: no remote copies, remote signals or barrier semaphores. Data moves between devices by JAX's collectives and lax.ppermute only.
A program may use at most 128 MiB of HBM per device.

v0:
```python
import jax
import jax.numpy as jnp
from jax import lax
from jax.sharding import PartitionSpec as P


def gelu_parts(value):
    normal_cdf = 0.5 * (1.0 + lax.erf(value * 0.7071067811865476))
    density = jnp.exp(-0.5 * value * value) * 0.3989422804014327
    return (value * normal_cdf, normal_cdf + value * density)


def contract(left, right, left_dim, right_dim):
    return lax.dot_general(
        left, right, (((left_dim,), (right_dim,)), ((), ())), preferred_element_type=jnp.float32
    )


def per_device(grad_out, expert_id, slot, gate_prob, saved_inputs, w_in, w_out):
    groups = lax.axis_size("wide")
    shards = lax.axis_size("local")
    capacity = saved_inputs.shape[2]
    width = grad_out.shape[1]
    kept = slot >= 0
    target = expert_id * capacity + slot
    columns = jnp.arange(groups * capacity, dtype=jnp.int32)
    placing = ((target[:, None] == columns[None, :]) & kept[:, None]).astype(jnp.bfloat16)
    scaled = (gate_prob[:, None] * grad_out.astype(jnp.float32)).astype(jnp.bfloat16)
    outgoing = contract(placing, scaled, 0, 0).astype(jnp.bfloat16).reshape(groups, capacity, width)
    inputs = lax.all_gather(saved_inputs[0], "local", axis=1, tiled=True)
    rows = inputs.reshape(-1, width)
    copies = jnp.broadcast_to(outgoing[:, None], (groups, shards, capacity, width))
    copies = copies.reshape(groups * shards, capacity, width)
    arrived = lax.all_to_all(copies, ("wide", "local"), split_axis=0, concat_axis=0, tiled=True)
    grads = arrived.reshape(-1, width)
    first = w_in[0]
    second = w_out[0]
    pre = jnp.dot(rows, first, preferred_element_type=jnp.float32)
    value, slope = gelu_parts(pre)
    hidden = value.astype(jnp.bfloat16)
    back = contract(grads, second, 1, 1)
    dhidden = (back * slope).astype(jnp.bfloat16)
    partial_value = contract(dhidden, first, 1, 1)
    grad_out_weight = contract(hidden, grads, 0, 0).astype(jnp.bfloat16)[None]
    grad_in_weight = contract(rows, dhidden, 0, 0).astype(jnp.bfloat16)[None]
    pieces = partial_value.astype(jnp.bfloat16).reshape(groups * shards, capacity, width)
    came_back = lax.all_to_all(pieces, ("wide", "local"), split_axis=0, concat_axis=0, tiled=True)
    summed = jnp.sum(came_back.astype(jnp.float32).reshape(groups, shards, capacity, width), axis=1)
    returned = summed.astype(jnp.bfloat16)
    collected = returned.reshape(groups * capacity, width)
    grad_tokens = jnp.dot(placing, collected, preferred_element_type=jnp.float32).astype(
        jnp.bfloat16
    )
    return (grad_tokens, grad_in_weight, grad_out_weight)


def solution(mesh):
    placed = (
        P(("wide", "local"), None),
        P(("wide", "local")),
        P(("wide", "local")),
        P(("wide", "local")),
        P("wide", None, "local", None),
        P("wide", None, "local"),
        P("wide", "local", None),
    )
    return jax.shard_map(
        per_device,
        mesh=mesh,
        in_specs=placed,
        out_specs=(P(("wide", "local"), None), P("wide", None, "local"), P("wide", "local", None)),
        check_vma=False,
    )
```

profile of v0, /device:TPU:1, one launch (start us, length us, event | category | flops | bytes accessed | tf_op | source)
XLA Modules:
  0.0 261.8 jit_solution(3616839179324590676)
XLA Ops:
  7.2 0.0 copy-start
  7.2 0.0 all-gather.3.cloned.1.call-start
  7.2 0.7 all-gather.3.cloned.1.call-update
  7.9 0.9 broadcast_compare_fusion
  8.8 0.7 multiply_add_fusion
  9.5 2.2 convolution_convert_fusion.4
  11.7 2.1 copy.11
  13.8 3.5 %broadcast_in_dim.18 = bf16[16,8,8,2080]{3,2,1,0:T(8,128)(2,1)} broadcast(bf16[16,8,2080]{2,1,0:T(8,128)(2,1)} %bitcast.38), dimensions={0,2,3} | broadcast | bytes 4792320 | tf_op jit(solution)/shard_map/broadcast_in_dim | solution.py:32
  17.3 11.9 %all-to-all-start = ((bf16[128,8,2080]{2,1,0:T(8,128)(2,1)}), bf16[128,8,2080]{2,1,0:T(8,128)(2,1)}, u32[]{:S(2)}, u32[]{:S(2)}) async-start(bf16[128,8,2080]{2,1,0:T(8,128)(2,1)} %bitcast.37), calls=%async_computation | async-start | bytes 8912896 | tf_op jit(solution)/shard_map/all_to_all | solution.py:34
  29.2 126.7 %all-gather.3.cloned.1.call-done = bf16[1,16,64,2080]{3,2,1,0:T(8,128)(2,1)} async-done(((bf16[1,16,8,2080]{3,2,1,0:T(8,128)(2,1)}), bf16[1,16,64,2080]{3,2,1,0:T(8,128)(2,1)}) %all-gather.3.cloned.1.call-update) | async-done | bytes 4259856 | tf_op jit(solution)/shard_map/all_gather | solution.py:30
  155.9 0.0 copy-done
  155.9 7.7 %fusion.6 = f32[1024,768]{1,0:T(8,128)} fusion(bf16[1024,2080]{1,0:T(8,128)(2,1)} %bitcast.39, bf16[1,2080,768]{2,1,0:T(8,128)(2,1)S(1)} %copy-done), kind=kOutput, calls=%fused_computation.13 | convolution fusion | flops 3271557120 | bytes 10600448 | tf_op jit(solution)/shard_map/dot_general | solution.py:38
  163.6 0.0 all-to-all-done
  163.6 8.5 %fusion.14 = bf16[1024,768]{1,0:T(8,128)(2,1)S(1)} fusion(f32[1024,768]{1,0:T(8,128)} %fusion.6, bf16[1,768,2080]{1,2,0:T(8,128)(2,1)} %param.13, bf16[128,8,2080]{2,1,0:T(8,128)(2,1)} %all-to-all-done), kind=kOutput, calls=%fused_computation.21 | convolution fusion | flops 3279421440 | bytes 12173312 | tf_op jit(solution)/shard_map/dot_general | solution.py:14
  172.1 0.0 copy-start.2
  172.1 1.2 copy-done.2
  173.3 5.0 %convolution_convert_fusion = bf16[1024,2080]{0,1:T(8,128)(2,1)} fusion(bf16[1024,768]{1,0:T(8,128)(2,1)S(1)} %fusion.14, bf16[1,2080,768]{2,1,0:T(8,128)(2,1)S(1)} %copy-done), kind=kOutput, calls=%fused_computation | convolution fusion | flops 3273687040 | bytes 9027584 | tf_op jit(solution)/shard_map/dot_general | solution.py:14
  178.3 6.4 %copy.12 = bf16[1024,2080]{1,0:T(8,128)(2,1)} copy(bf16[1024,2080]{0,1:T(8,128)(2,1)} %convolution_convert_fusion) | data formatting | bytes 8519680 | tf_op jit(solution)/shard_map/convert_element_type | solution.py:46
  184.7 11.1 %all-to-all-start.1 = ((bf16[128,8,2080]{2,1,0:T(8,128)(2,1)}), bf16[128,8,2080]{2,1,0:T(8,128)(2,1)}, u32[]{:S(2)}, u32[]{:S(2)}) async-start(bf16[128,8,2080]{2,1,0:T(8,128)(2,1)} %bitcast.36), calls=%async_computation.1 | async-start | bytes 8912896 | tf_op jit(solution)/shard_map/all_to_all | solution.py:47
  195.8 0.0 copy-start.1
  195.8 8.1 %fusion = bf16[1,2080,768]{2,1,0:T(8,128)(2,1)} fusion(bf16[1024,768]{1,0:T(8,128)(2,1)} %copy-done.2, bf16[1024,2080]{1,0:T(8,128)(2,1)} %bitcast.40), kind=kOutput, calls=%fused_computation.4 | convolution fusion | flops 3273154560 | bytes 9027584 | tf_op jit(solution)/shard_map/dot_general | solution.py:14
  203.9 0.0 copy-done.1
  203.9 7.6 %fusion.1 = bf16[1,768,2080]{1,2,0:T(8,128)(2,1)} fusion(bf16[128,8,2080]{2,1,0:T(8,128)(2,1)} %all-to-all-done, f32[1024,768]{1,0:T(8,128)S(1)} %copy-done.1), kind=kOutput, calls=%fused_computation.5 | convolution fusion | flops 3277086720 | bytes 10600448 | tf_op jit(solution)/shard_map/dot_general | solution.py:14
  211.5 39.4 %all-to-all-done.1 = bf16[128,8,2080]{2,1,0:T(8,128)(2,1)} async-done(((bf16[128,8,2080]{2,1,0:T(8,128)(2,1)}), bf16[128,8,2080]{2,1,0:T(8,128)(2,1)}, u32[]{:S(2)}, u32[]{:S(2)}) %all-to-all-start.1) | async-done | bytes 4259872 | tf_op jit(solution)/shard_map/all_to_all | solution.py:47
  250.9 2.9 %bitcast_reduce_fusion = bf16[16,8,2080]{2,1,0:T(8,128)(2,1)S(1)} fusion(bf16[128,8,2080]{2,1,0:T(8,128)(2,1)} %all-to-all-done.1), kind=kLoop, calls=%fused_computation.6 | loop fusion | flops 1863680 | bytes 4792320 | tf_op jit(solution)/shard_map/reduce_sum | solution.py:48
  253.8 1.2 convolution_convert_fusion.3
Async XLA Ops:
  7.2 148.7 %copy-start = (bf16[1,2080,768]{2,1,0:T(8,128)(2,1)S(1)}, bf16[1,2080,768]{2,1,0:T(8,128)(2,1)}, u32[]{:S(2)}) copy-start(bf16[1,2080,768]{2,1,0:T(8,128)(2,1)} %param.12) | copy-start | bytes 9584644
  7.2 148.7 %all-gather.3.cloned.1.call-start = ((), (), s32[]{:S(2)}) async-start(), calls=%async_computation.2 | async-start | bytes 5013504 | tf_op jit(solution)/shard_map/all_gather | solution.py:30
  17.3 146.4 %all-to-all-start = ((bf16[128,8,2080]{2,1,0:T(8,128)(2,1)}), bf16[128,8,2080]{2,1,0:T(8,128)(2,1)}, u32[]{:S(2)}, u32[]{:S(2)}) async-start(bf16[128,8,2080]{2,1,0:T(8,128)(2,1)} %bitcast.37), calls=%async_computation | async-start | bytes 8912896 | tf_op jit(solution)/shard_map/all_to_all | solution.py:34
  172.1 1.2 copy-start.2
  184.7 66.2 %all-to-all-start.1 = ((bf16[128,8,2080]{2,1,0:T(8,128)(2,1)}), bf16[128,8,2080]{2,1,0:T(8,128)(2,1)}, u32[]{:S(2)}, u32[]{:S(2)}) async-start(bf16[128,8,2080]{2,1,0:T(8,128)(2,1)} %bitcast.36), calls=%async_computation.1 | async-start | bytes 8912896 | tf_op jit(solution)/shard_map/all_to_all | solution.py:47
  195.8 8.1 %copy-start.1 = (f32[1024,768]{1,0:T(8,128)S(1)}, f32[1024,768]{1,0:T(8,128)}, u32[]{:S(2)}) copy-start(f32[1024,768]{1,0:T(8,128)} %fusion.6) | copy-start | bytes 9437188
Sparse Core Ops, SparseCore 0:
  9.7 146.1 all-gather.2
where the time goes:
time: 263 us; the launch traced here: 262 us
  waiting for transfers between devices  167 us (63%)
  matrix products  40.4 us (15%)
  starting transfers between devices  23 us (9%)
  between operations  14.1 us (5%)
  local copies, waits for them, and re-layouts  13.2 us (5%)
  other arithmetic  4.42 us (2%)
    all_gather x1, waiting for transfers between devices, per_device(): inputs = lax.all_gather(saved_inputs[0], 'local', axis=1, tiled=True)  127 us
    all_to_all x1, waiting for transfers between devices, per_device(): lax.all_to_all(pieces, ('wide', 'local'), split_axis=0, concat_axis=0, ti...  39.4 us
    dot_general x5, matrix products, contract(): lax.dot_general(left, right, (((left_dim,), (right_dim,)), ((), ())), pre...  31.4 us
    all_to_all x1, starting transfers between devices, per_device(): lax.all_to_all(copies, ('wide', 'local'), split_axis=0, concat_axis=0, ti...  11.9 us
    all_to_all x1, starting transfers between devices, per_device(): lax.all_to_all(pieces, ('wide', 'local'), split_axis=0, concat_axis=0, ti...  11.1 us
    dot_general x1, matrix products, per_device(): pre = jnp.dot(rows, first, preferred_element_type=jnp.float32)  7.74 us
    convert_element_type x1, local copies, waits for them, and re-layouts, per_device(): partial_value.astype(jnp.bfloat16).reshape(groups * shards, capacity, width)  6.38 us
  transfers between devices with their start and end apart: 3, of which 2 were waited for; matrix products, arithmetic and copies ran while one was open for 13% of the time, Pallas kernels for 0%

commit v1 on v0

v1 whole, which is shorter than its diff:
```python
import jax
import jax.numpy as jnp
from jax import lax
from jax.experimental import pallas as pl
from jax.experimental.pallas import tpu as pltpu
from jax.sharding import Mesh, PartitionSpec as P

AXES = ("y", "zh", "core", "x", "zl")
EXCHANGE = ("core", "zl", "y", "zh")
RIGHT = [(i, (i + 1) % 4) for i in range(4)]
LEFT = [(i, (i - 1) % 4) for i in range(4)]
SWAP = [(0, 1), (1, 0)]
BF = jnp.bfloat16
F32 = jnp.float32
VMEM = pl.BlockSpec(memory_space=pltpu.VMEM)
ANY = pl.BlockSpec(memory_space=pl.ANY)
PARAMS = pltpu.CompilerParams(vmem_limit_bytes=50 * 1024 * 1024)


def dot(a, b, da, db):
    return lax.dot_general(a, b, (((da,), (db,)), ((), ())), preferred_element_type=F32)


def cost(flops, nbytes):
    return pl.CostEstimate(flops=flops, bytes_accessed=nbytes, transcendentals=0)


def placing_of(expert, slot):
    target = (expert % 2) * 64 + (expert // 2) * 8 + slot
    target = jnp.where(slot >= 0, target, -1)
    columns = lax.broadcasted_iota(jnp.int32, (128, 128), 0)
    return jnp.where(columns == target, 1.0, 0.0).astype(BF)


def prepare_kernel(grad_ref, expert_ref, slot_ref, gate_ref, saved_ref, out_ref, own_ref):
    scaled = (gate_ref[...] * grad_ref[...].astype(F32)).astype(BF)
    placing = placing_of(expert_ref[...], slot_ref[...])
    outgoing = dot(placing, scaled, 1, 1).astype(BF)
    for core in range(2):
        for copy in range(2):
            out_ref[pl.ds(core * 128 + copy * 64, 64), :] = outgoing[core * 64 : core * 64 + 64]
    to = lax.broadcasted_iota(jnp.int32, (128, 128), 0)
    source = ((to % 64) // 8) * 16 + (to // 64) * 8 + to % 8
    columns = lax.broadcasted_iota(jnp.int32, (128, 128), 1)
    order = jnp.where(columns == source, 1.0, 0.0).astype(BF)
    own_ref[...] = dot(order, saved_ref[...], 1, 0).astype(BF)


def prepare(grad_t, expert, slot, gate, saved):
    width = saved.shape[1]
    return pl.pallas_call(
        prepare_kernel,
        out_shape=(jax.ShapeDtypeStruct((256, width), BF), jax.ShapeDtypeStruct((128, width), BF)),
        in_specs=[VMEM] * 5,
        out_specs=(VMEM, VMEM),
        compiler_params=PARAMS,
        cost_estimate=cost(2 * 2 * 128 * 128 * width, 5 * 128 * width * 2),
        name="prepare",
    )(grad_t, expert, slot, gate, saved)


def gelu_parts(value):
    normal_cdf = 0.5 * (1.0 + lax.erf(value * 0.7071067811865476))
    density = jnp.exp(-0.5 * value * value) * 0.3989422804014327
    return value * normal_cdf, normal_cdf + value * density


def forward_kernel(z_ref, own, lft, rgt, far0, far1, zown, zlft, zrgt, zfar0, zfar1, w_ref,
                   rows_ref, hidden_ref, slope_ref, sems):
    z = z_ref[0]
    copies = []

    def load(src, part, rel, here):
        zl = z if here else 1 - z
        start = pl.multiple_of(part * 512 + rel * 128 + zl * 64, 64)
        copies.append(pltpu.make_async_copy(src, rows_ref.at[pl.ds(start, 64), :], sems.at[len(copies)]))

    for part in range(2):
        for rel, (mine, other) in enumerate(((own, zown), (lft, zlft), (rgt, zrgt))):
            load(mine.at[pl.ds(part * 64, 64), :], part, rel, True)
            load(other.at[pl.ds(part * 64, 64), :], part, rel, False)
        load((far0, far1)[part], part, 3, True)
        load((zfar0, zfar1)[part], part, 3, False)
    for copy in copies:
        copy.start()
    for part in range(2):
        for copy in copies[part * 8 : part * 8 + 8]:
            copy.wait()
        for block in range(2):
            at = pl.ds(part * 512 + block * 256, 256)
            pre = dot(rows_ref[at, :], w_ref[...], 1, 0)
            value, slope = gelu_parts(pre)
            hidden_ref[at, :] = value.astype(BF)
            slope_ref[at, :] = slope


def forward(z, pieces, w_in):
    width, units = w_in.shape
    return pl.pallas_call(
        forward_kernel,
        out_shape=(
            jax.ShapeDtypeStruct((1024, width), BF),
            jax.ShapeDtypeStruct((1024, units), BF),
            jax.ShapeDtypeStruct((1024, units), F32),
        ),
        in_specs=[pl.BlockSpec(memory_space=pltpu.SMEM)] + [ANY] * 10 + [VMEM],
        out_specs=(VMEM, VMEM, VMEM),
        scratch_shapes=[pltpu.SemaphoreType.DMA((16,))],
        compiler_params=PARAMS,
        cost_estimate=cost(2 * 1024 * width * units, 20 << 20),
        name="forward",
    )(z, *pieces, w_in)


def backward_kernel(own, lft, rgt, far0, far1, slope_ref, wo_ref, wi_ref,
                    rows_ref, dhidden_ref, pown, plft, prgt, pfar0, pfar1, sems):
    copies = []
    sources = ((own, 0, 128), (lft, 128, 128), (rgt, 256, 128), (far0, 384, 64), (far1, 448, 64))
    for src, start, size in sources:
        copies.append(pltpu.make_async_copy(src, rows_ref.at[pl.ds(start, size), :], sems.at[len(copies)]))
    for copy in copies:
        copy.start()
    for copy in copies:
        copy.wait()
    for block in (1, 0):
        at = pl.ds(block * 256, 256)
        back = dot(rows_ref[at, :], wo_ref[...], 1, 0)
        dhidden = (back * slope_ref[at, :]).astype(BF)
        dhidden_ref[at, :] = dhidden
        partial_value = dot(dhidden, wi_ref[...], 1, 1).astype(BF)
        if block == 1:
            prgt[...] = partial_value[:128]
            pfar0[...] = partial_value[128:192]
            pfar1[...] = partial_value[192:]
        else:
            pown[...] = partial_value[:128]
            plft[...] = partial_value[128:]


def backward(part, pieces, slope, w_out_t, w_in):
    width, units = w_in.shape
    whole = lambda shape: pl.BlockSpec(shape, lambda i: (0, 0))
    return pl.pallas_call(
        backward_kernel,
        grid=(1,),
        out_shape=tuple(
            jax.ShapeDtypeStruct(s, BF)
            for s in ((512, width), (512, units)) + ((128, width),) * 3 + ((64, width),) * 2
        ),
        in_specs=[ANY] * 5
        + [
            pl.BlockSpec((512, units), lambda i: (part, 0)),
            whole((width, units)),
            whole((width, units)),
        ],
        out_specs=tuple(
            whole(s) for s in ((512, width), (512, units)) + ((128, width),) * 3 + ((64, width),) * 2
        ),
        scratch_shapes=[pltpu.SemaphoreType.DMA((5,))],
        compiler_params=PARAMS,
        cost_estimate=cost(2 * 2 * 512 * width * units, 14 << 20),
        name="backward",
    )(*pieces, slope, w_out_t, w_in)


def middle_kernel(right_ref, left_ref, far0_ref, far1_ref, right_out, left_out):
    right_out[...] = (right_ref[...].astype(F32) + far0_ref[...].astype(F32)).astype(BF)
    left_out[...] = (left_ref[...].astype(F32) + far1_ref[...].astype(F32)).astype(BF)


def middle(to_right, to_left, far0, far1):
    width = far0.shape[1]
    return pl.pallas_call(
        middle_kernel,
        grid=(1,),
        out_shape=(jax.ShapeDtypeStruct((128, width), BF),) * 2,
        in_specs=[
            pl.BlockSpec((64, width), lambda i: (0, 0)),
            pl.BlockSpec((64, width), lambda i: (1, 0)),
            pl.BlockSpec((64, width), lambda i: (0, 0)),
            pl.BlockSpec((64, width), lambda i: (0, 0)),
        ],
        out_specs=(
            pl.BlockSpec((64, width), lambda i: (0, 0)),
            pl.BlockSpec((64, width), lambda i: (1, 0)),
        ),
        input_output_aliases={0: 0, 1: 1},
        compiler_params=PARAMS,
        cost_estimate=cost(128 * width, 6 * 64 * width * 2),
        name="middle",
    )(to_right, to_left, far0, far1)


def total_kernel(own0, lft0, rgt0, own1, lft1, rgt1, out_ref):
    for part, (own, lft, rgt) in enumerate(((own0, lft0, rgt0), (own1, lft1, rgt1))):
        value = own[...].astype(F32) + lft[...].astype(F32) + rgt[...].astype(F32)
        out_ref[pl.ds(part * 128, 128), :] = value.astype(BF)


def total(parts):
    width = parts[0].shape[1]
    return pl.pallas_call(
        total_kernel,
        out_shape=jax.ShapeDtypeStruct((256, width), BF),
        in_specs=[VMEM] * 6,
        out_specs=VMEM,
        compiler_params=PARAMS,
        cost_estimate=cost(4 * 128 * width, 8 * 128 * width * 2),
        name="total",
    )(*parts)


def finish_kernel(back_ref, expert_ref, slot_ref, out_ref):
    sums = []
    for core in range(2):
        pair = [back_ref[pl.ds(core * 128 + z * 64, 64), :].astype(F32) for z in range(2)]
        sums.append((pair[0] + pair[1]).astype(BF))
    returned = jnp.concatenate(sums, axis=0)
    placing = placing_of(expert_ref[...], slot_ref[...])
    out_ref[...] = dot(returned, placing, 0, 0).astype(BF)


def finish(back, expert, slot):
    width = back.shape[1]
    return pl.pallas_call(
        finish_kernel,
        out_shape=jax.ShapeDtypeStruct((width, 128), BF),
        in_specs=[VMEM] * 3,
        out_specs=VMEM,
        compiler_params=PARAMS,
        cost_estimate=cost(2 * 128 * 128 * width, 3 * 128 * width * 2),
        name="finish",
    )(back, expert, slot)


def weights_kernel(a0, b0, a1, b1, out_ref):
    value = dot(a0[...], b0[...], 0, 0) + dot(a1[...], b1[...], 0, 0)
    out_ref[...] = value.astype(BF)


def weights(a, b, a_part, b_part):
    width, units = a[0].shape[1], b[0].shape[1]
    spec_a = [pl.BlockSpec((512, 256), lambda i, p=p: (p, i)) for p in a_part]
    spec_b = [pl.BlockSpec((512, units), lambda i, p=p: (p, 0)) for p in b_part]
    return pl.pallas_call(
        weights_kernel,
        grid=(pl.cdiv(width, 256),),
        out_shape=jax.ShapeDtypeStruct((width, units), BF),
        in_specs=[spec_a[0], spec_b[0], spec_a[1], spec_b[1]],
        out_specs=pl.BlockSpec((256, units), lambda i: (i, 0)),
        compiler_params=PARAMS,
        cost_estimate=cost(2 * 1024 * width * units, 10 << 20),
        name="weights",
    )(a[0], b[0], a[1], b[1])


def move(value, axis, pairs):
    blocks = value.reshape(-1, 64, value.shape[1])
    return lax.ppermute(blocks, axis, pairs).reshape(value.shape)


def right(value):
    return move(value, "x", RIGHT)


def left(value):
    return move(value, "x", LEFT)


def other_z(value):
    return move(value, "zl", SWAP)


def exchange(value):
    blocks = value.reshape(32, 8, value.shape[1])
    return lax.all_to_all(blocks, EXCHANGE, split_axis=0, concat_axis=0, tiled=True).reshape(value.shape)


def gather_x(own):
    from_left = right(own)
    from_right = left(own)
    return [own, from_left, from_right, right(from_left[:64]), left(from_right[64:])]


def per_device(grad_out, expert_id, slot, gate_prob, saved_inputs, w_in, w_out):
    width = grad_out.shape[1]
    z = lax.axis_index("zl").astype(jnp.int32).reshape(1)
    expert = expert_id.reshape(1, -1)
    place = slot.reshape(1, -1)
    first = w_in[0]
    second = w_out[0].T

    outgoing, own = prepare(grad_out.T, expert, place, gate_prob.reshape(1, -1), saved_inputs[0].reshape(128, width))
    arrived = exchange(outgoing)
    near = gather_x(own)
    far = [other_z(piece) for piece in near]
    cotangents = [gather_x(arrived[part * 128 : part * 128 + 128]) for part in range(2)]

    rows, hidden, slope = forward(z, near + far, first)
    grads = []
    dhiddens = []
    summands = []
    for part in range(2):
        g_rows, dhidden, pown, plft, prgt, pfar0, pfar1 = backward(part, cotangents[part], slope, second, first)
        grads.append(g_rows)
        dhiddens.append(dhidden)
        to_right, to_left = middle(prgt, plft, right(pfar0), left(pfar1))
        summands += [pown, right(to_right), left(to_left)]
    came_back = exchange(total(summands))
    grad_in = weights((rows, rows), dhiddens, (0, 1), (0, 0))
    grad_out_w = weights(grads, (hidden, hidden), (0, 0), (0, 1))
    tokens = finish(came_back, expert, place)
    return (tokens.T, grad_in[None], grad_out_w.T[None])


def solution(mesh):
    fine = Mesh(mesh.devices.reshape(4, 2, 2, 4, 2), AXES)
    wide = ("y", "zh", "core")
    local = ("x", "zl")
    placed = (
        P(wide + local, None),
        P(wide + local),
        P(wide + local),
        P(wide + local),
        P(wide, None, local, None),
        P(wide, None, local),
        P(wide, local, None),
    )
    return jax.shard_map(
        per_device,
        mesh=fine,
        in_specs=placed,
        out_specs=(P(wide + local, None), P(wide, None, local), P(wide, local, None)),
        check_vma=False,
    )
```

time: 263 us -> 177 us (0.67)
  waiting for transfers between devices: 167 us -> 60.8 us
  Pallas kernels: 0 us -> 51.4 us
  matrix products: 40.4 us -> 0 us
  starting transfers between devices: 23 us -> 52.1 us
  between operations: 14.1 us -> 0.83 us
  other arithmetic: 4.42 us -> 0 us
    all_gather x1 -> x0, waiting for transfers between devices: 127 us -> none  [per_device(): inputs = lax.all_gather(saved_inputs[0], 'local', axis=1, tiled=True)]
    ppermute x0 -> x25, waiting for transfers between devices: none -> 60 us  [move(): return lax.ppermute(blocks, axis, pairs).reshape(value.shape)]
    pallas_call x0 -> x10, Pallas kernels: none -> 51.4 us  [the longest x2 18.6 us: weights(): pl.pallas_call(weights_kernel, grid=(pl.cdiv(width, 256),), out_shape=jax...]
    dot_general x7 -> x0, matrix products: 40.4 us -> none  [the longest x5 31.4 us: contract(): lax.dot_general(left, right, (((left_dim,), (right_dim,)), ((), ())), pre...]
    all_to_all x2, waiting for transfers between devices: 39.4 us -> 0.76 us  [exchange(): lax.all_to_all(blocks, EXCHANGE, split_axis=0, concat_axis=0, tiled=True)]
    ppermute x0 -> x25, starting transfers between devices: none -> 32.7 us  [move(): return lax.ppermute(blocks, axis, pairs).reshape(value.shape)]
    convert_element_type x2 -> x0, local copies, waits for them, and re-layouts: 8.46 us -> none  [the longest x1 6.38 us: per_device(): partial_value.astype(jnp.bfloat16).reshape(groups * shards, capacity, width)]
    slice x0 -> x7, local copies, waits for them, and re-layouts: none -> 4.93 us  [the longest x1 2.19 us: per_device(): arrived[part * 128:part * 128 + 128]]
  transfers between devices with their start and end apart: 3 -> 27, of which waited for: 2 -> 10; matrix products, arithmetic and copies ran while one was open for 13% -> 3% of each run, Pallas kernels for 0% -> 27%
where the time goes in v1:
time: 177 us; the launch traced here: 176 us
  waiting for transfers between devices  60.8 us (34%)
  starting transfers between devices  52.1 us (29%)
  Pallas kernels  51.4 us (29%)
  local copies, waits for them, and re-layouts  10.9 us (6%)
    ppermute x25, waiting for transfers between devices, move(): return lax.ppermute(blocks, axis, pairs).reshape(value.shape)  60 us
    ppermute x25, starting transfers between devices, move(): return lax.ppermute(blocks, axis, pairs).reshape(value.shape)  32.7 us
    all_to_all x2, starting transfers between devices, exchange(): lax.all_to_all(blocks, EXCHANGE, split_axis=0, concat_axis=0, tiled=True)  19.4 us
    pallas_call x2, Pallas kernels, weights(): pl.pallas_call(weights_kernel, grid=(pl.cdiv(width, 256),), out_shape=jax...  18.6 us
    pallas_call x2, Pallas kernels, backward(): pl.pallas_call(backward_kernel, grid=(1,), out_shape=tuple((jax.ShapeDtyp...  18 us
    pallas_call x1, Pallas kernels, forward(): pl.pallas_call(forward_kernel, out_shape=(jax.ShapeDtypeStruct((1024, wid...  10.3 us
    unnamed x28, local copies, waits for them, and re-layouts  5.94 us
  transfers between devices with their start and end apart: 27, of which 10 were waited for; matrix products, arithmetic and copies ran while one was open for 3% of the time, Pallas kernels for 27%

profile of v1, /device:TPU:1, one launch (start us, length us, event | category | flops | bytes accessed | tf_op | source)
XLA Modules:
  0.0 176.0 jit_solution(8897626231539595627)
XLA Ops:
  0.6 1.0 copy-done.2
  1.7 1.0 copy-done.3
  2.7 0.7 copy-done.4
  3.4 0.7 copy-done.6
  4.0 0.7 copy-done.8
  4.7 1.3 prepare.1
  6.0 9.7 %all-to-all-start = ((bf16[32,8,2080]{2,1,0:T(8,128)(2,1)}), bf16[32,8,2080]{2,1,0:T(8,128)(2,1)}, u32[]{:S(2)}, u32[]{:S(2)}) async-start(bf16[32,8,2080]{2,1,0:T(8,128)(2,1)} %bitcast.5), calls=%async_computation | async-start | bytes 2228224 | tf_op jit(solution)/shard_map/all_to_all | solution.py:276
  15.7 1.3 collective-permute-start.4
  17.0 1.5 collective-permute-start.5
  18.4 1.4 collective-permute-start.8
  19.8 11.1 %collective-permute-done.4 = bf16[2,64,2080]{2,1,0:T(8,128)(2,1)S(1)} collective-permute-done((bf16[2,64,2080]{2,1,0:T(8,128)(2,1)S(1)}, bf16[2,64,2080]{2,1,0:T(8,128)(2,1)S(1)}, u32[]{:S(2)}, u32[]{:S(2)}) %collective-permute-start.4) | collective-permute-done | bytes 532512 | tf_op jit(solution)/shard_map/ppermute | solution.py:259
  30.9 0.7 slice.49
  31.6 0.1 collective-permute-start.6
  31.7 1.3 collective-permute-start.9
  33.0 0.8 all-to-all-done
  33.8 2.2 %fusion = (bf16[16,8,2080]{2,1,0:T(8,128)(2,1)}, bf16[128,2080]{1,0:T(8,128)(2,1)S(1)}, bf16[128,2080]{1,0:T(8,128)(2,1)S(1)}, bf16[16,8,2080]{2,1,0:T(8,128)(2,1)S(1)}) fusion(bf16[32,8,2080]{2,1,0:T(8,128)(2,1)} %all-to-all-done), kind=kLoop, calls=%fused_computation.2 | loop fusion | bytes 3194880 | tf_op jit(solution)/shard_map/slice | solution.py:297
  36.0 1.2 collective-permute-start
  37.2 0.0 collective-permute-done.5
  37.2 1.5 collective-permute-start.1
  38.7 3.2 %collective-permute-done.8 = bf16[2,64,2080]{2,1,0:T(8,128)(2,1)} collective-permute-done((bf16[2,64,2080]{2,1,0:T(8,128)(2,1)S(1)}, bf16[2,64,2080]{2,1,0:T(8,128)(2,1)}, u32[]{:S(2)}, u32[]{:S(2)}) %collective-permute-start.8) | collective-permute-done | bytes 532512 | tf_op jit(solution)/shard_map/ppermute | solution.py:259
  41.9 0.2 collective-permute-start.10
  42.1 2.5 %collective-permute-start.7 = (bf16[1,64,2080]{2,1,0:T(8,128)(2,1)S(1)}, bf16[1,64,2080]{2,1,0:T(8,128)(2,1)}, u32[]{:S(2)}, u32[]{:S(2)}) collective-permute-start(bf16[1,64,2080]{2,1,0:T(8,128)(2,1)S(1)} %slice.50), channel_id=1, source_target_pairs={{0,6},{2,0},{4,2},{6,4},{1,7},{3,1},{5,3},{7,5},{8,14},{10,8},{12,... | collective-permute-start | bytes 798728 | tf_op jit(solution)/shard_map/ppermute | solution.py:259
  44.6 11.6 %collective-permute-done.7 = bf16[1,64,2080]{2,1,0:T(8,128)(2,1)} collective-permute-done((bf16[1,64,2080]{2,1,0:T(8,128)(2,1)S(1)}, bf16[1,64,2080]{2,1,0:T(8,128)(2,1)}, u32[]{:S(2)}, u32[]{:S(2)}) %collective-permute-start.7) | collective-permute-done | bytes 266272 | tf_op jit(solution)/shard_map/ppermute | solution.py:259
  56.2 0.0 collective-permute-start.11
  56.2 1.5 collective-permute-start.12
  57.7 0.0 collective-permute-done
  57.7 1.5 collective-permute-start.17
  59.2 0.0 collective-permute-done.1
  59.2 0.8 copy-done.13
  60.0 1.2 collective-permute-start.18
  61.2 1.0 slice.48
  62.2 3.5 %collective-permute-done.10 = bf16[2,64,2080]{2,1,0:T(8,128)(2,1)} collective-permute-done((bf16[2,64,2080]{2,1,0:T(8,128)(2,1)S(1)}, bf16[2,64,2080]{2,1,0:T(8,128)(2,1)}, u32[]{:S(2)}, u32[]{:S(2)}) %collective-permute-start.10) | collective-permute-done | bytes 532512 | tf_op jit(solution)/shard_map/ppermute | solution.py:259
  65.8 1.2 collective-permute-start.2
  67.0 4.8 %collective-permute-done.11 = bf16[1,64,2080]{2,1,0:T(8,128)(2,1)} collective-permute-done((bf16[1,64,2080]{2,1,0:T(8,128)(2,1)}, bf16[1,64,2080]{2,1,0:T(8,128)(2,1)}, u32[]{:S(2)}, u32[]{:S(2)}) %collective-permute-start.11) | collective-permute-done | bytes 266272 | tf_op jit(solution)/shard_map/ppermute | solution.py:259
  71.7 2.5 %collective-permute-start.3 = (bf16[1,64,2080]{2,1,0:T(8,128)(2,1)S(1)}, bf16[1,64,2080]{2,1,0:T(8,128)(2,1)S(1)}, u32[]{:S(2)}, u32[]{:S(2)}) collective-permute-start(bf16[1,64,2080]{2,1,0:T(8,128)(2,1)S(1)} %slice.48), channel_id=1, source_target_pairs={{0,6},{2,0},{4,2},{6,4},{1,7},{3,1},{5,3},{7,5},{8,14},{10,8},{12,... | collective-permute-start | bytes 798728 | tf_op jit(solution)/shard_map/ppermute | solution.py:259
  74.2 3.5 %collective-permute-done.12 = bf16[1,64,2080]{2,1,0:T(8,128)(2,1)} collective-permute-done((bf16[1,64,2080]{2,1,0:T(8,128)(2,1)}, bf16[1,64,2080]{2,1,0:T(8,128)(2,1)}, u32[]{:S(2)}, u32[]{:S(2)}) %collective-permute-start.12) | collective-permute-done | bytes 266272 | tf_op jit(solution)/shard_map/ppermute | solution.py:259
  77.7 1.1 copy-done.10
  78.7 10.3 %forward.1 = (bf16[1024,2080]{1,0:T(8,128)(2,1)}, bf16[1024,768]{1,0:T(8,128)(2,1)}, f32[1024,768]{1,0:T(8,128)}) custom-call(s32[1]{0:T(128)} %bitcast.12.z_ref, bf16[128,2080]{1,0:T(8,128)(2,1)S(1)} %copy-done.10, bf16[128,2080]{1,0:T(8,128)(2,1)S(1)} %bitcast.74, bf16[128,2080]{1,0:T(8,128)(2,1)S(1)} %bitcast.75, bf16[64,2080]{1,0:T(8,128)(2,1)} %bitcast.16.far0, ...), custom_call_target="tpu_custom_call" | custom-call | flops 3271557120 | bytes 20971520 | tf_op jit(solution)/shard_map/forward/pallas_call | solution.py:99
  89.1 1.3 collective-permute-start.19
  90.4 1.0 slice.53
  91.3 1.7 collective-permute-start.20
  93.1 0.0 collective-permute-done.3
  93.1 9.0 %backward.2 = (bf16[512,2080]{1,0:T(8,128)(2,1)}, bf16[512,768]{1,0:T(8,128)(2,1)}, bf16[128,2080]{1,0:T(8,128)(2,1)S(1)}, bf16[128,2080]{1,0:T(8,128)(2,1)S(1)}...) custom-call(bf16[128,2080]{1,0:T(8,128)(2,1)S(1)} %get-tuple-element.50.own, ...), custom_call_target="tpu_custom_call" | custom-call | flops 3271557120 | bytes 14680064 | tf_op jit(solution)/shard_map/backward/pallas_call | solution.py:143
  102.0 0.1 collective-permute-start.13
  102.1 2.7 %collective-permute-start.14 = (bf16[1,64,2080]{2,1,0:T(8,128)(2,1)S(1)}, bf16[1,64,2080]{2,1,0:T(8,128)(2,1)S(1)}, u32[]{:S(2)}, u32[]{:S(2)}) collective-permute-start(bf16[1,64,2080]{2,1,0:T(8,128)(2,1)S(1)} %bitcast.88), channel_id=1, source_target_pairs={{0,6},{2,0},{4,2},{6,4},{1,7},{3,1},{5,3},{7,5},{8,14},{10,8},{12,... | collective-permute-start | bytes 798728 | tf_op jit(solution)/shard_map/ppermute | solution.py:259
  104.8 0.0 collective-permute-done.19
  104.8 9.0 %backward.3 = (bf16[512,2080]{1,0:T(8,128)(2,1)}, bf16[512,768]{1,0:T(8,128)(2,1)}, bf16[128,2080]{1,0:T(8,128)(2,1)S(1)}, bf16[128,2080]{1,0:T(8,128)(2,1)S(1)}...) custom-call(bf16[128,2080]{1,0:T(8,128)(2,1)S(1)} %get-tuple-element.51.own, ...), custom_call_target="tpu_custom_call" | custom-call | flops 3271557120 | bytes 14680064 | tf_op jit(solution)/shard_map/backward/pallas_call | solution.py:143
  113.8 0.1 collective-permute-start.21
  113.9 2.7 %collective-permute-start.22 = (bf16[1,64,2080]{2,1,0:T(8,128)(2,1)S(1)}, bf16[1,64,2080]{2,1,0:T(8,128)(2,1)S(1)}, u32[]{:S(2)}, u32[]{:S(2)}) collective-permute-start(bf16[1,64,2080]{2,1,0:T(8,128)(2,1)S(1)} %bitcast.91), channel_id=1, source_target_pairs={{0,6},{2,0},{4,2},{6,4},{1,7},{3,1},{5,3},{7,5},{8,14},{10,8},{12,... | collective-permute-start | bytes 798728 | tf_op jit(solution)/shard_map/ppermute | solution.py:259
  116.5 0.4 middle.2
  116.9 0.1 collective-permute-start.15
  117.0 2.7 %collective-permute-start.16 = (bf16[2,64,2080]{2,1,0:T(8,128)(2,1)S(1)}, bf16[2,64,2080]{2,1,0:T(8,128)(2,1)S(1)}, u32[]{:S(2)}, u32[]{:S(2)}) collective-permute-start(bf16[2,64,2080]{2,1,0:T(8,128)(2,1)S(1)} %bitcast.64), channel_id=1, source_target_pairs={{0,6},{2,0},{4,2},{6,4},{1,7},{3,1},{5,3},{7,5},{8,14},{10,8},{12,... | collective-permute-start | bytes 1597448 | tf_op jit(solution)/shard_map/ppermute | solution.py:259
  119.7 1.6 collective-permute-done.21
  121.2 0.4 middle.3
  121.6 0.1 collective-permute-start.23
  121.7 2.7 %collective-permute-start.24 = (bf16[2,64,2080]{2,1,0:T(8,128)(2,1)S(1)}, bf16[2,64,2080]{2,1,0:T(8,128)(2,1)S(1)}, u32[]{:S(2)}, u32[]{:S(2)}) collective-permute-start(bf16[2,64,2080]{2,1,0:T(8,128)(2,1)S(1)} %bitcast.66), channel_id=1, source_target_pairs={{0,6},{2,0},{4,2},{6,4},{1,7},{3,1},{5,3},{7,5},{8,14},{10,8},{12,... | collective-permute-start | bytes 1597448 | tf_op jit(solution)/shard_map/ppermute | solution.py:259
  124.4 8.8 %collective-permute-done.15 = bf16[2,64,2080]{2,1,0:T(8,128)(2,1)S(1)} collective-permute-done((bf16[2,64,2080]{2,1,0:T(8,128)(2,1)S(1)}, bf16[2,64,2080]{2,1,0:T(8,128)(2,1)S(1)}, u32[]{:S(2)}, u32[]{:S(2)}) %collective-permute-start.15) | collective-permute-done | bytes 532512 | tf_op jit(solution)/shard_map/ppermute | solution.py:259
  133.2 11.9 %collective-permute-done.23 = bf16[2,64,2080]{2,1,0:T(8,128)(2,1)S(1)} collective-permute-done((bf16[2,64,2080]{2,1,0:T(8,128)(2,1)S(1)}, bf16[2,64,2080]{2,1,0:T(8,128)(2,1)S(1)}, u32[]{:S(2)}, u32[]{:S(2)}) %collective-permute-start.23) | collective-permute-done | bytes 532512 | tf_op jit(solution)/shard_map/ppermute | solution.py:259
  145.1 1.4 total.1
  146.5 9.7 %all-to-all-start.1 = ((bf16[32,8,2080]{2,1,0:T(8,128)(2,1)}), bf16[32,8,2080]{2,1,0:T(8,128)(2,1)S(1)}, u32[]{:S(2)}, u32[]{:S(2)}) async-start(bf16[32,8,2080]{2,1,0:T(8,128)(2,1)} %bitcast.93), calls=%async_computation.1 | async-start | bytes 2228224 | tf_op jit(solution)/shard_map/all_to_all | solution.py:276
  156.2 9.6 %weights.2 = bf16[2080,768]{1,0:T(8,128)(2,1)} custom-call(bf16[1024,2080]{1,0:T(8,128)(2,1)} %get-tuple-element.43.a0.a1, bf16[512,768]{1,0:T(8,128)(2,1)S(1)} %copy-done, bf16[1024,2080]{1,0:T(8,128)(2,1)} %get-tuple-element.43.a0.a1, bf16[512,768]{1,0:T(8,128)(2,1)S(1)} %copy-done.1), custom_call_target="tpu_custom_call" | custom-call | flops 3271557120 | bytes 10485760 | tf_op jit(solution)/shard_map/weights/pallas_call | solution.py:245
  165.8 0.0 copy-start.7
  165.8 9.1 %weights.3 = bf16[2080,768]{1,0:T(8,128)(2,1)} custom-call(bf16[512,2080]{1,0:T(8,128)(2,1)S(1)} %copy-done.11, bf16[1024,768]{1,0:T(8,128)(2,1)S(1)} %copy-done.12, bf16[512,2080]{1,0:T(8,128)(2,1)} %get-tuple-element.48.a1, bf16[1024,768]{1,0:T(8,128)(2,1)S(1)} %copy-done.12), custom_call_target="tpu_custom_call" | custom-call | flops 3271557120 | bytes 10485760 | tf_op jit(solution)/shard_map/weights/pallas_call | solution.py:245
  174.9 1.1 finish.1
  (35 shorter events, 0.1 us)
Async XLA Ops:
  0.6 1.1 copy-start.2
  1.7 1.0 copy-start.3
  2.7 0.7 copy-start.4
  3.4 0.7 copy-start.6
  4.0 0.7 copy-start.8
  6.0 30.0 %copy-start.9 = (bf16[128,2080]{1,0:T(8,128)(2,1)}, bf16[128,2080]{1,0:T(8,128)(2,1)S(1)}, u32[]{:S(2)}) copy-start(bf16[128,2080]{1,0:T(8,128)(2,1)S(1)} %get-tuple-element.27.own) | copy-start | bytes 1597444
  6.0 27.8 %all-to-all-start = ((bf16[32,8,2080]{2,1,0:T(8,128)(2,1)}), bf16[32,8,2080]{2,1,0:T(8,128)(2,1)}, u32[]{:S(2)}, u32[]{:S(2)}) async-start(bf16[32,8,2080]{2,1,0:T(8,128)(2,1)} %bitcast.5), calls=%async_computation | async-start | bytes 2228224 | tf_op jit(solution)/shard_map/all_to_all | solution.py:276
  15.7 15.2 %collective-permute-start.4 = (bf16[2,64,2080]{2,1,0:T(8,128)(2,1)S(1)}, bf16[2,64,2080]{2,1,0:T(8,128)(2,1)S(1)}, u32[]{:S(2)}, u32[]{:S(2)}) collective-permute-start(bf16[2,64,2080]{2,1,0:T(8,128)(2,1)S(1)} %bitcast.82), channel_id=1, source_target_pairs={{0,2},{2,4},{4,6},{6,0},{1,3},{3,5},{5,7},{7,1},{8,10},{10,12},{12... | collective-permute-start | bytes 1597448 | tf_op jit(solution)/shard_map/ppermute | solution.py:259
  17.0 20.2 %collective-permute-start.5 = (bf16[2,64,2080]{2,1,0:T(8,128)(2,1)S(1)}, bf16[2,64,2080]{2,1,0:T(8,128)(2,1)S(1)}, u32[]{:S(2)}, u32[]{:S(2)}) collective-permute-start(bf16[2,64,2080]{2,1,0:T(8,128)(2,1)S(1)} %bitcast.83), channel_id=1, source_target_pairs={{0,6},{2,0},{4,2},{6,4},{1,7},{3,1},{5,3},{7,5},{8,14},{10,8},{12,... | collective-permute-start | bytes 1597448 | tf_op jit(solution)/shard_map/ppermute | solution.py:259
  18.4 23.4 %collective-permute-start.8 = (bf16[2,64,2080]{2,1,0:T(8,128)(2,1)S(1)}, bf16[2,64,2080]{2,1,0:T(8,128)(2,1)}, u32[]{:S(2)}, u32[]{:S(2)}) collective-permute-start(bf16[2,64,2080]{2,1,0:T(8,128)(2,1)S(1)} %bitcast.84), channel_id=1, source_target_pairs={{0,1},{1,0},{2,3},{3,2},{4,5},{5,4},{6,7},{7,6},{8,9},{9,8},{10,11... | collective-permute-start | bytes 1597448 | tf_op jit(solution)/shard_map/ppermute | solution.py:259
  31.6 10.5 %collective-permute-start.6 = (bf16[1,64,2080]{2,1,0:T(8,128)(2,1)}, bf16[1,64,2080]{2,1,0:T(8,128)(2,1)}, u32[]{:S(2)}, u32[]{:S(2)}) collective-permute-start(bf16[1,64,2080]{2,1,0:T(8,128)(2,1)} %slice.49), channel_id=1, source_target_pairs={{0,2},{2,4},{4,6},{6,0},{1,3},{3,5},{5,7},{7,1},{8,10},{10,12},{12... | collective-permute-start | bytes 798728 | tf_op jit(solution)/shard_map/ppermute | solution.py:259
  31.7 24.5 %collective-permute-start.9 = (bf16[2,64,2080]{2,1,0:T(8,128)(2,1)S(1)}, bf16[2,64,2080]{2,1,0:T(8,128)(2,1)}, u32[]{:S(2)}, u32[]{:S(2)}) collective-permute-start(bf16[2,64,2080]{2,1,0:T(8,128)(2,1)S(1)} %collective-permute-done.4), channel_id=1, source_target_pairs={{0,1},{1,0},{2,3},{3,2},{4,5},{5,4},{6,7},{7,6},{8,9},{9,8},{10,11... | collective-permute-start | bytes 1597448 | tf_op jit(solution)/shard_map/ppermute | solution.py:259
  36.0 21.7 %collective-permute-start = (bf16[2,64,2080]{2,1,0:T(8,128)(2,1)S(1)}, bf16[2,64,2080]{2,1,0:T(8,128)(2,1)S(1)}, u32[]{:S(2)}, u32[]{:S(2)}) collective-permute-start(bf16[2,64,2080]{2,1,0:T(8,128)(2,1)S(1)} %bitcast.95), channel_id=1, source_target_pairs={{0,2},{2,4},{4,6},{6,0},{1,3},{3,5},{5,7},{7,1},{8,10},{10,12},{12... | collective-permute-start | bytes 1597448 | tf_op jit(solution)/shard_map/ppermute | solution.py:259
  37.2 22.0 %collective-permute-start.1 = (bf16[2,64,2080]{2,1,0:T(8,128)(2,1)S(1)}, bf16[2,64,2080]{2,1,0:T(8,128)(2,1)S(1)}, u32[]{:S(2)}, u32[]{:S(2)}) collective-permute-start(bf16[2,64,2080]{2,1,0:T(8,128)(2,1)S(1)} %bitcast.96), channel_id=1, source_target_pairs={{0,6},{2,0},{4,2},{6,4},{1,7},{3,1},{5,3},{7,5},{8,14},{10,8},{12,... | collective-permute-start | bytes 1597448 | tf_op jit(solution)/shard_map/ppermute | solution.py:259
  41.9 23.9 %collective-permute-start.10 = (bf16[2,64,2080]{2,1,0:T(8,128)(2,1)S(1)}, bf16[2,64,2080]{2,1,0:T(8,128)(2,1)}, u32[]{:S(2)}, u32[]{:S(2)}) collective-permute-start(bf16[2,64,2080]{2,1,0:T(8,128)(2,1)S(1)} %collective-permute-done.5), channel_id=1, source_target_pairs={{0,1},{1,0},{2,3},{3,2},{4,5},{5,4},{6,7},{7,6},{8,9},{9,8},{10,11... | collective-permute-start | bytes 1597448 | tf_op jit(solution)/shard_map/ppermute | solution.py:259
  42.1 14.1 %collective-permute-start.7 = (bf16[1,64,2080]{2,1,0:T(8,128)(2,1)S(1)}, bf16[1,64,2080]{2,1,0:T(8,128)(2,1)}, u32[]{:S(2)}, u32[]{:S(2)}) collective-permute-start(bf16[1,64,2080]{2,1,0:T(8,128)(2,1)S(1)} %slice.50), channel_id=1, source_target_pairs={{0,6},{2,0},{4,2},{6,4},{1,7},{3,1},{5,3},{7,5},{8,14},{10,8},{12,... | collective-permute-start | bytes 798728 | tf_op jit(solution)/shard_map/ppermute | solution.py:259
  56.2 15.5 %collective-permute-start.11 = (bf16[1,64,2080]{2,1,0:T(8,128)(2,1)}, bf16[1,64,2080]{2,1,0:T(8,128)(2,1)}, u32[]{:S(2)}, u32[]{:S(2)}) collective-permute-start(bf16[1,64,2080]{2,1,0:T(8,128)(2,1)} %collective-permute-done.6), channel_id=1, source_target_pairs={{0,1},{1,0},{2,3},{3,2},{4,5},{5,4},{6,7},{7,6},{8,9},{9,8},{10,11... | collective-permute-start | bytes 798728 | tf_op jit(solution)/shard_map/ppermute | solution.py:259
  56.2 21.4 %collective-permute-start.12 = (bf16[1,64,2080]{2,1,0:T(8,128)(2,1)}, bf16[1,64,2080]{2,1,0:T(8,128)(2,1)}, u32[]{:S(2)}, u32[]{:S(2)}) collective-permute-start(bf16[1,64,2080]{2,1,0:T(8,128)(2,1)} %collective-permute-done.7), channel_id=1, source_target_pairs={{0,1},{1,0},{2,3},{3,2},{4,5},{5,4},{6,7},{7,6},{8,9},{9,8},{10,11... | collective-permute-start | bytes 798728 | tf_op jit(solution)/shard_map/ppermute | solution.py:259
  57.7 31.3 %collective-permute-start.17 = (bf16[2,64,2080]{2,1,0:T(8,128)(2,1)}, bf16[2,64,2080]{2,1,0:T(8,128)(2,1)S(1)}, u32[]{:S(2)}, u32[]{:S(2)}) collective-permute-start(bf16[2,64,2080]{2,1,0:T(8,128)(2,1)} %bitcast.35), channel_id=1, source_target_pairs={{0,2},{2,4},{4,6},{6,0},{1,3},{3,5},{5,7},{7,1},{8,10},{10,12},{12... | collective-permute-start | bytes 1597448 | tf_op jit(solution)/shard_map/ppermute | solution.py:259
  59.2 0.8 copy-start.13
  60.0 30.3 %collective-permute-start.18 = (bf16[2,64,2080]{2,1,0:T(8,128)(2,1)}, bf16[2,64,2080]{2,1,0:T(8,128)(2,1)}, u32[]{:S(2)}, u32[]{:S(2)}) collective-permute-start(bf16[2,64,2080]{2,1,0:T(8,128)(2,1)} %bitcast.35), channel_id=1, source_target_pairs={{0,6},{2,0},{4,2},{6,4},{1,7},{3,1},{5,3},{7,5},{8,14},{10,8},{12,... | collective-permute-start | bytes 1597448 | tf_op jit(solution)/shard_map/ppermute | solution.py:259
  65.8 27.3 %collective-permute-start.2 = (bf16[1,64,2080]{2,1,0:T(8,128)(2,1)S(1)}, bf16[1,64,2080]{2,1,0:T(8,128)(2,1)S(1)}, u32[]{:S(2)}, u32[]{:S(2)}) collective-permute-start(bf16[1,64,2080]{2,1,0:T(8,128)(2,1)S(1)} %slice.47), channel_id=1, source_target_pairs={{0,2},{2,4},{4,6},{6,0},{1,3},{3,5},{5,7},{7,1},{8,10},{10,12},{12... | collective-permute-start | bytes 798728 | tf_op jit(solution)/shard_map/ppermute | solution.py:259
  71.7 21.3 %collective-permute-start.3 = (bf16[1,64,2080]{2,1,0:T(8,128)(2,1)S(1)}, bf16[1,64,2080]{2,1,0:T(8,128)(2,1)S(1)}, u32[]{:S(2)}, u32[]{:S(2)}) collective-permute-start(bf16[1,64,2080]{2,1,0:T(8,128)(2,1)S(1)} %slice.48), channel_id=1, source_target_pairs={{0,6},{2,0},{4,2},{6,4},{1,7},{3,1},{5,3},{7,5},{8,14},{10,8},{12,... | collective-permute-start | bytes 798728 | tf_op jit(solution)/shard_map/ppermute | solution.py:259
  77.7 1.1 copy-start.10
  89.1 15.7 %collective-permute-start.19 = (bf16[1,64,2080]{2,1,0:T(8,128)(2,1)S(1)}, bf16[1,64,2080]{2,1,0:T(8,128)(2,1)S(1)}, u32[]{:S(2)}, u32[]{:S(2)}) collective-permute-start(bf16[1,64,2080]{2,1,0:T(8,128)(2,1)S(1)} %slice.52), channel_id=1, source_target_pairs={{0,2},{2,4},{4,6},{6,0},{1,3},{3,5},{5,7},{7,1},{8,10},{10,12},{12... | collective-permute-start | bytes 798728 | tf_op jit(solution)/shard_map/ppermute | solution.py:259
  91.3 13.5 %collective-permute-start.20 = (bf16[1,64,2080]{2,1,0:T(8,128)(2,1)S(1)}, bf16[1,64,2080]{2,1,0:T(8,128)(2,1)S(1)}, u32[]{:S(2)}, u32[]{:S(2)}) collective-permute-start(bf16[1,64,2080]{2,1,0:T(8,128)(2,1)S(1)} %slice.53), channel_id=1, source_target_pairs={{0,6},{2,0},{4,2},{6,4},{1,7},{3,1},{5,3},{7,5},{8,14},{10,8},{12,... | collective-permute-start | bytes 798728 | tf_op jit(solution)/shard_map/ppermute | solution.py:259
  102.0 14.5 %collective-permute-start.13 = (bf16[1,64,2080]{2,1,0:T(8,128)(2,1)S(1)}, bf16[1,64,2080]{2,1,0:T(8,128)(2,1)S(1)}, u32[]{:S(2)}, u32[]{:S(2)}) collective-permute-start(bf16[1,64,2080]{2,1,0:T(8,128)(2,1)S(1)} %bitcast.90), channel_id=1, source_target_pairs={{0,2},{2,4},{4,6},{6,0},{1,3},{3,5},{5,7},{7,1},{8,10},{10,12},{12... | collective-permute-start | bytes 798728 | tf_op jit(solution)/shard_map/ppermute | solution.py:259
  102.1 14.4 %collective-permute-start.14 = (bf16[1,64,2080]{2,1,0:T(8,128)(2,1)S(1)}, bf16[1,64,2080]{2,1,0:T(8,128)(2,1)S(1)}, u32[]{:S(2)}, u32[]{:S(2)}) collective-permute-start(bf16[1,64,2080]{2,1,0:T(8,128)(2,1)S(1)} %bitcast.88), channel_id=1, source_target_pairs={{0,6},{2,0},{4,2},{6,4},{1,7},{3,1},{5,3},{7,5},{8,14},{10,8},{12,... | collective-permute-start | bytes 798728 | tf_op jit(solution)/shard_map/ppermute | solution.py:259
  113.8 7.5 %collective-permute-start.21 = (bf16[1,64,2080]{2,1,0:T(8,128)(2,1)S(1)}, bf16[1,64,2080]{2,1,0:T(8,128)(2,1)S(1)}, u32[]{:S(2)}, u32[]{:S(2)}) collective-permute-start(bf16[1,64,2080]{2,1,0:T(8,128)(2,1)S(1)} %bitcast.92), channel_id=1, source_target_pairs={{0,2},{2,4},{4,6},{6,0},{1,3},{3,5},{5,7},{7,1},{8,10},{10,12},{12... | collective-permute-start | bytes 798728 | tf_op jit(solution)/shard_map/ppermute | solution.py:259
  113.9 7.4 %collective-permute-start.22 = (bf16[1,64,2080]{2,1,0:T(8,128)(2,1)S(1)}, bf16[1,64,2080]{2,1,0:T(8,128)(2,1)S(1)}, u32[]{:S(2)}, u32[]{:S(2)}) collective-permute-start(bf16[1,64,2080]{2,1,0:T(8,128)(2,1)S(1)} %bitcast.91), channel_id=1, source_target_pairs={{0,6},{2,0},{4,2},{6,4},{1,7},{3,1},{5,3},{7,5},{8,14},{10,8},{12,... | collective-permute-start | bytes 798728 | tf_op jit(solution)/shard_map/ppermute | solution.py:259
  116.9 16.3 %collective-permute-start.15 = (bf16[2,64,2080]{2,1,0:T(8,128)(2,1)S(1)}, bf16[2,64,2080]{2,1,0:T(8,128)(2,1)S(1)}, u32[]{:S(2)}, u32[]{:S(2)}) collective-permute-start(bf16[2,64,2080]{2,1,0:T(8,128)(2,1)S(1)} %bitcast.65), channel_id=1, source_target_pairs={{0,2},{2,4},{4,6},{6,0},{1,3},{3,5},{5,7},{7,1},{8,10},{10,12},{12... | collective-permute-start | bytes 1597448 | tf_op jit(solution)/shard_map/ppermute | solution.py:259
  117.0 16.2 %collective-permute-start.16 = (bf16[2,64,2080]{2,1,0:T(8,128)(2,1)S(1)}, bf16[2,64,2080]{2,1,0:T(8,128)(2,1)S(1)}, u32[]{:S(2)}, u32[]{:S(2)}) collective-permute-start(bf16[2,64,2080]{2,1,0:T(8,128)(2,1)S(1)} %bitcast.64), channel_id=1, source_target_pairs={{0,6},{2,0},{4,2},{6,4},{1,7},{3,1},{5,3},{7,5},{8,14},{10,8},{12,... | collective-permute-start | bytes 1597448 | tf_op jit(solution)/shard_map/ppermute | solution.py:259
  121.6 23.5 %collective-permute-start.23 = (bf16[2,64,2080]{2,1,0:T(8,128)(2,1)S(1)}, bf16[2,64,2080]{2,1,0:T(8,128)(2,1)S(1)}, u32[]{:S(2)}, u32[]{:S(2)}) collective-permute-start(bf16[2,64,2080]{2,1,0:T(8,128)(2,1)S(1)} %bitcast.67), channel_id=1, source_target_pairs={{0,2},{2,4},{4,6},{6,0},{1,3},{3,5},{5,7},{7,1},{8,10},{10,12},{12... | collective-permute-start | bytes 1597448 | tf_op jit(solution)/shard_map/ppermute | solution.py:259
  121.7 23.4 %collective-permute-start.24 = (bf16[2,64,2080]{2,1,0:T(8,128)(2,1)S(1)}, bf16[2,64,2080]{2,1,0:T(8,128)(2,1)S(1)}, u32[]{:S(2)}, u32[]{:S(2)}) collective-permute-start(bf16[2,64,2080]{2,1,0:T(8,128)(2,1)S(1)} %bitcast.66), channel_id=1, source_target_pairs={{0,6},{2,0},{4,2},{6,4},{1,7},{3,1},{5,3},{7,5},{8,14},{10,8},{12,... | collective-permute-start | bytes 1597448 | tf_op jit(solution)/shard_map/ppermute | solution.py:259
  146.5 9.7 %copy-start = (bf16[512,768]{1,0:T(8,128)(2,1)S(1)}, bf16[512,768]{1,0:T(8,128)(2,1)}, u32[]{:S(2)}) copy-start(bf16[512,768]{1,0:T(8,128)(2,1)} %get-tuple-element.44.b0) | copy-start | bytes 2359300
  146.5 9.7 %copy-start.1 = (bf16[512,768]{1,0:T(8,128)(2,1)S(1)}, bf16[512,768]{1,0:T(8,128)(2,1)}, u32[]{:S(2)}) copy-start(bf16[512,768]{1,0:T(8,128)(2,1)} %get-tuple-element.45.b1) | copy-start | bytes 2359300
  146.5 28.4 %all-to-all-start.1 = ((bf16[32,8,2080]{2,1,0:T(8,128)(2,1)}), bf16[32,8,2080]{2,1,0:T(8,128)(2,1)S(1)}, u32[]{:S(2)}, u32[]{:S(2)}) async-start(bf16[32,8,2080]{2,1,0:T(8,128)(2,1)} %bitcast.93), calls=%async_computation.1 | async-start | bytes 2228224 | tf_op jit(solution)/shard_map/all_to_all | solution.py:276
  156.2 9.6 %copy-start.11 = (bf16[512,2080]{1,0:T(8,128)(2,1)S(1)}, bf16[512,2080]{1,0:T(8,128)(2,1)}, u32[]{:S(2)}) copy-start(bf16[512,2080]{1,0:T(8,128)(2,1)} %get-tuple-element.46.a0) | copy-start | bytes 6389764
  156.2 9.6 %copy-start.12 = (bf16[1024,768]{1,0:T(8,128)(2,1)S(1)}, bf16[1024,768]{1,0:T(8,128)(2,1)}, u32[]{:S(2)}) copy-start(bf16[1024,768]{1,0:T(8,128)(2,1)} %get-tuple-element.47.b0.b1) | copy-start | bytes 4718596
  165.8 9.1 %copy-start.5 = (s32[128]{0:T(128)S(1)}, s32[128]{0:T(128)}, u32[]{:S(2)}) copy-start(s32[128]{0:T(128)} %param.8) | copy-start | bytes 1540
  165.8 9.1 %copy-start.7 = (s32[128]{0:T(128)S(1)}, s32[128]{0:T(128)}, u32[]{:S(2)}) copy-start(s32[128]{0:T(128)} %param.9) | copy-start | bytes 1540

commit v2 on v0

v2 whole, which is shorter than its diff:
```python
import jax
import jax.numpy as jnp
from jax import lax
from jax.experimental import pallas as pl
from jax.experimental.pallas import tpu as pltpu
from jax.sharding import Mesh, PartitionSpec as P

AXES = ("y", "zh", "core", "x", "zl")
WIDE = ("y", "zh", "core")
LOCAL = ("x", "zl")
WIDE_AND_Z = ("zl",) + WIDE
RIGHT = [(i, (i + 1) % 4) for i in range(4)]
LEFT = [(i, (i - 1) % 4) for i in range(4)]
ACROSS = [(i, (i + 2) % 4) for i in range(4)]
SWAP = [(0, 1), (1, 0)]
BF = jnp.bfloat16
F32 = jnp.float32
VMEM = pl.BlockSpec(memory_space=pltpu.VMEM)
ANY = pl.BlockSpec(memory_space=pl.ANY)
SMEM = pl.BlockSpec(memory_space=pltpu.SMEM)
PARAMS = pltpu.CompilerParams(vmem_limit_bytes=24 * 1024 * 1024)


def dot(a, b, da, db):
    return lax.dot_general(a, b, (((da,), (db,)), ((), ())), preferred_element_type=F32)


def call(kernel, outs, args, name, after=()):
    def ordered(*refs):
        kernel(*refs[: len(args)], *refs[len(args) + len(after) :])

    return pl.pallas_call(
        ordered,
        out_shape=tuple(jax.ShapeDtypeStruct(s, d) for s, d in outs),
        in_specs=[VMEM] * len(args) + [ANY] * len(after),
        out_specs=(VMEM,) * len(outs),
        compiler_params=PARAMS,
        cost_estimate=pl.CostEstimate(flops=0, bytes_accessed=0, transcendentals=0),
        name=name,
    )(*args, *after)


def stacked(refs):
    return jnp.concatenate([ref[...] for ref in refs], axis=0)


def placing_of(expert, slot):
    target = jnp.where(slot >= 0, expert * 8 + slot, -1)
    rows = lax.broadcasted_iota(jnp.int32, (128, 128), 0)
    return jnp.where(rows == target, 1.0, 0.0).astype(BF)


def prepare_kernel(grad, expert, slot, gate, out_ref, grad_ref, expert_ref, slot_ref, gate_ref, sems):
    pairs = ((grad, grad_ref), (expert, expert_ref), (slot, slot_ref), (gate, gate_ref))
    copies = [pltpu.make_async_copy(src, dst, sems.at[i]) for i, (src, dst) in enumerate(pairs)]
    for copy in copies:
        copy.start()
    for copy in copies:
        copy.wait()
    scaled = (gate_ref[...] * grad_ref[...].astype(F32)).astype(BF)
    outgoing = dot(placing_of(expert_ref[...], slot_ref[...]), scaled, 1, 1).astype(BF)
    out_ref[...] = outgoing


def prepare(*args):
    width = args[0].shape[0]
    args = [pltpu.with_memory_space_constraint(a, pltpu.HBM) for a in args]
    return pl.pallas_call(
        prepare_kernel,
        out_shape=jax.ShapeDtypeStruct((128, width), BF),
        in_specs=[pl.BlockSpec(memory_space=pltpu.HBM)] * 4,
        out_specs=VMEM,
        scratch_shapes=[pltpu.VMEM(a.shape, a.dtype) for a in args] + [pltpu.SemaphoreType.DMA((4,))],
        compiler_params=PARAMS,
        cost_estimate=pl.CostEstimate(
            flops=2 * 128 * 128 * width, bytes_accessed=8 * 128 * width, transcendentals=0
        ),
        name="prepare",
    )(*args)


def gelu_parts(value):
    normal_cdf = 0.5 * (1.0 + lax.erf(value * 0.7071067811865476))
    density = jnp.exp(-0.5 * value * value) * 0.3989422804014327
    return value * normal_cdf, normal_cdf + value * density


def forward_kernel(own, lft, rgt, far, w_ref, hidden_ref, slope_ref):
    pre = dot(stacked((own, lft, rgt, far)), w_ref[...], 1, 0)
    value, slope = gelu_parts(pre)
    hidden_ref[...] = value.astype(BF)
    slope_ref[...] = slope


def forward(pieces, w_in, after=()):
    units = w_in.shape[1]
    outs = (((512, units), BF), ((512, units), F32))
    return call(forward_kernel, outs, (*pieces, w_in), "forward", after)


def backward_kernel(own, lft, rgt, far, slope_ref, wo_ref, wi_ref, dhidden_ref, *outs):
    back = dot(stacked((own, lft, rgt, far)), wo_ref[...], 1, 0)
    dhidden = (back * slope_ref[...]).astype(BF)
    dhidden_ref[...] = dhidden
    partial_value = dot(dhidden, wi_ref[...], 1, 1).astype(BF)
    start = 0
    for out in outs:
        size = out.shape[0]
        out[...] = partial_value[start : start + size]
        start += size


def backward(pieces, slope, w_out_t, w_in, after=()):
    width, units = w_in.shape
    outs = (((512, units), BF),) + (((128, width), BF),) * 3 + (((64, width), BF),) * 2
    args = (*pieces, slope, w_out_t, w_in)
    dhidden, *partials = call(backward_kernel, outs, args, "backward", after)
    return dhidden, partials


def middle_kernel(rgt, lft, far0, far1, rgt_out, lft_out):
    top, low = pl.ds(0, 64), pl.ds(64, 64)
    rgt_out[top, :] = (rgt[top, :].astype(F32) + far0[...].astype(F32)).astype(BF)
    rgt_out[low, :] = rgt[low, :]
    lft_out[top, :] = lft[top, :]
    lft_out[low, :] = (lft[low, :].astype(F32) + far1[...].astype(F32)).astype(BF)


def reduce_x(partials):
    own, lft, rgt, from_left, from_right = partials
    outs = ((rgt.shape, BF),) * 2
    rgt, lft = call(middle_kernel, outs, (rgt, lft, from_left, from_right), "middle")
    return own, right(rgt), left(lft)


def nothing(*refs):
    pass


def after(value, *others):
    return pl.pallas_call(
        nothing,
        out_shape=jax.ShapeDtypeStruct(value.shape, value.dtype),
        in_specs=[ANY] * (1 + len(others)),
        out_specs=ANY,
        input_output_aliases={0: 0},
        compiler_params=PARAMS,
        cost_estimate=pl.CostEstimate(flops=0, bytes_accessed=0, transcendentals=0),
        name="after",
    )(value, *others)


def total_kernel(z_ref, *refs):
    out_ref = refs[-1]
    for i, start in enumerate((z_ref[0] * 128, (1 - z_ref[0]) * 128)):
        value = sum(ref[...].astype(F32) for ref in refs[3 * i : 3 * i + 3])
        out_ref[pl.ds(pl.multiple_of(start, 128), 128), :] = value.astype(BF)


def total(z, near, far, later):
    width = near[0].shape[1]
    return pl.pallas_call(
        total_kernel,
        out_shape=jax.ShapeDtypeStruct((256, width), BF),
        in_specs=[SMEM] + [VMEM] * 6 + [ANY] * len(later),
        out_specs=VMEM,
        compiler_params=PARAMS,
        cost_estimate=pl.CostEstimate(flops=0, bytes_accessed=0, transcendentals=0),
        name="total",
    )(z, *near, *far, *later)


def finish_kernel(back_ref, expert_ref, slot_ref, out_ref):
    returned = (back_ref[:128, :].astype(F32) + back_ref[128:, :].astype(F32)).astype(BF)
    out_ref[...] = dot(returned, placing_of(expert_ref[...], slot_ref[...]), 0, 0).astype(BF)


def finish(back, expert, slot):
    width = back.shape[1]
    outs = (((width, 128), BF),)
    return call(finish_kernel, outs, (back, expert, slot), "finish")[0]


def weights_kernel(*refs):
    pieces, b0, b1, out, rows, b, blocks, sems, b_sems, out_sems = refs[:8], *refs[8:]
    width = out.shape[0]
    cut = 1024
    loads = []
    for part, at in enumerate((pl.ds(0, cut), pl.ds(cut, width - cut))):
        loads.append(
            [
                pltpu.make_async_copy(piece.at[:, at], rows.at[pl.ds(i * 128, 128), at], sems.at[part * 8 + i])
                for i, piece in enumerate(pieces)
            ]
        )
    loads[0] += [
        pltpu.make_async_copy(half, b.at[pl.ds(i * 512, 512), :], b_sems.at[i]) for i, half in enumerate((b0, b1))
    ]
    for part in loads:
        for copy in part:
            copy.start()
    writes = []
    for i, start in enumerate(range(0, width, 256)):
        if start in (0, cut):
            for copy in loads[start // cut]:
                copy.wait()
        size = min(256, width - start)
        if i >= 2:
            writes[i - 2].wait()
        block = blocks.at[i % 2, pl.ds(0, size), :]
        block[...] = dot(rows[:, pl.ds(start, size)], b[...], 0, 0).astype(BF)
        writes.append(pltpu.make_async_copy(block, out.at[pl.ds(start, size), :], out_sems.at[i % 2]))
        writes[i].start()
    for write in writes[-2:]:
        write.wait()


def weights(pieces, b0, b1):
    width, units = pieces[0].shape[1], b0.shape[1]
    args = [pltpu.with_memory_space_constraint(a, pltpu.HBM) for a in (*pieces, b0, b1)]
    return pl.pallas_call(
        weights_kernel,
        out_shape=pltpu.HBM((width, units), BF),
        in_specs=[pl.BlockSpec(memory_space=pltpu.HBM)] * 10,
        out_specs=pl.BlockSpec(memory_space=pltpu.HBM),
        scratch_shapes=[
            pltpu.VMEM((1024, width), BF),
            pltpu.VMEM((1024, units), BF),
            pltpu.VMEM((2, 256, units), BF),
            pltpu.SemaphoreType.DMA((16,)),
            pltpu.SemaphoreType.DMA((2,)),
            pltpu.SemaphoreType.DMA((2,)),
        ],
        compiler_params=PARAMS,
        cost_estimate=pl.CostEstimate(
            flops=2 * 1024 * width * units, bytes_accessed=10 << 20, transcendentals=0
        ),
        name="weights",
    )(*args)


def move(value, axis, pairs):
    blocks = value.reshape(-1, 64, value.shape[1])
    return lax.ppermute(blocks, axis, pairs).reshape(value.shape)


def right(value):
    return move(value, "x", RIGHT)


def left(value):
    return move(value, "x", LEFT)


def opposite(value):
    return move(value, "x", ACROSS)


def other_z(value):
    return move(value, "zl", SWAP)


def exchange(value, axes):
    blocks = value.reshape(-1, 8, value.shape[1])
    return lax.all_to_all(blocks, axes, split_axis=0, concat_axis=0, tiled=True).reshape(value.shape)


def per_device(grad_out, expert_id, slot, gate_prob, saved_inputs, w_in, w_out):
    width = grad_out.shape[1]
    expert = expert_id.reshape(1, -1)
    place = slot.reshape(1, -1)
    first = w_in[0]
    second = w_out[0].T
    z = lax.axis_index("zl").astype(jnp.int32).reshape(1)

    x_own = saved_inputs[0].reshape(128, width)
    x_lft, x_rgt, x_far, xz_own = right(x_own), left(x_own), opposite(x_own), other_z(x_own)
    g_own = exchange(prepare(grad_out.T, expert, place, gate_prob.reshape(1, -1)), WIDE)
    g_own = after(g_own, x_lft, x_rgt, x_far, xz_own)

    g_lft, g_rgt, gz_own = right(g_own), left(g_own), other_z(g_own)
    xz_lft = other_z(x_lft)

    gz_own = after(gz_own, g_lft, g_rgt)
    gz_lft, g_far, xz_rgt = right(gz_own), left(g_rgt), other_z(x_rgt)
    hidden, slope = forward((x_own, x_lft, x_rgt, x_far), first)

    gz_lft = after(gz_lft, g_far, xz_lft)
    gz_own = after(gz_own, gz_lft)
    gz_far, gz_rgt, xz_far = right(gz_lft), left(gz_own), other_z(x_far)
    dhidden, (*partials, far0, far1) = backward((g_own, g_lft, g_rgt, g_far), slope, second, first)
    arrived = right(far0), left(far1)
    summands = reduce_x((*partials, *arrived))

    hidden_z, slope_z = forward((xz_own, xz_lft, xz_rgt, xz_far), first, arrived)
    dhidden_z, (*partials_z, far0, far1) = backward((gz_own, gz_lft, gz_rgt, gz_far), slope_z, second, first)
    summands_z = reduce_x((*partials_z, right(far0), left(far1)))
    grad_out_w = weights((g_own, g_lft, g_rgt, g_far, gz_own, gz_lft, gz_rgt, gz_far), hidden, hidden_z)
    grad_in = weights((x_own, x_lft, x_rgt, x_far, xz_own, xz_lft, xz_rgt, xz_far), dhidden, dhidden_z)
    came_back = exchange(total(z, summands, summands_z, ()), WIDE_AND_Z)
    tokens = finish(came_back, expert, place)
    return (tokens.T, grad_in[None], grad_out_w.T[None])


def solution(mesh):
    fine = Mesh(mesh.devices.reshape(4, 2, 2, 4, 2), AXES)
    every = WIDE + LOCAL
    placed = (
        P(every, None),
        P(every),
        P(every),
        P(every),
        P(WIDE, None, LOCAL, None),
        P(WIDE, None, LOCAL),
        P(WIDE, LOCAL, None),
    )
    return jax.shard_map(
        per_device,
        mesh=fine,
        in_specs=placed,
        out_specs=(P(every, None), P(WIDE, None, LOCAL), P(WIDE, LOCAL, None)),
        check_vma=False,
    )
```

time: 263 us -> 153 us (0.58)
  waiting for transfers between devices: 167 us -> 52.1 us
  matrix products: 40.4 us -> 0 us
  Pallas kernels: 0 us -> 40.1 us
  blocking collectives: 0 us -> 21.7 us
  between operations: 14.1 us -> 1 us
  starting transfers between devices: 23 us -> 34.8 us
  local copies, waits for them, and re-layouts: 13.2 us -> 3.56 us
  other arithmetic: 4.42 us -> 0 us
    all_gather x1 -> x0, waiting for transfers between devices: 127 us -> none  [per_device(): inputs = lax.all_gather(saved_inputs[0], 'local', axis=1, tiled=True)]
    ppermute x0 -> x22, waiting for transfers between devices: none -> 52.1 us  [move(): return lax.ppermute(blocks, axis, pairs).reshape(value.shape)]
    dot_general x7 -> x0, matrix products: 40.4 us -> none  [the longest x5 31.4 us: contract(): lax.dot_general(left, right, (((left_dim,), (right_dim,)), ((), ())), pre...]
    pallas_call x0 -> x15, Pallas kernels: none -> 40.1 us  [the longest x2 19.6 us: weights(): pl.pallas_call(weights_kernel, out_shape=pltpu.HBM((width, units), BF), i...]
    all_to_all x2 -> x1, waiting for transfers between devices: 39.4 us -> 0.01 us  [exchange(): lax.all_to_all(blocks, axes, split_axis=0, concat_axis=0, tiled=True)]
    ppermute x0 -> x22, starting transfers between devices: none -> 26.2 us  [move(): return lax.ppermute(blocks, axis, pairs).reshape(value.shape)]
    all_to_all x0 -> x1, blocking collectives: none -> 21.7 us  [exchange(): lax.all_to_all(blocks, axes, split_axis=0, concat_axis=0, tiled=True)]
    all_to_all x2 -> x1, starting transfers between devices: 23 us -> 8.58 us  [exchange(): lax.all_to_all(blocks, axes, split_axis=0, concat_axis=0, tiled=True)]
  transfers between devices with their start and end apart: 3 -> 23, of which waited for: 2 -> 8; matrix products, arithmetic and copies ran while one was open for 13% -> 0% of each run, Pallas kernels for 0% -> 21%
where the time goes in v2:
time: 153 us
  waiting for transfers between devices  52.1 us (34%)
  Pallas kernels  40.1 us (26%)
  starting transfers between devices  34.8 us (23%)
  blocking collectives  21.7 us (14%)
  local copies, waits for them, and re-layouts  3.56 us (2%)
    ppermute x22, waiting for transfers between devices, move(): return lax.ppermute(blocks, axis, pairs).reshape(value.shape)  52.1 us
    ppermute x22, starting transfers between devices, move(): return lax.ppermute(blocks, axis, pairs).reshape(value.shape)  26.2 us
    all_to_all x1, blocking collectives, exchange(): lax.all_to_all(blocks, axes, split_axis=0, concat_axis=0, tiled=True)  21.7 us
    pallas_call x2, Pallas kernels, weights(): pl.pallas_call(weights_kernel, out_shape=pltpu.HBM((width, units), BF), i...  19.6 us
    pallas_call x7, Pallas kernels, call(): pl.pallas_call(ordered, out_shape=tuple((jax.ShapeDtypeStruct(s, d) for s...  17.6 us
    all_to_all x1, starting transfers between devices, exchange(): lax.all_to_all(blocks, axes, split_axis=0, concat_axis=0, tiled=True)  8.58 us
    unnamed x52, local copies, waits for them, and re-layouts  3.56 us
  transfers between devices with their start and end apart: 23, of which 8 were waited for; matrix products, arithmetic and copies ran while one was open for 0% of the time, Pallas kernels for 21%

profile of v2, /device:TPU:1, one launch (start us, length us, event | category | flops | bytes accessed | tf_op | source)
XLA Modules:
  0.0 153.2 jit_solution(5537071982721219691)
XLA Ops:
  0.6 2.1 %collective-permute-start = (bf16[2,64,2080]{2,1,0:T(8,128)(2,1)}, bf16[2,64,2080]{2,1,0:T(8,128)(2,1)S(1)}, u32[]{:S(2)}, u32[]{:S(2)}) collective-permute-start(bf16[2,64,2080]{2,1,0:T(8,128)(2,1)} %bitcast.111), channel_id=1, source_target_pairs={{0,2},{2,4},{4,6},{6,0},{1,3},{3,5},{5,7},{7,1},{8,10},{10,12},{12... | collective-permute-start | bytes 1597448 | tf_op jit(solution)/shard_map/ppermute | solution.py:244
  2.7 1.4 collective-permute-start.1
  4.1 1.6 %collective-permute-start.2 = (bf16[2,64,2080]{2,1,0:T(8,128)(2,1)}, bf16[2,64,2080]{2,1,0:T(8,128)(2,1)S(1)}, u32[]{:S(2)}, u32[]{:S(2)}) collective-permute-start(bf16[2,64,2080]{2,1,0:T(8,128)(2,1)} %bitcast.113), channel_id=1, source_target_pairs={{0,4},{2,6},{4,0},{6,2},{1,5},{3,7},{5,1},{7,3},{8,12},{10,14},{12... | collective-permute-start | bytes 1597448 | tf_op jit(solution)/shard_map/ppermute | solution.py:244
  5.7 1.6 %collective-permute-start.3 = (bf16[2,64,2080]{2,1,0:T(8,128)(2,1)}, bf16[2,64,2080]{2,1,0:T(8,128)(2,1)S(1)}, u32[]{:S(2)}, u32[]{:S(2)}) collective-permute-start(bf16[2,64,2080]{2,1,0:T(8,128)(2,1)} %bitcast.114), channel_id=1, source_target_pairs={{0,1},{1,0},{2,3},{3,2},{4,5},{5,4},{6,7},{7,6},{8,9},{9,8},{10,11... | collective-permute-start | bytes 1597448 | tf_op jit(solution)/shard_map/ppermute | solution.py:244
  7.4 1.4 prepare.1
  8.8 21.7 %all_to_all.10 = bf16[16,8,2080]{2,1,0:T(8,128)(2,1)S(1)} all-to-all(bf16[16,8,2080]{2,1,0:T(8,128)(2,1)S(1)} %bitcast.94), channel_id=1, replica_groups=mesh['y'=4,'zh'=2,'core'=2,'x'=4,'zl'=2] {'y','zh','core'}, dimensions={0} | all-to-all | bytes 1064960 | tf_op jit(solution)/shard_map/all_to_all | solution.py:265
  30.5 0.0 collective-permute-done
  30.5 0.0 collective-permute-done.1
  30.5 0.0 collective-permute-done.2
  30.5 0.0 collective-permute-done.3
  30.5 0.0 copy-start
  30.6 0.0 copy-start.19
  30.6 0.4 collective-permute-start.4
  30.9 2.4 %collective-permute-start.5 = (bf16[2,64,2080]{2,1,0:T(8,128)(2,1)S(1)}, bf16[2,64,2080]{2,1,0:T(8,128)(2,1)S(1)}, u32[]{:S(2)}, u32[]{:S(2)}) collective-permute-start(bf16[2,64,2080]{2,1,0:T(8,128)(2,1)S(1)} %bitcast.62), channel_id=1, source_target_pairs={{0,6},{2,0},{4,2},{6,4},{1,7},{3,1},{5,3},{7,5},{8,14},{10,8},{12,... | collective-permute-start | bytes 1597448 | tf_op jit(solution)/shard_map/ppermute | solution.py:244
  33.3 0.5 collective-permute-start.11
  33.8 1.0 collective-permute-start.13
  34.8 10.9 %collective-permute-done.4 = bf16[2,64,2080]{2,1,0:T(8,128)(2,1)S(1)} collective-permute-done((bf16[2,64,2080]{2,1,0:T(8,128)(2,1)S(1)}, bf16[2,64,2080]{2,1,0:T(8,128)(2,1)S(1)}, u32[]{:S(2)}, u32[]{:S(2)}) %collective-permute-start.4) | collective-permute-done | bytes 532512 | tf_op jit(solution)/shard_map/ppermute | solution.py:244
  45.7 0.0 collective-permute-done.5
  45.7 0.8 collective-permute-done.11
  46.5 1.5 %collective-permute-start.6 = (bf16[2,64,2080]{2,1,0:T(8,128)(2,1)S(1)}, bf16[2,64,2080]{2,1,0:T(8,128)(2,1)S(1)}, u32[]{:S(2)}, u32[]{:S(2)}) collective-permute-start(bf16[2,64,2080]{2,1,0:T(8,128)(2,1)S(1)} %collective-permute-done.5), channel_id=1, source_target_pairs={{0,6},{2,0},{4,2},{6,4},{1,7},{3,1},{5,3},{7,5},{8,14},{10,8},{12,... | collective-permute-start | bytes 1597448 | tf_op jit(solution)/shard_map/ppermute | solution.py:244
  48.0 0.0 collective-permute-start.12
  48.0 0.0 collective-permute-start.16
  48.0 1.5 collective-permute-start.17
  49.5 8.9 %collective-permute-done.13 = bf16[2,64,2080]{2,1,0:T(8,128)(2,1)S(1)} collective-permute-done((bf16[2,64,2080]{2,1,0:T(8,128)(2,1)S(1)}, bf16[2,64,2080]{2,1,0:T(8,128)(2,1)S(1)}, u32[]{:S(2)}, u32[]{:S(2)}) %collective-permute-start.13) | collective-permute-done | bytes 532512 | tf_op jit(solution)/shard_map/ppermute | solution.py:244
  58.4 0.0 collective-permute-done.6
  58.4 2.4 %collective-permute-done.12 = bf16[2,64,2080]{2,1,0:T(8,128)(2,1)S(1)} collective-permute-done((bf16[2,64,2080]{2,1,0:T(8,128)(2,1)S(1)}, bf16[2,64,2080]{2,1,0:T(8,128)(2,1)S(1)}, u32[]{:S(2)}, u32[]{:S(2)}) %collective-permute-start.12) | collective-permute-done | bytes 532512 | tf_op jit(solution)/shard_map/ppermute | solution.py:244
  60.9 0.4 collective-permute-start.14
  61.2 1.2 collective-permute-start.15
  62.4 2.3 %forward.2 = (bf16[512,768]{1,0:T(8,128)(2,1)S(1)}, f32[512,768]{1,0:T(8,128)S(1)}) custom-call(bf16[128,2080]{1,0:T(8,128)(2,1)S(1)} %bitcast.116, bf16[128,2080]{1,0:T(8,128)(2,1)S(1)} %bitcast.86, bf16[128,2080]{1,0:T(8,128)(2,1)S(1)} %bitcast.89, bf16[128,2080]{1,0:T(8,128)(2,1)S(1)} %bitcast.92, bf16[2080,768]{1,0:T(8,128)(2,1)S(1)} %bitcast.54), custom_call_target="tpu_custom_call" | custom-call | tf_op jit(solution)/shard_map/forward/pallas_call | solution.py:32
  64.8 0.9 copy-done.22
  65.7 4.8 %backward.2 = (bf16[512,768]{1,0:T(8,128)(2,1)S(1)}, bf16[128,2080]{1,0:T(8,128)(2,1)S(1)}, bf16[128,2080]{1,0:T(8,128)(2,1)S(1)}, bf16[128,2080]{1,0:T(8,128)(2...) custom-call(bf16[128,2080]{1,0:T(8,128)(2,1)S(1)} %after.4.refs_0_, bf16[128,2080]{1,0:T(8,128)(2,1)S(1)} %bitcast.74, ...), custom_call_target="tpu_custom_call" | custom-call | tf_op jit(solution)/shard_map/backward/pallas_call | solution.py:32
  70.5 0.0 copy-start.17
  70.5 0.8 copy-done.17
  71.3 0.9 copy-done.23
  72.1 0.0 collective-permute-start.7
  72.2 0.0 collective-permute-done.16
  72.2 2.7 %collective-permute-start.8 = (bf16[1,64,2080]{2,1,0:T(8,128)(2,1)S(1)}, bf16[1,64,2080]{2,1,0:T(8,128)(2,1)S(1)}, u32[]{:S(2)}, u32[]{:S(2)}) collective-permute-start(bf16[1,64,2080]{2,1,0:T(8,128)(2,1)S(1)} %bitcast.125), channel_id=1, source_target_pairs={{0,6},{2,0},{4,2},{6,4},{1,7},{3,1},{5,3},{7,5},{8,14},{10,8},{12,... | collective-permute-start | bytes 798728 | tf_op jit(solution)/shard_map/ppermute | solution.py:244
  74.8 7.5 %collective-permute-done.17 = bf16[2,64,2080]{2,1,0:T(8,128)(2,1)S(1)} collective-permute-done((bf16[2,64,2080]{2,1,0:T(8,128)(2,1)S(1)}, bf16[2,64,2080]{2,1,0:T(8,128)(2,1)S(1)}, u32[]{:S(2)}, u32[]{:S(2)}) %collective-permute-start.17) | collective-permute-done | bytes 532512 | tf_op jit(solution)/shard_map/ppermute | solution.py:244
  82.3 0.0 collective-permute-done.7
  82.3 2.3 %forward.3 = (bf16[512,768]{1,0:T(8,128)(2,1)S(1)}, f32[512,768]{1,0:T(8,128)S(1)}) custom-call(bf16[128,2080]{1,0:T(8,128)(2,1)S(1)} %bitcast.71, bf16[128,2080]{1,0:T(8,128)(2,1)S(1)} %bitcast.80, bf16[128,2080]{1,0:T(8,128)(2,1)S(1)} %bitcast.99, bf16[128,2080]{1,0:T(8,128)(2,1)S(1)} %bitcast.101, bf16[2080,768]{1,0:T(8,128)(2,1)S(1)} %bitcast.56, ...), custom_call_target="tpu_custom_call" | custom-call | tf_op jit(solution)/shard_map/forward/pallas_call | solution.py:32
  84.7 0.0 collective-permute-done.14
  84.7 0.0 collective-permute-done.15
  84.7 4.8 %backward.3 = (bf16[512,768]{1,0:T(8,128)(2,1)S(1)}, bf16[128,2080]{1,0:T(8,128)(2,1)S(1)}, bf16[128,2080]{1,0:T(8,128)(2,1)S(1)}, bf16[128,2080]{1,0:T(8,128)(2...) custom-call(bf16[128,2080]{1,0:T(8,128)(2,1)S(1)} %after.7.refs_0_.refs_4_, ...), custom_call_target="tpu_custom_call" | custom-call | tf_op jit(solution)/shard_map/backward/pallas_call | solution.py:32
  89.6 0.9 copy-done.25
  90.5 2.7 %collective-permute-start.19 = (bf16[1,64,2080]{2,1,0:T(8,128)(2,1)S(1)}, bf16[1,64,2080]{2,1,0:T(8,128)(2,1)S(1)}, u32[]{:S(2)}, u32[]{:S(2)}) collective-permute-start(bf16[1,64,2080]{2,1,0:T(8,128)(2,1)S(1)} %bitcast.123), channel_id=1, source_target_pairs={{0,6},{2,0},{4,2},{6,4},{1,7},{3,1},{5,3},{7,5},{8,14},{10,8},{12,... | collective-permute-start | bytes 798728 | tf_op jit(solution)/shard_map/ppermute | solution.py:244
  93.1 1.1 middle.2
  94.3 0.0 collective-permute-start.9
  94.3 2.7 %collective-permute-start.10 = (bf16[2,64,2080]{2,1,0:T(8,128)(2,1)}, bf16[2,64,2080]{2,1,0:T(8,128)(2,1)S(1)}, u32[]{:S(2)}, u32[]{:S(2)}) collective-permute-start(bf16[2,64,2080]{2,1,0:T(8,128)(2,1)} %bitcast.26), channel_id=1, source_target_pairs={{0,6},{2,0},{4,2},{6,4},{1,7},{3,1},{5,3},{7,5},{8,14},{10,8},{12,... | collective-permute-start | bytes 1597448 | tf_op jit(solution)/shard_map/ppermute | solution.py:244
  97.0 1.0 collective-permute-done.18
  98.0 0.0 collective-permute-done.19
  98.0 1.2 middle.3
  99.1 0.0 collective-permute-start.20
  99.1 2.7 %collective-permute-start.21 = (bf16[2,64,2080]{2,1,0:T(8,128)(2,1)}, bf16[2,64,2080]{2,1,0:T(8,128)(2,1)S(1)}, u32[]{:S(2)}, u32[]{:S(2)}) collective-permute-start(bf16[2,64,2080]{2,1,0:T(8,128)(2,1)} %bitcast.45), channel_id=1, source_target_pairs={{0,6},{2,0},{4,2},{6,4},{1,7},{3,1},{5,3},{7,5},{8,14},{10,8},{12,... | collective-permute-start | bytes 1597448 | tf_op jit(solution)/shard_map/ppermute | solution.py:244
  101.8 8.6 %collective-permute-done.9 = bf16[2,64,2080]{2,1,0:T(8,128)(2,1)S(1)} collective-permute-done((bf16[2,64,2080]{2,1,0:T(8,128)(2,1)}, bf16[2,64,2080]{2,1,0:T(8,128)(2,1)S(1)}, u32[]{:S(2)}, u32[]{:S(2)}) %collective-permute-start.9) | collective-permute-done | bytes 532512 | tf_op jit(solution)/shard_map/ppermute | solution.py:244
  110.4 0.0 collective-permute-done.10
  110.4 11.9 %collective-permute-done.20 = bf16[2,64,2080]{2,1,0:T(8,128)(2,1)S(1)} collective-permute-done((bf16[2,64,2080]{2,1,0:T(8,128)(2,1)}, bf16[2,64,2080]{2,1,0:T(8,128)(2,1)S(1)}, u32[]{:S(2)}, u32[]{:S(2)}) %collective-permute-start.20) | collective-permute-done | bytes 532512 | tf_op jit(solution)/shard_map/ppermute | solution.py:244
  122.3 1.4 total.1
  123.8 8.6 %all-to-all-start.1 = ((bf16[32,8,2080]{2,1,0:T(8,128)(2,1)}), bf16[32,8,2080]{2,1,0:T(8,128)(2,1)S(1)}, u32[]{:S(2)}, u32[]{:S(2)}) async-start(bf16[32,8,2080]{2,1,0:T(8,128)(2,1)} %bitcast.47), calls=%async_computation.1 | async-start | bytes 2228224 | tf_op jit(solution)/shard_map/all_to_all | solution.py:265
  132.4 9.8 %weights.2 = bf16[2080,768]{1,0:T(8,128)(2,1)} custom-call(bf16[128,2080]{1,0:T(8,128)(2,1)} %bitcast.115, bf16[128,2080]{1,0:T(8,128)(2,1)} %bitcast.87, bf16[128,2080]{1,0:T(8,128)(2,1)} %bitcast.90, bf16[128,2080]{1,0:T(8,128)(2,1)} %bitcast.93, bf16[128,2080]{1,0:T(8,128)(2,1)} %bitcast.72, bf16[128,2080]{1,0:T(8,128)(2,1)} %bitcast.81, ...), custom_call_target="tpu_custom_call" | custom-call | flops 3271557120 | bytes 10485760 | tf_op jit(solution)/shard_map/weights/pallas_call | solution.py:221
  142.2 0.0 copy-start.20
  142.2 0.0 copy-start.21
  142.2 9.8 %weights.3 = bf16[2080,768]{1,0:T(8,128)(2,1)} custom-call(bf16[128,2080]{1,0:T(8,128)(2,1)} %copy-done.2, bf16[128,2080]{1,0:T(8,128)(2,1)} %bitcast.75, bf16[128,2080]{1,0:T(8,128)(2,1)} %bitcast.78, bf16[128,2080]{1,0:T(8,128)(2,1)} %bitcast.84, bf16[128,2080]{1,0:T(8,128)(2,1)} %copy-done.4, bf16[128,2080]{1,0:T(8,128)(2,1)} %copy-done.3, ...), custom_call_target="tpu_custom_call" | custom-call | flops 3271557120 | bytes 10485760 | tf_op jit(solution)/shard_map/weights/pallas_call | solution.py:221
  152.0 0.0 all-to-all-done.1
  152.0 1.1 finish.1
  (50 shorter events, 0.1 us)
Async XLA Ops:
  0.6 29.8 %collective-permute-start = (bf16[2,64,2080]{2,1,0:T(8,128)(2,1)}, bf16[2,64,2080]{2,1,0:T(8,128)(2,1)S(1)}, u32[]{:S(2)}, u32[]{:S(2)}) collective-permute-start(bf16[2,64,2080]{2,1,0:T(8,128)(2,1)} %bitcast.111), channel_id=1, source_target_pairs={{0,2},{2,4},{4,6},{6,0},{1,3},{3,5},{5,7},{7,1},{8,10},{10,12},{12... | collective-permute-start | bytes 1597448 | tf_op jit(solution)/shard_map/ppermute | solution.py:244
  2.7 27.7 %collective-permute-start.1 = (bf16[2,64,2080]{2,1,0:T(8,128)(2,1)}, bf16[2,64,2080]{2,1,0:T(8,128)(2,1)S(1)}, u32[]{:S(2)}, u32[]{:S(2)}) collective-permute-start(bf16[2,64,2080]{2,1,0:T(8,128)(2,1)} %bitcast.112), channel_id=1, source_target_pairs={{0,6},{2,0},{4,2},{6,4},{1,7},{3,1},{5,3},{7,5},{8,14},{10,8},{12,... | collective-permute-start | bytes 1597448 | tf_op jit(solution)/shard_map/ppermute | solution.py:244
  4.1 26.4 %collective-permute-start.2 = (bf16[2,64,2080]{2,1,0:T(8,128)(2,1)}, bf16[2,64,2080]{2,1,0:T(8,128)(2,1)S(1)}, u32[]{:S(2)}, u32[]{:S(2)}) collective-permute-start(bf16[2,64,2080]{2,1,0:T(8,128)(2,1)} %bitcast.113), channel_id=1, source_target_pairs={{0,4},{2,6},{4,0},{6,2},{1,5},{3,7},{5,1},{7,3},{8,12},{10,14},{12... | collective-permute-start | bytes 1597448 | tf_op jit(solution)/shard_map/ppermute | solution.py:244
  5.7 24.8 %collective-permute-start.3 = (bf16[2,64,2080]{2,1,0:T(8,128)(2,1)}, bf16[2,64,2080]{2,1,0:T(8,128)(2,1)S(1)}, u32[]{:S(2)}, u32[]{:S(2)}) collective-permute-start(bf16[2,64,2080]{2,1,0:T(8,128)(2,1)} %bitcast.114), channel_id=1, source_target_pairs={{0,1},{1,0},{2,3},{3,2},{4,5},{5,4},{6,7},{7,6},{8,9},{9,8},{10,11... | collective-permute-start | bytes 1597448 | tf_op jit(solution)/shard_map/ppermute | solution.py:244
  30.5 31.9 %copy-start.10 = (bf16[2,64,2080]{2,1,0:T(8,128)(2,1)}, bf16[2,64,2080]{2,1,0:T(8,128)(2,1)S(1)}, u32[]{:S(2)}) copy-start(bf16[2,64,2080]{2,1,0:T(8,128)(2,1)S(1)} %collective-permute-done) | copy-start | bytes 1597444
  30.5 31.9 %copy-start.11 = (bf16[2,64,2080]{2,1,0:T(8,128)(2,1)}, bf16[2,64,2080]{2,1,0:T(8,128)(2,1)S(1)}, u32[]{:S(2)}) copy-start(bf16[2,64,2080]{2,1,0:T(8,128)(2,1)S(1)} %collective-permute-done.1) | copy-start | bytes 1597444
  30.5 31.9 %copy-start.12 = (bf16[2,64,2080]{2,1,0:T(8,128)(2,1)}, bf16[2,64,2080]{2,1,0:T(8,128)(2,1)S(1)}, u32[]{:S(2)}) copy-start(bf16[2,64,2080]{2,1,0:T(8,128)(2,1)S(1)} %collective-permute-done.2) | copy-start | bytes 1597444
  30.5 51.8 %copy-start.5 = (bf16[2,64,2080]{2,1,0:T(8,128)(2,1)}, bf16[2,64,2080]{2,1,0:T(8,128)(2,1)S(1)}, u32[]{:S(2)}) copy-start(bf16[2,64,2080]{2,1,0:T(8,128)(2,1)S(1)} %collective-permute-done.3) | copy-start | bytes 1597444
  30.5 35.1 %copy-start.2 = (bf16[128,2080]{1,0:T(8,128)(2,1)}, bf16[128,2080]{1,0:T(8,128)(2,1)S(1)}, u32[]{:S(2)}) copy-start(bf16[128,2080]{1,0:T(8,128)(2,1)S(1)} %after.4.refs_0_) | copy-start | bytes 1597444
  30.5 31.9 %copy-start = (bf16[1,2080,768]{2,1,0:T(8,128)(2,1)S(1)}, bf16[1,2080,768]{2,1,0:T(8,128)(2,1)}, u32[]{:S(2)}) copy-start(bf16[1,2080,768]{2,1,0:T(8,128)(2,1)} %param.12) | copy-start | bytes 9584644
  30.6 31.9 %copy-start.19 = (bf16[1,16,8,2080]{3,2,1,0:T(8,128)(2,1)S(1)}, bf16[1,16,8,2080]{3,2,1,0:T(8,128)(2,1)}, u32[]{:S(2)}) copy-start(bf16[1,16,8,2080]{3,2,1,0:T(8,128)(2,1)} %param.11) | copy-start | bytes 1597444
  30.6 15.1 %collective-permute-start.4 = (bf16[2,64,2080]{2,1,0:T(8,128)(2,1)S(1)}, bf16[2,64,2080]{2,1,0:T(8,128)(2,1)S(1)}, u32[]{:S(2)}, u32[]{:S(2)}) collective-permute-start(bf16[2,64,2080]{2,1,0:T(8,128)(2,1)S(1)} %bitcast.61), channel_id=1, source_target_pairs={{0,2},{2,4},{4,6},{6,0},{1,3},{3,5},{5,7},{7,1},{8,10},{10,12},{12... | collective-permute-start | bytes 1597448 | tf_op jit(solution)/shard_map/ppermute | solution.py:244
  30.9 14.7 %collective-permute-start.5 = (bf16[2,64,2080]{2,1,0:T(8,128)(2,1)S(1)}, bf16[2,64,2080]{2,1,0:T(8,128)(2,1)S(1)}, u32[]{:S(2)}, u32[]{:S(2)}) collective-permute-start(bf16[2,64,2080]{2,1,0:T(8,128)(2,1)S(1)} %bitcast.62), channel_id=1, source_target_pairs={{0,6},{2,0},{4,2},{6,4},{1,7},{3,1},{5,3},{7,5},{8,14},{10,8},{12,... | collective-permute-start | bytes 1597448 | tf_op jit(solution)/shard_map/ppermute | solution.py:244
  33.3 13.2 %collective-permute-start.11 = (bf16[2,64,2080]{2,1,0:T(8,128)(2,1)S(1)}, bf16[2,64,2080]{2,1,0:T(8,128)(2,1)S(1)}, u32[]{:S(2)}, u32[]{:S(2)}) collective-permute-start(bf16[2,64,2080]{2,1,0:T(8,128)(2,1)S(1)} %bitcast.63), channel_id=1, source_target_pairs={{0,1},{1,0},{2,3},{3,2},{4,5},{5,4},{6,7},{7,6},{8,9},{9,8},{10,11... | collective-permute-start | bytes 1597448 | tf_op jit(solution)/shard_map/ppermute | solution.py:244
  33.8 24.6 %collective-permute-start.13 = (bf16[2,64,2080]{2,1,0:T(8,128)(2,1)S(1)}, bf16[2,64,2080]{2,1,0:T(8,128)(2,1)S(1)}, u32[]{:S(2)}, u32[]{:S(2)}) collective-permute-start(bf16[2,64,2080]{2,1,0:T(8,128)(2,1)S(1)} %collective-permute-done), channel_id=1, source_target_pairs={{0,1},{1,0},{2,3},{3,2},{4,5},{5,4},{6,7},{7,6},{8,9},{9,8},{10,11... | collective-permute-start | bytes 1597448 | tf_op jit(solution)/shard_map/ppermute | solution.py:244
  45.7 20.0 %copy-start.6 = (bf16[2,64,2080]{2,1,0:T(8,128)(2,1)}, bf16[2,64,2080]{2,1,0:T(8,128)(2,1)S(1)}, u32[]{:S(2)}) copy-start(bf16[2,64,2080]{2,1,0:T(8,128)(2,1)S(1)} %collective-permute-done.4) | copy-start | bytes 1597444
  45.7 20.0 %copy-start.7 = (bf16[2,64,2080]{2,1,0:T(8,128)(2,1)}, bf16[2,64,2080]{2,1,0:T(8,128)(2,1)S(1)}, u32[]{:S(2)}) copy-start(bf16[2,64,2080]{2,1,0:T(8,128)(2,1)S(1)} %collective-permute-done.5) | copy-start | bytes 1597444
  46.5 11.9 %collective-permute-start.6 = (bf16[2,64,2080]{2,1,0:T(8,128)(2,1)S(1)}, bf16[2,64,2080]{2,1,0:T(8,128)(2,1)S(1)}, u32[]{:S(2)}, u32[]{:S(2)}) collective-permute-start(bf16[2,64,2080]{2,1,0:T(8,128)(2,1)S(1)} %collective-permute-done.5), channel_id=1, source_target_pairs={{0,6},{2,0},{4,2},{6,4},{1,7},{3,1},{5,3},{7,5},{8,14},{10,8},{12,... | collective-permute-start | bytes 1597448 | tf_op jit(solution)/shard_map/ppermute | solution.py:244
  48.0 12.8 %collective-permute-start.12 = (bf16[2,64,2080]{2,1,0:T(8,128)(2,1)S(1)}, bf16[2,64,2080]{2,1,0:T(8,128)(2,1)S(1)}, u32[]{:S(2)}, u32[]{:S(2)}) collective-permute-start(bf16[2,64,2080]{2,1,0:T(8,128)(2,1)S(1)} %bitcast.67), channel_id=1, source_target_pairs={{0,2},{2,4},{4,6},{6,0},{1,3},{3,5},{5,7},{7,1},{8,10},{10,12},{12... | collective-permute-start | bytes 1597448 | tf_op jit(solution)/shard_map/ppermute | solution.py:244
  48.0 24.1 %collective-permute-start.16 = (bf16[2,64,2080]{2,1,0:T(8,128)(2,1)S(1)}, bf16[2,64,2080]{2,1,0:T(8,128)(2,1)S(1)}, u32[]{:S(2)}, u32[]{:S(2)}) collective-permute-start(bf16[2,64,2080]{2,1,0:T(8,128)(2,1)S(1)} %collective-permute-done.1), channel_id=1, source_target_pairs={{0,1},{1,0},{2,3},{3,2},{4,5},{5,4},{6,7},{7,6},{8,9},{9,8},{10,11... | collective-permute-start | bytes 1597448 | tf_op jit(solution)/shard_map/ppermute | solution.py:244
  48.0 34.3 %collective-permute-start.17 = (bf16[2,64,2080]{2,1,0:T(8,128)(2,1)S(1)}, bf16[2,64,2080]{2,1,0:T(8,128)(2,1)S(1)}, u32[]{:S(2)}, u32[]{:S(2)}) collective-permute-start(bf16[2,64,2080]{2,1,0:T(8,128)(2,1)S(1)} %collective-permute-done.2), channel_id=1, source_target_pairs={{0,1},{1,0},{2,3},{3,2},{4,5},{5,4},{6,7},{7,6},{8,9},{9,8},{10,11... | collective-permute-start | bytes 1597448 | tf_op jit(solution)/shard_map/ppermute | solution.py:244
  58.4 23.9 %copy-start.8 = (bf16[2,64,2080]{2,1,0:T(8,128)(2,1)}, bf16[2,64,2080]{2,1,0:T(8,128)(2,1)S(1)}, u32[]{:S(2)}) copy-start(bf16[2,64,2080]{2,1,0:T(8,128)(2,1)S(1)} %collective-permute-done.13) | copy-start | bytes 1597444
  58.4 7.3 %copy-start.9 = (bf16[2,64,2080]{2,1,0:T(8,128)(2,1)}, bf16[2,64,2080]{2,1,0:T(8,128)(2,1)S(1)}, u32[]{:S(2)}) copy-start(bf16[2,64,2080]{2,1,0:T(8,128)(2,1)S(1)} %collective-permute-done.6) | copy-start | bytes 1597444
  60.9 23.9 %copy-start.3 = (bf16[128,2080]{1,0:T(8,128)(2,1)}, bf16[128,2080]{1,0:T(8,128)(2,1)S(1)}, u32[]{:S(2)}) copy-start(bf16[128,2080]{1,0:T(8,128)(2,1)S(1)} %after.6.refs_1_.refs_5_) | copy-start | bytes 1597444
  60.9 4.8 %copy-start.1 = (bf16[1,768,2080]{1,2,0:T(8,128)(2,1)S(1)}, bf16[1,768,2080]{1,2,0:T(8,128)(2,1)}, u32[]{:S(2)}) copy-start(bf16[1,768,2080]{1,2,0:T(8,128)(2,1)} %param.13) | copy-start | bytes 9584644
  60.9 23.9 %copy-start.4 = (bf16[128,2080]{1,0:T(8,128)(2,1)}, bf16[128,2080]{1,0:T(8,128)(2,1)S(1)}, u32[]{:S(2)}) copy-start(bf16[128,2080]{1,0:T(8,128)(2,1)S(1)} %after.7.refs_0_.refs_4_) | copy-start | bytes 1597444
  60.9 23.8 %collective-permute-start.14 = (bf16[2,64,2080]{2,1,0:T(8,128)(2,1)S(1)}, bf16[2,64,2080]{2,1,0:T(8,128)(2,1)S(1)}, u32[]{:S(2)}, u32[]{:S(2)}) collective-permute-start(bf16[2,64,2080]{2,1,0:T(8,128)(2,1)S(1)} %bitcast.68), channel_id=1, source_target_pairs={{0,6},{2,0},{4,2},{6,4},{1,7},{3,1},{5,3},{7,5},{8,14},{10,8},{12,... | collective-permute-start | bytes 1597448 | tf_op jit(solution)/shard_map/ppermute | solution.py:244
  61.2 23.5 %collective-permute-start.15 = (bf16[2,64,2080]{2,1,0:T(8,128)(2,1)S(1)}, bf16[2,64,2080]{2,1,0:T(8,128)(2,1)S(1)}, u32[]{:S(2)}, u32[]{:S(2)}) collective-permute-start(bf16[2,64,2080]{2,1,0:T(8,128)(2,1)S(1)} %bitcast.65), channel_id=1, source_target_pairs={{0,2},{2,4},{4,6},{6,0},{1,3},{3,5},{5,7},{7,1},{8,10},{10,12},{12... | collective-permute-start | bytes 1597448 | tf_op jit(solution)/shard_map/ppermute | solution.py:244
  64.8 0.9 copy-start.22
  70.5 0.8 copy-start.17
  71.3 0.9 copy-start.23
  72.1 10.2 %collective-permute-start.7 = (bf16[1,64,2080]{2,1,0:T(8,128)(2,1)S(1)}, bf16[1,64,2080]{2,1,0:T(8,128)(2,1)S(1)}, u32[]{:S(2)}, u32[]{:S(2)}) collective-permute-start(bf16[1,64,2080]{2,1,0:T(8,128)(2,1)S(1)} %bitcast.126), channel_id=1, source_target_pairs={{0,2},{2,4},{4,6},{6,0},{1,3},{3,5},{5,7},{7,1},{8,10},{10,12},{12... | collective-permute-start | bytes 798728 | tf_op jit(solution)/shard_map/ppermute | solution.py:244
  72.2 17.3 %copy-start.13 = (bf16[2,64,2080]{2,1,0:T(8,128)(2,1)}, bf16[2,64,2080]{2,1,0:T(8,128)(2,1)S(1)}, u32[]{:S(2)}) copy-start(bf16[2,64,2080]{2,1,0:T(8,128)(2,1)S(1)} %collective-permute-done.16) | copy-start | bytes 1597444
  72.2 10.1 %collective-permute-start.8 = (bf16[1,64,2080]{2,1,0:T(8,128)(2,1)S(1)}, bf16[1,64,2080]{2,1,0:T(8,128)(2,1)S(1)}, u32[]{:S(2)}, u32[]{:S(2)}) collective-permute-start(bf16[1,64,2080]{2,1,0:T(8,128)(2,1)S(1)} %bitcast.125), channel_id=1, source_target_pairs={{0,6},{2,0},{4,2},{6,4},{1,7},{3,1},{5,3},{7,5},{8,14},{10,8},{12,... | collective-permute-start | bytes 798728 | tf_op jit(solution)/shard_map/ppermute | solution.py:244
  82.3 7.2 %copy-start.14 = (bf16[2,64,2080]{2,1,0:T(8,128)(2,1)}, bf16[2,64,2080]{2,1,0:T(8,128)(2,1)S(1)}, u32[]{:S(2)}) copy-start(bf16[2,64,2080]{2,1,0:T(8,128)(2,1)S(1)} %collective-permute-done.17) | copy-start | bytes 1597444
  84.7 4.9 %copy-start.24 = (bf16[512,768]{1,0:T(8,128)(2,1)}, bf16[512,768]{1,0:T(8,128)(2,1)S(1)}, u32[]{:S(2)}) copy-start(bf16[512,768]{1,0:T(8,128)(2,1)S(1)} %get-tuple-element.42.refs_9_) | copy-start | bytes 2359300
  84.7 4.8 %copy-start.15 = (bf16[2,64,2080]{2,1,0:T(8,128)(2,1)}, bf16[2,64,2080]{2,1,0:T(8,128)(2,1)S(1)}, u32[]{:S(2)}) copy-start(bf16[2,64,2080]{2,1,0:T(8,128)(2,1)S(1)} %collective-permute-done.14) | copy-start | bytes 1597444
  84.7 4.8 %copy-start.16 = (bf16[2,64,2080]{2,1,0:T(8,128)(2,1)}, bf16[2,64,2080]{2,1,0:T(8,128)(2,1)S(1)}, u32[]{:S(2)}) copy-start(bf16[2,64,2080]{2,1,0:T(8,128)(2,1)S(1)} %collective-permute-done.15) | copy-start | bytes 1597444
  89.6 0.9 copy-start.25
  90.5 31.9 %copy-start.18 = (bf16[128,2080]{1,0:T(8,128)(2,1)S(1)}, bf16[128,2080]{1,0:T(8,128)(2,1)}, u32[]{:S(2)}) copy-start(bf16[128,2080]{1,0:T(8,128)(2,1)} %copy-done.17) | copy-start | bytes 1597444
  90.5 7.5 %collective-permute-start.18 = (bf16[1,64,2080]{2,1,0:T(8,128)(2,1)S(1)}, bf16[1,64,2080]{2,1,0:T(8,128)(2,1)S(1)}, u32[]{:S(2)}, u32[]{:S(2)}) collective-permute-start(bf16[1,64,2080]{2,1,0:T(8,128)(2,1)S(1)} %bitcast.124), channel_id=1, source_target_pairs={{0,2},{2,4},{4,6},{6,0},{1,3},{3,5},{5,7},{7,1},{8,10},{10,12},{12... | collective-permute-start | bytes 798728 | tf_op jit(solution)/shard_map/ppermute | solution.py:244
  90.5 7.5 %collective-permute-start.19 = (bf16[1,64,2080]{2,1,0:T(8,128)(2,1)S(1)}, bf16[1,64,2080]{2,1,0:T(8,128)(2,1)S(1)}, u32[]{:S(2)}, u32[]{:S(2)}) collective-permute-start(bf16[1,64,2080]{2,1,0:T(8,128)(2,1)S(1)} %bitcast.123), channel_id=1, source_target_pairs={{0,6},{2,0},{4,2},{6,4},{1,7},{3,1},{5,3},{7,5},{8,14},{10,8},{12,... | collective-permute-start | bytes 798728 | tf_op jit(solution)/shard_map/ppermute | solution.py:244
  94.3 16.1 %collective-permute-start.9 = (bf16[2,64,2080]{2,1,0:T(8,128)(2,1)}, bf16[2,64,2080]{2,1,0:T(8,128)(2,1)S(1)}, u32[]{:S(2)}, u32[]{:S(2)}) collective-permute-start(bf16[2,64,2080]{2,1,0:T(8,128)(2,1)} %bitcast.24), channel_id=1, source_target_pairs={{0,2},{2,4},{4,6},{6,0},{1,3},{3,5},{5,7},{7,1},{8,10},{10,12},{12... | collective-permute-start | bytes 1597448 | tf_op jit(solution)/shard_map/ppermute | solution.py:244
  94.3 16.1 %collective-permute-start.10 = (bf16[2,64,2080]{2,1,0:T(8,128)(2,1)}, bf16[2,64,2080]{2,1,0:T(8,128)(2,1)S(1)}, u32[]{:S(2)}, u32[]{:S(2)}) collective-permute-start(bf16[2,64,2080]{2,1,0:T(8,128)(2,1)} %bitcast.26), channel_id=1, source_target_pairs={{0,6},{2,0},{4,2},{6,4},{1,7},{3,1},{5,3},{7,5},{8,14},{10,8},{12,... | collective-permute-start | bytes 1597448 | tf_op jit(solution)/shard_map/ppermute | solution.py:244
  99.1 23.2 %collective-permute-start.20 = (bf16[2,64,2080]{2,1,0:T(8,128)(2,1)}, bf16[2,64,2080]{2,1,0:T(8,128)(2,1)S(1)}, u32[]{:S(2)}, u32[]{:S(2)}) collective-permute-start(bf16[2,64,2080]{2,1,0:T(8,128)(2,1)} %bitcast.43), channel_id=1, source_target_pairs={{0,2},{2,4},{4,6},{6,0},{1,3},{3,5},{5,7},{7,1},{8,10},{10,12},{12... | collective-permute-start | bytes 1597448 | tf_op jit(solution)/shard_map/ppermute | solution.py:244
  99.1 23.2 %collective-permute-start.21 = (bf16[2,64,2080]{2,1,0:T(8,128)(2,1)}, bf16[2,64,2080]{2,1,0:T(8,128)(2,1)S(1)}, u32[]{:S(2)}, u32[]{:S(2)}) collective-permute-start(bf16[2,64,2080]{2,1,0:T(8,128)(2,1)} %bitcast.45), channel_id=1, source_target_pairs={{0,6},{2,0},{4,2},{6,4},{1,7},{3,1},{5,3},{7,5},{8,14},{10,8},{12,... | collective-permute-start | bytes 1597448 | tf_op jit(solution)/shard_map/ppermute | solution.py:244
  123.8 28.2 %all-to-all-start.1 = ((bf16[32,8,2080]{2,1,0:T(8,128)(2,1)}), bf16[32,8,2080]{2,1,0:T(8,128)(2,1)S(1)}, u32[]{:S(2)}, u32[]{:S(2)}) async-start(bf16[32,8,2080]{2,1,0:T(8,128)(2,1)} %bitcast.47), calls=%async_computation.1 | async-start | bytes 2228224 | tf_op jit(solution)/shard_map/all_to_all | solution.py:265
  142.2 9.8 %copy-start.20 = (s32[128]{0:T(128)S(1)}, s32[128]{0:T(128)}, u32[]{:S(2)}) copy-start(s32[128]{0:T(128)} %param.8) | copy-start | bytes 1540
  142.2 9.8 %copy-start.21 = (s32[128]{0:T(128)S(1)}, s32[128]{0:T(128)}, u32[]{:S(2)}) copy-start(s32[128]{0:T(128)} %param.9) | copy-start | bytes 1540

commit v3 on v2

--- a/solution.py
+++ b/solution.py
@@ -1,3 +1,5 @@
+import functools
+
 import jax
 import jax.numpy as jnp
 from jax import lax
@@ -85,22 +87,12 @@
     return value * normal_cdf, normal_cdf + value * density
 
 
-def forward_kernel(own, lft, rgt, far, w_ref, hidden_ref, slope_ref):
-    pre = dot(stacked((own, lft, rgt, far)), w_ref[...], 1, 0)
-    value, slope = gelu_parts(pre)
+def layer_kernel(count, *refs):
+    x, g = refs[:count], refs[count : 2 * count]
+    wi_ref, wo_ref, hidden_ref, dhidden_ref, *outs = refs[2 * count :]
+    value, slope = gelu_parts(dot(stacked(x), wi_ref[...], 1, 0))
     hidden_ref[...] = value.astype(BF)
-    slope_ref[...] = slope
-
-
-def forward(pieces, w_in, after=()):
-    units = w_in.shape[1]
-    outs = (((512, units), BF), ((512, units), F32))
-    return call(forward_kernel, outs, (*pieces, w_in), "forward", after)
-
-
-def backward_kernel(own, lft, rgt, far, slope_ref, wo_ref, wi_ref, dhidden_ref, *outs):
-    back = dot(stacked((own, lft, rgt, far)), wo_ref[...], 1, 0)
-    dhidden = (back * slope_ref[...]).astype(BF)
+    dhidden = (dot(stacked(g), wo_ref[...], 1, 0) * slope).astype(BF)
     dhidden_ref[...] = dhidden
     partial_value = dot(dhidden, wi_ref[...], 1, 1).astype(BF)
     start = 0
@@ -110,27 +102,22 @@
         start += size
 
 
-def backward(pieces, slope, w_out_t, w_in, after=()):
+def layer(x, g, w_in, w_out_t, sizes, before=()):
     width, units = w_in.shape
-    outs = (((512, units), BF),) + (((128, width), BF),) * 3 + (((64, width), BF),) * 2
-    args = (*pieces, slope, w_out_t, w_in)
-    dhidden, *partials = call(backward_kernel, outs, args, "backward", after)
-    return dhidden, partials
+    rows = 128 * len(x)
+    outs = (((rows, units), BF),) * 2 + tuple(((size, width), BF) for size in sizes)
+    kernel = functools.partial(layer_kernel, len(x))
+    hidden, dhidden, *partials = call(kernel, outs, (*x, *g, w_in, w_out_t), "layer", before)
+    return hidden, dhidden, partials
 
 
 def middle_kernel(rgt, lft, far0, far1, rgt_out, lft_out):
-    top, low = pl.ds(0, 64), pl.ds(64, 64)
-    rgt_out[top, :] = (rgt[top, :].astype(F32) + far0[...].astype(F32)).astype(BF)
-    rgt_out[low, :] = rgt[low, :]
-    lft_out[top, :] = lft[top, :]
-    lft_out[low, :] = (lft[low, :].astype(F32) + far1[...].astype(F32)).astype(BF)
-
-
-def reduce_x(partials):
-    own, lft, rgt, from_left, from_right = partials
-    outs = ((rgt.shape, BF),) * 2
-    rgt, lft = call(middle_kernel, outs, (rgt, lft, from_left, from_right), "middle")
-    return own, right(rgt), left(lft)
+    rgt_out[...] = (rgt[...].astype(F32) + far0[...].astype(F32)).astype(BF)
+    lft_out[...] = (lft[...].astype(F32) + far1[...].astype(F32)).astype(BF)
+
+
+def middle(rgt, lft, from_left, from_right, before=()):
+    return call(middle_kernel, ((rgt.shape, BF),) * 2, (rgt, lft, from_left, from_right), "middle", before)
 
 
 def nothing(*refs):
@@ -153,21 +140,25 @@
 def total_kernel(z_ref, *refs):
     out_ref = refs[-1]
     for i, start in enumerate((z_ref[0] * 128, (1 - z_ref[0]) * 128)):
-        value = sum(ref[...].astype(F32) for ref in refs[3 * i : 3 * i + 3])
-        out_ref[pl.ds(pl.multiple_of(start, 128), 128), :] = value.astype(BF)
-
-
-def total(z, near, far, later):
+        own, *halves = refs[5 * i : 5 * i + 5]
+        for half in range(2):
+            value = own[pl.ds(half * 64, 64), :].astype(F32)
+            for ref in halves[half::2]:
+                value = value + ref[...].astype(F32)
+            out_ref[pl.ds(pl.multiple_of(start + half * 64, 64), 64), :] = value.astype(BF)
+
+
+def total(z, near, far):
     width = near[0].shape[1]
     return pl.pallas_call(
         total_kernel,
         out_shape=jax.ShapeDtypeStruct((256, width), BF),
-        in_specs=[SMEM] + [VMEM] * 6 + [ANY] * len(later),
+        in_specs=[SMEM] + [VMEM] * 10,
         out_specs=VMEM,
         compiler_params=PARAMS,
         cost_estimate=pl.CostEstimate(flops=0, bytes_accessed=0, transcendentals=0),
         name="total",
-    )(z, *near, *far, *later)
+    )(z, *near, *far)
 
 
 def finish_kernel(back_ref, expert_ref, slot_ref, out_ref):
@@ -182,7 +173,8 @@
 
 
 def weights_kernel(*refs):
-    pieces, b0, b1, out, rows, b, blocks, sems, b_sems, out_sems = refs[:8], *refs[8:]
+    pieces, factors = refs[:8], refs[8:12]
+    out, rows, b, blocks, sems, b_sems, out_sems = refs[12:]
     width = out.shape[0]
     cut = 1024
     loads = []
@@ -194,7 +186,8 @@
             ]
         )
     loads[0] += [
-        pltpu.make_async_copy(half, b.at[pl.ds(i * 512, 512), :], b_sems.at[i]) for i, half in enumerate((b0, b1))
+        pltpu.make_async_copy(factor, b.at[pl.ds(start, factor.shape[0]), :], b_sems.at[i])
+        for i, (factor, start) in enumerate(zip(factors, (0, 384, 512, 896)))
     ]
     for part in loads:
         for copy in part:
@@ -215,20 +208,20 @@
         write.wait()
 
 
-def weights(pieces, b0, b1):
-    width, units = pieces[0].shape[1], b0.shape[1]
-    args = [pltpu.with_memory_space_constraint(a, pltpu.HBM) for a in (*pieces, b0, b1)]
+def weights(pieces, factors):
+    width, units = pieces[0].shape[1], factors[0].shape[1]
+    args = [pltpu.with_memory_space_constraint(a, pltpu.HBM) for a in (*pieces, *factors)]
     return pl.pallas_call(
         weights_kernel,
         out_shape=pltpu.HBM((width, units), BF),
-        in_specs=[pl.BlockSpec(memory_space=pltpu.HBM)] * 10,
+        in_specs=[pl.BlockSpec(memory_space=pltpu.HBM)] * 12,
         out_specs=pl.BlockSpec(memory_space=pltpu.HBM),
         scratch_shapes=[
             pltpu.VMEM((1024, width), BF),
             pltpu.VMEM((1024, units), BF),
             pltpu.VMEM((2, 256, units), BF),
             pltpu.SemaphoreType.DMA((16,)),
-            pltpu.SemaphoreType.DMA((2,)),
+            pltpu.SemaphoreType.DMA((4,)),
             pltpu.SemaphoreType.DMA((2,)),
         ],
         compiler_params=PARAMS,
@@ -282,22 +275,33 @@
     xz_lft = other_z(x_lft)
 
     gz_own = after(gz_own, g_lft, g_rgt)
-    gz_lft, g_far, xz_rgt = right(gz_own), left(g_rgt), other_z(x_rgt)
-    hidden, slope = forward((x_own, x_lft, x_rgt, x_far), first)
-
-    gz_lft = after(gz_lft, g_far, xz_lft)
+    gz_lft, g_far, xz_far = right(gz_own), left(g_rgt), other_z(x_far)
+    hidden_b, dhidden_b, partials = layer(
+        (x_own, x_lft, x_rgt), (g_own, g_lft, g_rgt), first, second, (128, 64, 64, 64, 64)
+    )
+
+    gz_lft = after(gz_lft, g_far)
     gz_own = after(gz_own, gz_lft)
-    gz_far, gz_rgt, xz_far = right(gz_lft), left(gz_own), other_z(x_far)
-    dhidden, (*partials, far0, far1) = backward((g_own, g_lft, g_rgt, g_far), slope, second, first)
-    arrived = right(far0), left(far1)
-    summands = reduce_x((*partials, *arrived))
-
-    hidden_z, slope_z = forward((xz_own, xz_lft, xz_rgt, xz_far), first, arrived)
-    dhidden_z, (*partials_z, far0, far1) = backward((gz_own, gz_lft, gz_rgt, gz_far), slope_z, second, first)
-    summands_z = reduce_x((*partials_z, right(far0), left(far1)))
-    grad_out_w = weights((g_own, g_lft, g_rgt, g_far, gz_own, gz_lft, gz_rgt, gz_far), hidden, hidden_z)
-    grad_in = weights((x_own, x_lft, x_rgt, x_far, xz_own, xz_lft, xz_rgt, xz_far), dhidden, dhidden_z)
-    came_back = exchange(total(z, summands, summands_z, ()), WIDE_AND_Z)
+    gz_far, gz_rgt, xz_rgt = right(gz_lft), left(gz_own), other_z(x_rgt)
+    p_own, lft0, lft1, rgt0, rgt1 = partials
+    s_lft1, s_rgt0 = right(rgt1), left(lft0)
+    hidden_a, dhidden_a, (far0, far1) = layer((x_far,), (g_far,), first, second, (64, 64), (s_lft1, s_rgt0))
+    rgt0, lft1 = middle(rgt0, lft1, right(far0), left(far1), (xz_far, xz_lft))
+    summands = p_own, right(rgt0), s_lft1, s_rgt0, left(lft1)
+
+    hidden_az, dhidden_az, (far0, far1) = layer((xz_far,), (gz_far,), first, second, (64, 64), (rgt0, gz_rgt))
+    hidden_bz, dhidden_bz, partials_z = layer(
+        (xz_own, xz_lft, xz_rgt), (gz_own, gz_lft, gz_rgt), first, second, (128, 64, 64, 64, 64), (dhidden_az,)
+    )
+    pz_own, lft0, lft1, rgt0, rgt1 = partials_z
+    s_lft1, s_rgt0 = right(rgt1), left(lft0)
+    rgt0, lft1 = middle(rgt0, lft1, right(far0), left(far1), summands[1:])
+    summands_z = pz_own, right(rgt0), s_lft1, s_rgt0, left(lft1)
+    g_all = (g_own, g_lft, g_rgt, g_far, gz_own, gz_lft, gz_rgt, gz_far)
+    x_all = (x_own, x_lft, x_rgt, x_far, xz_own, xz_lft, xz_rgt, xz_far)
+    grad_out_w = weights(g_all, (hidden_b, hidden_a, hidden_bz, hidden_az))
+    grad_in = weights(x_all, (dhidden_b, dhidden_a, dhidden_bz, dhidden_az))
+    came_back = exchange(total(z, summands, summands_z), WIDE_AND_Z)
     tokens = finish(came_back, expert, place)
     return (tokens.T, grad_in[None], grad_out_w.T[None])
 

time: 153 us -> 143 us (0.935)
  waiting for transfers between devices: 52.1 us -> 41 us
  starting transfers between devices: 34.8 us -> 38.5 us
  Pallas kernels: 40.1 us -> 37.7 us
  local copies, waits for them, and re-layouts: 3.56 us -> 2 us
    ppermute x22 -> x26, waiting for transfers between devices: 52.1 us -> 40.9 us  [move(): return lax.ppermute(blocks, axis, pairs).reshape(value.shape)]
    pallas_call x7, Pallas kernels: 17.6 us -> 15.3 us  [call(): pl.pallas_call(ordered, out_shape=tuple((jax.ShapeDtypeStruct(s, d) for s...]
    ppermute x22 -> x26, starting transfers between devices: 26.2 us -> 28.3 us  [move(): return lax.ppermute(blocks, axis, pairs).reshape(value.shape)]
    all_to_all x1, starting transfers between devices: 8.58 us -> 10.2 us  [exchange(): lax.all_to_all(blocks, axes, split_axis=0, concat_axis=0, tiled=True)]
    unnamed x52 -> x64, local copies, waits for them, and re-layouts: 3.56 us -> 2 us
  transfers between devices with their start and end apart: 23 -> 27, of which waited for: 8 -> 6; matrix products, arithmetic and copies ran while one was open for 0% -> 0% of each run, Pallas kernels for 21% -> 25%
where the time goes in v3:
time: 143 us; the launch traced here: 142 us
  waiting for transfers between devices  41 us (29%)
  starting transfers between devices  38.5 us (27%)
  Pallas kernels  37.7 us (26%)
  blocking collectives  21.9 us (15%)
  local copies, waits for them, and re-layouts  2 us (1%)
    ppermute x26, waiting for transfers between devices, move(): return lax.ppermute(blocks, axis, pairs).reshape(value.shape)  40.9 us
    ppermute x26, starting transfers between devices, move(): return lax.ppermute(blocks, axis, pairs).reshape(value.shape)  28.3 us
    all_to_all x1, blocking collectives, exchange(): lax.all_to_all(blocks, axes, split_axis=0, concat_axis=0, tiled=True)  21.9 us
    pallas_call x2, Pallas kernels, weights(): pl.pallas_call(weights_kernel, out_shape=pltpu.HBM((width, units), BF), i...  19.5 us
    pallas_call x7, Pallas kernels, call(): pl.pallas_call(ordered, out_shape=tuple((jax.ShapeDtypeStruct(s, d) for s...  15.3 us
    all_to_all x1, starting transfers between devices, exchange(): lax.all_to_all(blocks, axes, split_axis=0, concat_axis=0, tiled=True)  10.2 us
  transfers between devices with their start and end apart: 27, of which 6 were waited for; matrix products, arithmetic and copies ran while one was open for 0% of the time, Pallas kernels for 25%

profile of v3, /device:TPU:1, one launch (start us, length us, event | category | flops | bytes accessed | tf_op | source)
XLA Modules:
  0.0 142.3 jit_solution(10077221265978712615)
XLA Ops:
  0.6 2.1 %collective-permute-start = (bf16[2,64,2080]{2,1,0:T(8,128)(2,1)}, bf16[2,64,2080]{2,1,0:T(8,128)(2,1)S(1)}, u32[]{:S(2)}, u32[]{:S(2)}) collective-permute-start(bf16[2,64,2080]{2,1,0:T(8,128)(2,1)} %bitcast.121), channel_id=1, source_target_pairs={{0,2},{2,4},{4,6},{6,0},{1,3},{3,5},{5,7},{7,1},{8,10},{10,12},{12... | collective-permute-start | bytes 1597448 | tf_op jit(solution)/shard_map/ppermute | solution.py:237
  2.7 1.4 collective-permute-start.1
  4.1 1.6 %collective-permute-start.2 = (bf16[2,64,2080]{2,1,0:T(8,128)(2,1)}, bf16[2,64,2080]{2,1,0:T(8,128)(2,1)S(1)}, u32[]{:S(2)}, u32[]{:S(2)}) collective-permute-start(bf16[2,64,2080]{2,1,0:T(8,128)(2,1)} %bitcast.123), channel_id=1, source_target_pairs={{0,4},{2,6},{4,0},{6,2},{1,5},{3,7},{5,1},{7,3},{8,12},{10,14},{12... | collective-permute-start | bytes 1597448 | tf_op jit(solution)/shard_map/ppermute | solution.py:237
  5.7 1.6 %collective-permute-start.3 = (bf16[2,64,2080]{2,1,0:T(8,128)(2,1)}, bf16[2,64,2080]{2,1,0:T(8,128)(2,1)S(1)}, u32[]{:S(2)}, u32[]{:S(2)}) collective-permute-start(bf16[2,64,2080]{2,1,0:T(8,128)(2,1)} %bitcast.124), channel_id=1, source_target_pairs={{0,1},{1,0},{2,3},{3,2},{4,5},{5,4},{6,7},{7,6},{8,9},{9,8},{10,11... | collective-permute-start | bytes 1597448 | tf_op jit(solution)/shard_map/ppermute | solution.py:237
  7.4 1.5 %prepare.1 = bf16[128,2080]{1,0:T(8,128)(2,1)S(1)} custom-call(bf16[2080,128]{1,0:T(8,128)(2,1)} %bitcast.153, s32[1,128]{1,0:T(1,128)} %bitcast.140, s32[1,128]{1,0:T(1,128)} %bitcast.142, f32[1,128]{1,0:T(1,128)} %bitcast.155), custom_call_target="tpu_custom_call" | custom-call | flops 68157440 | bytes 2129920 | tf_op jit(solution)/shard_map/prepare/pallas_call | solution.py:70
  8.9 0.0 copy-start
  8.9 0.0 copy-start.1
  8.9 21.9 %all_to_all.10 = bf16[16,8,2080]{2,1,0:T(8,128)(2,1)S(1)} all-to-all(bf16[16,8,2080]{2,1,0:T(8,128)(2,1)S(1)} %bitcast.110), channel_id=1, replica_groups=mesh['y'=4,'zh'=2,'core'=2,'x'=4,'zl'=2] {'y','zh','core'}, dimensions={0} | all-to-all | bytes 1064960 | tf_op jit(solution)/shard_map/all_to_all | solution.py:258
  30.8 0.0 collective-permute-done
  30.8 0.0 collective-permute-done.1
  30.8 0.0 collective-permute-done.2
  30.9 0.0 collective-permute-done.3
  30.9 0.9 collective-permute-start.5
  31.8 0.6 collective-permute-start.4
  32.4 0.1 collective-permute-start.16
  32.6 12.2 %collective-permute-done.5 = bf16[2,64,2080]{2,1,0:T(8,128)(2,1)S(1)} collective-permute-done((bf16[2,64,2080]{2,1,0:T(8,128)(2,1)S(1)}, bf16[2,64,2080]{2,1,0:T(8,128)(2,1)S(1)}, u32[]{:S(2)}, u32[]{:S(2)}) %collective-permute-start.5) | collective-permute-done | bytes 532512 | tf_op jit(solution)/shard_map/ppermute | solution.py:237
  44.8 1.6 %collective-permute-start.6 = (bf16[2,64,2080]{2,1,0:T(8,128)(2,1)S(1)}, bf16[2,64,2080]{2,1,0:T(8,128)(2,1)S(1)}, u32[]{:S(2)}, u32[]{:S(2)}) collective-permute-start(bf16[2,64,2080]{2,1,0:T(8,128)(2,1)S(1)} %collective-permute-done.5), channel_id=1, source_target_pairs={{0,6},{2,0},{4,2},{6,4},{1,7},{3,1},{5,3},{7,5},{8,14},{10,8},{12,... | collective-permute-start | bytes 1597448 | tf_op jit(solution)/shard_map/ppermute | solution.py:237
  46.4 0.1 collective-permute-start.17
  46.5 0.1 collective-permute-start.11
  46.6 1.5 %collective-permute-start.12 = (bf16[2,64,2080]{2,1,0:T(8,128)(2,1)S(1)}, bf16[2,64,2080]{2,1,0:T(8,128)(2,1)S(1)}, u32[]{:S(2)}, u32[]{:S(2)}) collective-permute-start(bf16[2,64,2080]{2,1,0:T(8,128)(2,1)S(1)} %collective-permute-done), channel_id=1, source_target_pairs={{0,1},{1,0},{2,3},{3,2},{4,5},{5,4},{6,7},{7,6},{8,9},{9,8},{10,11... | collective-permute-start | bytes 1597448 | tf_op jit(solution)/shard_map/ppermute | solution.py:237
  48.1 4.4 %layer.4 = (bf16[384,768]{1,0:T(8,128)(2,1)S(1)}, bf16[384,768]{1,0:T(8,128)(2,1)S(1)}, bf16[128,2080]{1,0:T(8,128)(2,1)S(1)}, bf16[64,2080]{1,0:T(8,128)(2,1)S(...) custom-call(bf16[128,2080]{1,0:T(8,128)(2,1)S(1)} %bitcast.126, ...), custom_call_target="tpu_custom_call" | custom-call | tf_op jit(solution)/shard_map/layer/pallas_call | solution.py:34
  52.5 0.0 copy-start.26
  52.5 0.0 copy-start.17
  52.5 0.2 collective-permute-start.7
  52.8 4.9 %collective-permute-done.6 = bf16[2,64,2080]{2,1,0:T(8,128)(2,1)S(1)} collective-permute-done((bf16[2,64,2080]{2,1,0:T(8,128)(2,1)S(1)}, bf16[2,64,2080]{2,1,0:T(8,128)(2,1)S(1)}, u32[]{:S(2)}, u32[]{:S(2)}) %collective-permute-start.6) | collective-permute-done | bytes 532512 | tf_op jit(solution)/shard_map/ppermute | solution.py:237
  57.7 2.4 %collective-permute-start.8 = (bf16[1,64,2080]{2,1,0:T(8,128)(2,1)S(1)}, bf16[1,64,2080]{2,1,0:T(8,128)(2,1)S(1)}, u32[]{:S(2)}, u32[]{:S(2)}) collective-permute-start(bf16[1,64,2080]{2,1,0:T(8,128)(2,1)S(1)} %bitcast.147), channel_id=1, source_target_pairs={{0,6},{2,0},{4,2},{6,4},{1,7},{3,1},{5,3},{7,5},{8,14},{10,8},{12,... | collective-permute-start | bytes 798728 | tf_op jit(solution)/shard_map/ppermute | solution.py:237
  60.1 0.0 collective-permute-done.17
  60.1 0.1 collective-permute-start.18
  60.2 5.7 %collective-permute-done.7 = bf16[1,64,2080]{2,1,0:T(8,128)(2,1)S(1)} collective-permute-done((bf16[1,64,2080]{2,1,0:T(8,128)(2,1)S(1)}, bf16[1,64,2080]{2,1,0:T(8,128)(2,1)S(1)}, u32[]{:S(2)}, u32[]{:S(2)}) %collective-permute-start.7) | collective-permute-done | bytes 266272 | tf_op jit(solution)/shard_map/ppermute | solution.py:237
  65.8 0.0 collective-permute-start.19
  65.8 0.0 collective-permute-done.8
  65.9 2.1 %layer.5 = (bf16[128,768]{1,0:T(8,128)(2,1)S(1)}, bf16[128,768]{1,0:T(8,128)(2,1)S(1)}, bf16[64,2080]{1,0:T(8,128)(2,1)S(1)}, bf16[64,2080]{1,0:T(8,128)(2,1)S(1)}) custom-call(bf16[128,2080]{1,0:T(8,128)(2,1)S(1)} %bitcast.112, bf16[128,2080]{1,0:T(8,128)(2,1)S(1)} %bitcast.115, bf16[2080,768]{1,0:T(8,128)(2,1)S(1)} %bitcast.63, ...), custom_call_target="tpu_custom_call" | custom-call | tf_op jit(solution)/shard_map/layer/pallas_call | solution.py:34
  68.1 0.1 collective-permute-start.9
  68.2 2.7 %collective-permute-start.10 = (bf16[1,64,2080]{2,1,0:T(8,128)(2,1)S(1)}, bf16[1,64,2080]{2,1,0:T(8,128)(2,1)S(1)}, u32[]{:S(2)}, u32[]{:S(2)}) collective-permute-start(bf16[1,64,2080]{2,1,0:T(8,128)(2,1)S(1)} %bitcast.151), channel_id=1, source_target_pairs={{0,6},{2,0},{4,2},{6,4},{1,7},{3,1},{5,3},{7,5},{8,14},{10,8},{12,... | collective-permute-start | bytes 798728 | tf_op jit(solution)/shard_map/ppermute | solution.py:237
  70.9 0.3 collective-permute-start.15
  71.2 13.1 %collective-permute-done.9 = bf16[1,64,2080]{2,1,0:T(8,128)(2,1)S(1)} collective-permute-done((bf16[1,64,2080]{2,1,0:T(8,128)(2,1)S(1)}, bf16[1,64,2080]{2,1,0:T(8,128)(2,1)S(1)}, u32[]{:S(2)}, u32[]{:S(2)}) %collective-permute-start.9) | collective-permute-done | bytes 266272 | tf_op jit(solution)/shard_map/ppermute | solution.py:237
  84.3 0.0 collective-permute-done.10
  84.3 0.1 middle.2
  84.4 0.1 collective-permute-start.13
  84.5 2.7 %collective-permute-start.14 = (bf16[1,64,2080]{2,1,0:T(8,128)(2,1)S(1)}, bf16[1,64,2080]{2,1,0:T(8,128)(2,1)S(1)}, u32[]{:S(2)}, u32[]{:S(2)}) collective-permute-start(bf16[1,64,2080]{2,1,0:T(8,128)(2,1)S(1)} %bitcast.144), channel_id=1, source_target_pairs={{0,6},{2,0},{4,2},{6,4},{1,7},{3,1},{5,3},{7,5},{8,14},{10,8},{12,... | collective-permute-start | bytes 798728 | tf_op jit(solution)/shard_map/ppermute | solution.py:237
  87.1 0.0 collective-permute-done.18
  87.2 0.0 collective-permute-done.19
  87.2 2.2 %layer.6 = (bf16[128,768]{1,0:T(8,128)(2,1)S(1)}, bf16[128,768]{1,0:T(8,128)(2,1)S(1)}, bf16[64,2080]{1,0:T(8,128)(2,1)S(1)}, bf16[64,2080]{1,0:T(8,128)(2,1)S(1)}) custom-call(bf16[128,2080]{1,0:T(8,128)(2,1)S(1)} %bitcast.105, bf16[128,2080]{1,0:T(8,128)(2,1)S(1)} %bitcast.127, bf16[2080,768]{1,0:T(8,128)(2,1)S(1)} %bitcast.64, ...), custom_call_target="tpu_custom_call" | custom-call | tf_op jit(solution)/shard_map/layer/pallas_call | solution.py:34
  89.4 0.1 collective-permute-start.20
  89.5 2.7 %collective-permute-start.21 = (bf16[1,64,2080]{2,1,0:T(8,128)(2,1)S(1)}, bf16[1,64,2080]{2,1,0:T(8,128)(2,1)S(1)}, u32[]{:S(2)}, u32[]{:S(2)}) collective-permute-start(bf16[1,64,2080]{2,1,0:T(8,128)(2,1)S(1)} %bitcast.145), channel_id=1, source_target_pairs={{0,6},{2,0},{4,2},{6,4},{1,7},{3,1},{5,3},{7,5},{8,14},{10,8},{12,... | collective-permute-start | bytes 798728 | tf_op jit(solution)/shard_map/ppermute | solution.py:237
  92.2 0.0 copy-start.18
  92.2 5.2 %layer.7 = (bf16[384,768]{1,0:T(8,128)(2,1)S(1)}, bf16[384,768]{1,0:T(8,128)(2,1)S(1)}, bf16[128,2080]{1,0:T(8,128)(2,1)S(1)}, bf16[64,2080]{1,0:T(8,128)(2,1)},...) custom-call(bf16[128,2080]{1,0:T(8,128)(2,1)S(1)} %bitcast.93, ...), custom_call_target="tpu_custom_call" | custom-call | tf_op jit(solution)/shard_map/layer/pallas_call | solution.py:34
  97.4 0.8 copy-done.20
  98.2 0.0 collective-permute-start.23
  98.2 0.0 collective-permute-done.13
  98.2 2.7 %collective-permute-start.24 = (bf16[1,64,2080]{2,1,0:T(8,128)(2,1)}, bf16[1,64,2080]{2,1,0:T(8,128)(2,1)S(1)}, u32[]{:S(2)}, u32[]{:S(2)}) collective-permute-start(bf16[1,64,2080]{2,1,0:T(8,128)(2,1)} %bitcast.51), channel_id=1, source_target_pairs={{0,6},{2,0},{4,2},{6,4},{1,7},{3,1},{5,3},{7,5},{8,14},{10,8},{12,... | collective-permute-start | bytes 798728 | tf_op jit(solution)/shard_map/ppermute | solution.py:237
  100.9 0.1 middle.3
  101.0 0.1 collective-permute-start.22
  101.1 2.6 %collective-permute-start.25 = (bf16[1,64,2080]{2,1,0:T(8,128)(2,1)S(1)}, bf16[1,64,2080]{2,1,0:T(8,128)(2,1)S(1)}, u32[]{:S(2)}, u32[]{:S(2)}) collective-permute-start(bf16[1,64,2080]{2,1,0:T(8,128)(2,1)S(1)} %bitcast.148), channel_id=1, source_target_pairs={{0,6},{2,0},{4,2},{6,4},{1,7},{3,1},{5,3},{7,5},{8,14},{10,8},{12,... | collective-permute-start | bytes 798728 | tf_op jit(solution)/shard_map/ppermute | solution.py:237
  103.8 1.2 collective-permute-done.23
  105.0 3.8 %collective-permute-done.22 = bf16[1,64,2080]{2,1,0:T(8,128)(2,1)S(1)} collective-permute-done((bf16[1,64,2080]{2,1,0:T(8,128)(2,1)S(1)}, bf16[1,64,2080]{2,1,0:T(8,128)(2,1)S(1)}, u32[]{:S(2)}, u32[]{:S(2)}) %collective-permute-start.22) | collective-permute-done | bytes 266272 | tf_op jit(solution)/shard_map/ppermute | solution.py:237
  108.8 1.1 copy-done.21
  109.9 1.4 %total.1 = bf16[256,2080]{1,0:T(8,128)(2,1)} custom-call(s32[1]{0:T(128)} %bitcast.z_ref, bf16[128,2080]{1,0:T(8,128)(2,1)S(1)} %copy-done.18, bf16[64,2080]{1,0:T(8,128)(2,1)S(1)} %bitcast.118, bf16[64,2080]{1,0:T(8,128)(2,1)S(1)} %bitcast.82, bf16[64,2080]{1,0:T(8,128)(2,1)S(1)} %bitcast.85, bf16[64,2080]{1,0:T(8,128)(2,1)S(1)} %bitcast.120, ...), custom_call_target="tpu_custom_call" | custom-call | tf_op jit(solution)/shard_map/total/pallas_call | solution.py:153
  111.3 10.2 %all-to-all-start.1 = ((bf16[32,8,2080]{2,1,0:T(8,128)(2,1)}), bf16[32,8,2080]{2,1,0:T(8,128)(2,1)S(1)}, u32[]{:S(2)}, u32[]{:S(2)}) async-start(bf16[32,8,2080]{2,1,0:T(8,128)(2,1)} %bitcast.55), calls=%async_computation.1 | async-start | bytes 2228224 | tf_op jit(solution)/shard_map/all_to_all | solution.py:258
  121.5 9.8 %weights.2 = bf16[2080,768]{1,0:T(8,128)(2,1)} custom-call(bf16[128,2080]{1,0:T(8,128)(2,1)} %bitcast.125, bf16[128,2080]{1,0:T(8,128)(2,1)} %bitcast.88, bf16[128,2080]{1,0:T(8,128)(2,1)} %bitcast.91, bf16[128,2080]{1,0:T(8,128)(2,1)} %bitcast.113, bf16[128,2080]{1,0:T(8,128)(2,1)} %bitcast.94, bf16[128,2080]{1,0:T(8,128)(2,1)} %bitcast.109, ...), custom_call_target="tpu_custom_call" | custom-call | flops 3271557120 | bytes 10485760 | tf_op jit(solution)/shard_map/weights/pallas_call | solution.py:214
  131.3 0.0 copy-start.23
  131.3 0.0 copy-start.24
  131.3 9.8 %weights.3 = bf16[2080,768]{1,0:T(8,128)(2,1)} custom-call(bf16[128,2080]{1,0:T(8,128)(2,1)} %copy-done.2, bf16[128,2080]{1,0:T(8,128)(2,1)} %bitcast.103, bf16[128,2080]{1,0:T(8,128)(2,1)} %bitcast.100, bf16[128,2080]{1,0:T(8,128)(2,1)} %bitcast.116, bf16[128,2080]{1,0:T(8,128)(2,1)} %copy-done.4, bf16[128,2080]{1,0:T(8,128)(2,1)} %copy-done.3, ...), custom_call_target="tpu_custom_call" | custom-call | flops 3271557120 | bytes 10485760 | tf_op jit(solution)/shard_map/weights/pallas_call | solution.py:214
  141.2 1.2 finish.1
  (70 shorter events, 0.1 us)
Async XLA Ops:
  0.6 30.2 %collective-permute-start = (bf16[2,64,2080]{2,1,0:T(8,128)(2,1)}, bf16[2,64,2080]{2,1,0:T(8,128)(2,1)S(1)}, u32[]{:S(2)}, u32[]{:S(2)}) collective-permute-start(bf16[2,64,2080]{2,1,0:T(8,128)(2,1)} %bitcast.121), channel_id=1, source_target_pairs={{0,2},{2,4},{4,6},{6,0},{1,3},{3,5},{5,7},{7,1},{8,10},{10,12},{12... | collective-permute-start | bytes 1597448 | tf_op jit(solution)/shard_map/ppermute | solution.py:237
  2.7 28.1 %collective-permute-start.1 = (bf16[2,64,2080]{2,1,0:T(8,128)(2,1)}, bf16[2,64,2080]{2,1,0:T(8,128)(2,1)S(1)}, u32[]{:S(2)}, u32[]{:S(2)}) collective-permute-start(bf16[2,64,2080]{2,1,0:T(8,128)(2,1)} %bitcast.122), channel_id=1, source_target_pairs={{0,6},{2,0},{4,2},{6,4},{1,7},{3,1},{5,3},{7,5},{8,14},{10,8},{12,... | collective-permute-start | bytes 1597448 | tf_op jit(solution)/shard_map/ppermute | solution.py:237
  4.1 26.7 %collective-permute-start.2 = (bf16[2,64,2080]{2,1,0:T(8,128)(2,1)}, bf16[2,64,2080]{2,1,0:T(8,128)(2,1)S(1)}, u32[]{:S(2)}, u32[]{:S(2)}) collective-permute-start(bf16[2,64,2080]{2,1,0:T(8,128)(2,1)} %bitcast.123), channel_id=1, source_target_pairs={{0,4},{2,6},{4,0},{6,2},{1,5},{3,7},{5,1},{7,3},{8,12},{10,14},{12... | collective-permute-start | bytes 1597448 | tf_op jit(solution)/shard_map/ppermute | solution.py:237
  5.7 25.1 %collective-permute-start.3 = (bf16[2,64,2080]{2,1,0:T(8,128)(2,1)}, bf16[2,64,2080]{2,1,0:T(8,128)(2,1)S(1)}, u32[]{:S(2)}, u32[]{:S(2)}) collective-permute-start(bf16[2,64,2080]{2,1,0:T(8,128)(2,1)} %bitcast.124), channel_id=1, source_target_pairs={{0,1},{1,0},{2,3},{3,2},{4,5},{5,4},{6,7},{7,6},{8,9},{9,8},{10,11... | collective-permute-start | bytes 1597448 | tf_op jit(solution)/shard_map/ppermute | solution.py:237
  7.4 40.7 %copy-start.15 = (bf16[1,16,8,2080]{3,2,1,0:T(8,128)(2,1)S(1)}, bf16[1,16,8,2080]{3,2,1,0:T(8,128)(2,1)}, u32[]{:S(2)}) copy-start(bf16[1,16,8,2080]{3,2,1,0:T(8,128)(2,1)} %param.11) | copy-start | bytes 1597444
  8.9 39.2 %copy-start = (bf16[1,2080,768]{2,1,0:T(8,128)(2,1)S(1)}, bf16[1,2080,768]{2,1,0:T(8,128)(2,1)}, u32[]{:S(2)}) copy-start(bf16[1,2080,768]{2,1,0:T(8,128)(2,1)} %param.12) | copy-start | bytes 9584644
  8.9 39.2 %copy-start.1 = (bf16[1,768,2080]{1,2,0:T(8,128)(2,1)S(1)}, bf16[1,768,2080]{1,2,0:T(8,128)(2,1)}, u32[]{:S(2)}) copy-start(bf16[1,768,2080]{1,2,0:T(8,128)(2,1)} %param.13) | copy-start | bytes 9584644
  30.8 21.7 %copy-start.5 = (bf16[2,64,2080]{2,1,0:T(8,128)(2,1)}, bf16[2,64,2080]{2,1,0:T(8,128)(2,1)S(1)}, u32[]{:S(2)}) copy-start(bf16[2,64,2080]{2,1,0:T(8,128)(2,1)S(1)} %collective-permute-done) | copy-start | bytes 1597444
  30.8 40.1 %copy-start.6 = (bf16[2,64,2080]{2,1,0:T(8,128)(2,1)}, bf16[2,64,2080]{2,1,0:T(8,128)(2,1)S(1)}, u32[]{:S(2)}) copy-start(bf16[2,64,2080]{2,1,0:T(8,128)(2,1)S(1)} %collective-permute-done.1) | copy-start | bytes 1597444
  30.8 35.0 %copy-start.13 = (bf16[2,64,2080]{2,1,0:T(8,128)(2,1)}, bf16[2,64,2080]{2,1,0:T(8,128)(2,1)S(1)}, u32[]{:S(2)}) copy-start(bf16[2,64,2080]{2,1,0:T(8,128)(2,1)S(1)} %collective-permute-done.2) | copy-start | bytes 1597444
  30.9 61.3 %copy-start.7 = (bf16[2,64,2080]{2,1,0:T(8,128)(2,1)}, bf16[2,64,2080]{2,1,0:T(8,128)(2,1)S(1)}, u32[]{:S(2)}) copy-start(bf16[2,64,2080]{2,1,0:T(8,128)(2,1)S(1)} %collective-permute-done.3) | copy-start | bytes 1597444
  30.9 21.6 %copy-start.2 = (bf16[128,2080]{1,0:T(8,128)(2,1)}, bf16[128,2080]{1,0:T(8,128)(2,1)S(1)}, u32[]{:S(2)}) copy-start(bf16[128,2080]{1,0:T(8,128)(2,1)S(1)} %after.4.refs_3_.refs_0_) | copy-start | bytes 1597444
  30.9 13.9 %collective-permute-start.5 = (bf16[2,64,2080]{2,1,0:T(8,128)(2,1)S(1)}, bf16[2,64,2080]{2,1,0:T(8,128)(2,1)S(1)}, u32[]{:S(2)}, u32[]{:S(2)}) collective-permute-start(bf16[2,64,2080]{2,1,0:T(8,128)(2,1)S(1)} %bitcast.71), channel_id=1, source_target_pairs={{0,6},{2,0},{4,2},{6,4},{1,7},{3,1},{5,3},{7,5},{8,14},{10,8},{12,... | collective-permute-start | bytes 1597448 | tf_op jit(solution)/shard_map/ppermute | solution.py:237
  31.8 14.6 %collective-permute-start.4 = (bf16[2,64,2080]{2,1,0:T(8,128)(2,1)S(1)}, bf16[2,64,2080]{2,1,0:T(8,128)(2,1)S(1)}, u32[]{:S(2)}, u32[]{:S(2)}) collective-permute-start(bf16[2,64,2080]{2,1,0:T(8,128)(2,1)S(1)} %bitcast.72), channel_id=1, source_target_pairs={{0,2},{2,4},{4,6},{6,0},{1,3},{3,5},{5,7},{7,1},{8,10},{10,12},{12... | collective-permute-start | bytes 1597448 | tf_op jit(solution)/shard_map/ppermute | solution.py:237
  32.4 14.0 %collective-permute-start.16 = (bf16[2,64,2080]{2,1,0:T(8,128)(2,1)S(1)}, bf16[2,64,2080]{2,1,0:T(8,128)(2,1)S(1)}, u32[]{:S(2)}, u32[]{:S(2)}) collective-permute-start(bf16[2,64,2080]{2,1,0:T(8,128)(2,1)S(1)} %bitcast.73), channel_id=1, source_target_pairs={{0,1},{1,0},{2,3},{3,2},{4,5},{5,4},{6,7},{7,6},{8,9},{9,8},{10,11... | collective-permute-start | bytes 1597448 | tf_op jit(solution)/shard_map/ppermute | solution.py:237
  44.8 7.7 %copy-start.9 = (bf16[2,64,2080]{2,1,0:T(8,128)(2,1)}, bf16[2,64,2080]{2,1,0:T(8,128)(2,1)S(1)}, u32[]{:S(2)}) copy-start(bf16[2,64,2080]{2,1,0:T(8,128)(2,1)S(1)} %collective-permute-done.5) | copy-start | bytes 1597444
  44.8 12.9 %collective-permute-start.6 = (bf16[2,64,2080]{2,1,0:T(8,128)(2,1)S(1)}, bf16[2,64,2080]{2,1,0:T(8,128)(2,1)S(1)}, u32[]{:S(2)}, u32[]{:S(2)}) collective-permute-start(bf16[2,64,2080]{2,1,0:T(8,128)(2,1)S(1)} %collective-permute-done.5), channel_id=1, source_target_pairs={{0,6},{2,0},{4,2},{6,4},{1,7},{3,1},{5,3},{7,5},{8,14},{10,8},{12,... | collective-permute-start | bytes 1597448 | tf_op jit(solution)/shard_map/ppermute | solution.py:237
  46.4 6.1 %copy-start.10 = (bf16[2,64,2080]{2,1,0:T(8,128)(2,1)}, bf16[2,64,2080]{2,1,0:T(8,128)(2,1)S(1)}, u32[]{:S(2)}) copy-start(bf16[2,64,2080]{2,1,0:T(8,128)(2,1)S(1)} %collective-permute-done.4) | copy-start | bytes 1597444
  46.4 13.6 %collective-permute-start.17 = (bf16[2,64,2080]{2,1,0:T(8,128)(2,1)S(1)}, bf16[2,64,2080]{2,1,0:T(8,128)(2,1)S(1)}, u32[]{:S(2)}, u32[]{:S(2)}) collective-permute-start(bf16[2,64,2080]{2,1,0:T(8,128)(2,1)S(1)} %bitcast.77), channel_id=1, source_target_pairs={{0,2},{2,4},{4,6},{6,0},{1,3},{3,5},{5,7},{7,1},{8,10},{10,12},{12... | collective-permute-start | bytes 1597448 | tf_op jit(solution)/shard_map/ppermute | solution.py:237
  46.5 21.6 %collective-permute-start.11 = (bf16[2,64,2080]{2,1,0:T(8,128)(2,1)S(1)}, bf16[2,64,2080]{2,1,0:T(8,128)(2,1)S(1)}, u32[]{:S(2)}, u32[]{:S(2)}) collective-permute-start(bf16[2,64,2080]{2,1,0:T(8,128)(2,1)S(1)} %collective-permute-done.2), channel_id=1, source_target_pairs={{0,1},{1,0},{2,3},{3,2},{4,5},{5,4},{6,7},{7,6},{8,9},{9,8},{10,11... | collective-permute-start | bytes 1597448 | tf_op jit(solution)/shard_map/ppermute | solution.py:237
  46.6 24.3 %collective-permute-start.12 = (bf16[2,64,2080]{2,1,0:T(8,128)(2,1)S(1)}, bf16[2,64,2080]{2,1,0:T(8,128)(2,1)S(1)}, u32[]{:S(2)}, u32[]{:S(2)}) collective-permute-start(bf16[2,64,2080]{2,1,0:T(8,128)(2,1)S(1)} %collective-permute-done), channel_id=1, source_target_pairs={{0,1},{1,0},{2,3},{3,2},{4,5},{5,4},{6,7},{7,6},{8,9},{9,8},{10,11... | collective-permute-start | bytes 1597448 | tf_op jit(solution)/shard_map/ppermute | solution.py:237
  52.5 13.3 %copy-start.25 = (bf16[384,768]{1,0:T(8,128)(2,1)}, bf16[384,768]{1,0:T(8,128)(2,1)S(1)}, u32[]{:S(2)}) copy-start(bf16[384,768]{1,0:T(8,128)(2,1)S(1)} %get-tuple-element.51.refs_8_) | copy-start | bytes 1769476
  52.5 13.3 %copy-start.26 = (bf16[384,768]{1,0:T(8,128)(2,1)}, bf16[384,768]{1,0:T(8,128)(2,1)S(1)}, u32[]{:S(2)}) copy-start(bf16[384,768]{1,0:T(8,128)(2,1)S(1)} %get-tuple-element.48.refs_8_) | copy-start | bytes 1769476
  52.5 15.5 %copy-start.17 = (bf16[128,2080]{1,0:T(8,128)(2,1)}, bf16[128,2080]{1,0:T(8,128)(2,1)S(1)}, u32[]{:S(2)}) copy-start(bf16[128,2080]{1,0:T(8,128)(2,1)S(1)} %get-tuple-element.29.refs_0_) | copy-start | bytes 1597444
  52.5 13.3 %collective-permute-start.7 = (bf16[1,64,2080]{2,1,0:T(8,128)(2,1)S(1)}, bf16[1,64,2080]{2,1,0:T(8,128)(2,1)S(1)}, u32[]{:S(2)}, u32[]{:S(2)}) collective-permute-start(bf16[1,64,2080]{2,1,0:T(8,128)(2,1)S(1)} %bitcast.149), channel_id=1, source_target_pairs={{0,2},{2,4},{4,6},{6,0},{1,3},{3,5},{5,7},{7,1},{8,10},{10,12},{12... | collective-permute-start | bytes 798728 | tf_op jit(solution)/shard_map/ppermute | solution.py:237
  57.7 10.4 %copy-start.14 = (bf16[2,64,2080]{2,1,0:T(8,128)(2,1)}, bf16[2,64,2080]{2,1,0:T(8,128)(2,1)S(1)}, u32[]{:S(2)}) copy-start(bf16[2,64,2080]{2,1,0:T(8,128)(2,1)S(1)} %collective-permute-done.6) | copy-start | bytes 1597444
  57.7 8.2 %collective-permute-start.8 = (bf16[1,64,2080]{2,1,0:T(8,128)(2,1)S(1)}, bf16[1,64,2080]{2,1,0:T(8,128)(2,1)S(1)}, u32[]{:S(2)}, u32[]{:S(2)}) collective-permute-start(bf16[1,64,2080]{2,1,0:T(8,128)(2,1)S(1)} %bitcast.147), channel_id=1, source_target_pairs={{0,6},{2,0},{4,2},{6,4},{1,7},{3,1},{5,3},{7,5},{8,14},{10,8},{12,... | collective-permute-start | bytes 798728 | tf_op jit(solution)/shard_map/ppermute | solution.py:237
  60.1 32.1 %copy-start.3 = (bf16[128,2080]{1,0:T(8,128)(2,1)}, bf16[128,2080]{1,0:T(8,128)(2,1)S(1)}, u32[]{:S(2)}) copy-start(bf16[128,2080]{1,0:T(8,128)(2,1)S(1)} %after.6.refs_1_.refs_4_.refs_5_) | copy-start | bytes 1597444
  60.1 32.1 %copy-start.4 = (bf16[128,2080]{1,0:T(8,128)(2,1)}, bf16[128,2080]{1,0:T(8,128)(2,1)S(1)}, u32[]{:S(2)}) copy-start(bf16[128,2080]{1,0:T(8,128)(2,1)S(1)} %after.7.refs_3_.refs_4_) | copy-start | bytes 1597444
  60.1 27.1 %collective-permute-start.18 = (bf16[2,64,2080]{2,1,0:T(8,128)(2,1)S(1)}, bf16[2,64,2080]{2,1,0:T(8,128)(2,1)S(1)}, u32[]{:S(2)}, u32[]{:S(2)}) collective-permute-start(bf16[2,64,2080]{2,1,0:T(8,128)(2,1)S(1)} %bitcast.78), channel_id=1, source_target_pairs={{0,6},{2,0},{4,2},{6,4},{1,7},{3,1},{5,3},{7,5},{8,14},{10,8},{12,... | collective-permute-start | bytes 1597448 | tf_op jit(solution)/shard_map/ppermute | solution.py:237
  65.8 21.3 %collective-permute-start.19 = (bf16[2,64,2080]{2,1,0:T(8,128)(2,1)S(1)}, bf16[2,64,2080]{2,1,0:T(8,128)(2,1)S(1)}, u32[]{:S(2)}, u32[]{:S(2)}) collective-permute-start(bf16[2,64,2080]{2,1,0:T(8,128)(2,1)S(1)} %bitcast.75), channel_id=1, source_target_pairs={{0,2},{2,4},{4,6},{6,0},{1,3},{3,5},{5,7},{7,1},{8,10},{10,12},{12... | collective-permute-start | bytes 1597448 | tf_op jit(solution)/shard_map/ppermute | solution.py:237
  68.0 21.3 %copy-start.29 = (bf16[128,768]{1,0:T(8,128)(2,1)}, bf16[128,768]{1,0:T(8,128)(2,1)S(1)}, u32[]{:S(2)}) copy-start(bf16[128,768]{1,0:T(8,128)(2,1)S(1)} %get-tuple-element.52.refs_9_) | copy-start | bytes 589828
  68.1 21.3 %copy-start.30 = (bf16[128,768]{1,0:T(8,128)(2,1)}, bf16[128,768]{1,0:T(8,128)(2,1)S(1)}, u32[]{:S(2)}) copy-start(bf16[128,768]{1,0:T(8,128)(2,1)S(1)} %get-tuple-element.49.refs_9_) | copy-start | bytes 589828
  68.1 16.2 %collective-permute-start.9 = (bf16[1,64,2080]{2,1,0:T(8,128)(2,1)S(1)}, bf16[1,64,2080]{2,1,0:T(8,128)(2,1)S(1)}, u32[]{:S(2)}, u32[]{:S(2)}) collective-permute-start(bf16[1,64,2080]{2,1,0:T(8,128)(2,1)S(1)} %bitcast.152), channel_id=1, source_target_pairs={{0,2},{2,4},{4,6},{6,0},{1,3},{3,5},{5,7},{7,1},{8,10},{10,12},{12... | collective-permute-start | bytes 798728 | tf_op jit(solution)/shard_map/ppermute | solution.py:237
  68.2 21.2 %copy-start.11 = (bf16[2,64,2080]{2,1,0:T(8,128)(2,1)}, bf16[2,64,2080]{2,1,0:T(8,128)(2,1)S(1)}, u32[]{:S(2)}) copy-start(bf16[2,64,2080]{2,1,0:T(8,128)(2,1)S(1)} %collective-permute-done.11) | copy-start | bytes 1597444
  68.2 16.1 %collective-permute-start.10 = (bf16[1,64,2080]{2,1,0:T(8,128)(2,1)S(1)}, bf16[1,64,2080]{2,1,0:T(8,128)(2,1)S(1)}, u32[]{:S(2)}, u32[]{:S(2)}) collective-permute-start(bf16[1,64,2080]{2,1,0:T(8,128)(2,1)S(1)} %bitcast.151), channel_id=1, source_target_pairs={{0,6},{2,0},{4,2},{6,4},{1,7},{3,1},{5,3},{7,5},{8,14},{10,8},{12,... | collective-permute-start | bytes 798728 | tf_op jit(solution)/shard_map/ppermute | solution.py:237
  70.9 21.2 %copy-start.12 = (bf16[2,64,2080]{2,1,0:T(8,128)(2,1)}, bf16[2,64,2080]{2,1,0:T(8,128)(2,1)S(1)}, u32[]{:S(2)}) copy-start(bf16[2,64,2080]{2,1,0:T(8,128)(2,1)S(1)} %collective-permute-done.12) | copy-start | bytes 1597444
  70.9 21.2 %collective-permute-start.15 = (bf16[2,64,2080]{2,1,0:T(8,128)(2,1)S(1)}, bf16[2,64,2080]{2,1,0:T(8,128)(2,1)S(1)}, u32[]{:S(2)}, u32[]{:S(2)}) collective-permute-start(bf16[2,64,2080]{2,1,0:T(8,128)(2,1)S(1)} %collective-permute-done.1), channel_id=1, source_target_pairs={{0,1},{1,0},{2,3},{3,2},{4,5},{5,4},{6,7},{7,6},{8,9},{9,8},{10,11... | collective-permute-start | bytes 1597448 | tf_op jit(solution)/shard_map/ppermute | solution.py:237
  84.4 13.8 %collective-permute-start.13 = (bf16[1,64,2080]{2,1,0:T(8,128)(2,1)S(1)}, bf16[1,64,2080]{2,1,0:T(8,128)(2,1)S(1)}, u32[]{:S(2)}, u32[]{:S(2)}) collective-permute-start(bf16[1,64,2080]{2,1,0:T(8,128)(2,1)S(1)} %bitcast.133), channel_id=1, source_target_pairs={{0,2},{2,4},{4,6},{6,0},{1,3},{3,5},{5,7},{7,1},{8,10},{10,12},{12... | collective-permute-start | bytes 798728 | tf_op jit(solution)/shard_map/ppermute | solution.py:237
  84.5 16.4 %collective-permute-start.14 = (bf16[1,64,2080]{2,1,0:T(8,128)(2,1)S(1)}, bf16[1,64,2080]{2,1,0:T(8,128)(2,1)S(1)}, u32[]{:S(2)}, u32[]{:S(2)}) collective-permute-start(bf16[1,64,2080]{2,1,0:T(8,128)(2,1)S(1)} %bitcast.144), channel_id=1, source_target_pairs={{0,6},{2,0},{4,2},{6,4},{1,7},{3,1},{5,3},{7,5},{8,14},{10,8},{12,... | collective-permute-start | bytes 798728 | tf_op jit(solution)/shard_map/ppermute | solution.py:237
  87.2 5.0 %copy-start.8 = (bf16[2,64,2080]{2,1,0:T(8,128)(2,1)}, bf16[2,64,2080]{2,1,0:T(8,128)(2,1)S(1)}, u32[]{:S(2)}) copy-start(bf16[2,64,2080]{2,1,0:T(8,128)(2,1)S(1)} %collective-permute-done.18) | copy-start | bytes 1597444
  87.2 2.2 %copy-start.16 = (bf16[2,64,2080]{2,1,0:T(8,128)(2,1)}, bf16[2,64,2080]{2,1,0:T(8,128)(2,1)S(1)}, u32[]{:S(2)}) copy-start(bf16[2,64,2080]{2,1,0:T(8,128)(2,1)S(1)} %collective-permute-done.19) | copy-start | bytes 1597444
  89.4 8.0 %copy-start.22 = (bf16[128,768]{1,0:T(8,128)(2,1)}, bf16[128,768]{1,0:T(8,128)(2,1)S(1)}, u32[]{:S(2)}) copy-start(bf16[128,768]{1,0:T(8,128)(2,1)S(1)} %get-tuple-element.38.refs_8_.refs_11_) | copy-start | bytes 589828
  89.4 8.0 %copy-start.31 = (bf16[128,768]{1,0:T(8,128)(2,1)}, bf16[128,768]{1,0:T(8,128)(2,1)S(1)}, u32[]{:S(2)}) copy-start(bf16[128,768]{1,0:T(8,128)(2,1)S(1)} %get-tuple-element.54.refs_11_) | copy-start | bytes 589828
  89.4 11.5 %collective-permute-start.20 = (bf16[1,64,2080]{2,1,0:T(8,128)(2,1)S(1)}, bf16[1,64,2080]{2,1,0:T(8,128)(2,1)S(1)}, u32[]{:S(2)}, u32[]{:S(2)}) collective-permute-start(bf16[1,64,2080]{2,1,0:T(8,128)(2,1)S(1)} %bitcast.146), channel_id=1, source_target_pairs={{0,2},{2,4},{4,6},{6,0},{1,3},{3,5},{5,7},{7,1},{8,10},{10,12},{12... | collective-permute-start | bytes 798728 | tf_op jit(solution)/shard_map/ppermute | solution.py:237
  89.5 11.4 %collective-permute-start.21 = (bf16[1,64,2080]{2,1,0:T(8,128)(2,1)S(1)}, bf16[1,64,2080]{2,1,0:T(8,128)(2,1)S(1)}, u32[]{:S(2)}, u32[]{:S(2)}) collective-permute-start(bf16[1,64,2080]{2,1,0:T(8,128)(2,1)S(1)} %bitcast.145), channel_id=1, source_target_pairs={{0,6},{2,0},{4,2},{6,4},{1,7},{3,1},{5,3},{7,5},{8,14},{10,8},{12,... | collective-permute-start | bytes 798728 | tf_op jit(solution)/shard_map/ppermute | solution.py:237
  92.1 5.2 %copy-start.19 = (bf16[2,64,2080]{2,1,0:T(8,128)(2,1)}, bf16[2,64,2080]{2,1,0:T(8,128)(2,1)S(1)}, u32[]{:S(2)}) copy-start(bf16[2,64,2080]{2,1,0:T(8,128)(2,1)S(1)} %collective-permute-done.15) | copy-start | bytes 1597444
  92.2 16.6 %copy-start.18 = (bf16[128,2080]{1,0:T(8,128)(2,1)S(1)}, bf16[128,2080]{1,0:T(8,128)(2,1)}, u32[]{:S(2)}) copy-start(bf16[128,2080]{1,0:T(8,128)(2,1)} %copy-done.17) | copy-start | bytes 1597444
  97.4 0.8 copy-start.20
  98.2 2.9 %copy-start.27 = (bf16[384,768]{1,0:T(8,128)(2,1)}, bf16[384,768]{1,0:T(8,128)(2,1)S(1)}, u32[]{:S(2)}) copy-start(bf16[384,768]{1,0:T(8,128)(2,1)S(1)} %get-tuple-element.53.refs_10_) | copy-start | bytes 1769476
  98.2 2.9 %copy-start.28 = (bf16[384,768]{1,0:T(8,128)(2,1)}, bf16[384,768]{1,0:T(8,128)(2,1)S(1)}, u32[]{:S(2)}) copy-start(bf16[384,768]{1,0:T(8,128)(2,1)S(1)} %get-tuple-element.50.refs_10_) | copy-start | bytes 1769476
  98.2 6.8 %collective-permute-start.23 = (bf16[1,64,2080]{2,1,0:T(8,128)(2,1)}, bf16[1,64,2080]{2,1,0:T(8,128)(2,1)S(1)}, u32[]{:S(2)}, u32[]{:S(2)}) collective-permute-start(bf16[1,64,2080]{2,1,0:T(8,128)(2,1)} %bitcast.49), channel_id=1, source_target_pairs={{0,2},{2,4},{4,6},{6,0},{1,3},{3,5},{5,7},{7,1},{8,10},{10,12},{12... | collective-permute-start | bytes 798728 | tf_op jit(solution)/shard_map/ppermute | solution.py:237
  98.2 6.8 %collective-permute-start.24 = (bf16[1,64,2080]{2,1,0:T(8,128)(2,1)}, bf16[1,64,2080]{2,1,0:T(8,128)(2,1)S(1)}, u32[]{:S(2)}, u32[]{:S(2)}) collective-permute-start(bf16[1,64,2080]{2,1,0:T(8,128)(2,1)} %bitcast.51), channel_id=1, source_target_pairs={{0,6},{2,0},{4,2},{6,4},{1,7},{3,1},{5,3},{7,5},{8,14},{10,8},{12,... | collective-permute-start | bytes 798728 | tf_op jit(solution)/shard_map/ppermute | solution.py:237
  101.0 7.8 %collective-permute-start.22 = (bf16[1,64,2080]{2,1,0:T(8,128)(2,1)S(1)}, bf16[1,64,2080]{2,1,0:T(8,128)(2,1)S(1)}, u32[]{:S(2)}, u32[]{:S(2)}) collective-permute-start(bf16[1,64,2080]{2,1,0:T(8,128)(2,1)S(1)} %bitcast.150), channel_id=1, source_target_pairs={{0,2},{2,4},{4,6},{6,0},{1,3},{3,5},{5,7},{7,1},{8,10},{10,12},{12... | collective-permute-start | bytes 798728 | tf_op jit(solution)/shard_map/ppermute | solution.py:237
  101.1 7.7 %collective-permute-start.25 = (bf16[1,64,2080]{2,1,0:T(8,128)(2,1)S(1)}, bf16[1,64,2080]{2,1,0:T(8,128)(2,1)S(1)}, u32[]{:S(2)}, u32[]{:S(2)}) collective-permute-start(bf16[1,64,2080]{2,1,0:T(8,128)(2,1)S(1)} %bitcast.148), channel_id=1, source_target_pairs={{0,6},{2,0},{4,2},{6,4},{1,7},{3,1},{5,3},{7,5},{8,14},{10,8},{12,... | collective-permute-start | bytes 798728 | tf_op jit(solution)/shard_map/ppermute | solution.py:237
  108.8 1.1 copy-start.21
  111.3 29.8 %all-to-all-start.1 = ((bf16[32,8,2080]{2,1,0:T(8,128)(2,1)}), bf16[32,8,2080]{2,1,0:T(8,128)(2,1)S(1)}, u32[]{:S(2)}, u32[]{:S(2)}) async-start(bf16[32,8,2080]{2,1,0:T(8,128)(2,1)} %bitcast.55), calls=%async_computation.1 | async-start | bytes 2228224 | tf_op jit(solution)/shard_map/all_to_all | solution.py:258
  131.3 9.8 %copy-start.23 = (s32[128]{0:T(128)S(1)}, s32[128]{0:T(128)}, u32[]{:S(2)}) copy-start(s32[128]{0:T(128)} %param.8) | copy-start | bytes 1540
  131.3 9.8 %copy-start.24 = (s32[128]{0:T(128)S(1)}, s32[128]{0:T(128)}, u32[]{:S(2)}) copy-start(s32[128]{0:T(128)} %param.9) | copy-start | bytes 1540

commit v4 on v3

--- a/solution.py
+++ b/solution.py
@@ -20,7 +20,7 @@
 VMEM = pl.BlockSpec(memory_space=pltpu.VMEM)
 ANY = pl.BlockSpec(memory_space=pl.ANY)
 SMEM = pl.BlockSpec(memory_space=pltpu.SMEM)
-PARAMS = pltpu.CompilerParams(vmem_limit_bytes=24 * 1024 * 1024)
+PARAMS = pltpu.CompilerParams(vmem_limit_bytes=14 * 1024 * 1024)
 
 
 def dot(a, b, da, db):
@@ -286,10 +286,10 @@
     p_own, lft0, lft1, rgt0, rgt1 = partials
     s_lft1, s_rgt0 = right(rgt1), left(lft0)
     hidden_a, dhidden_a, (far0, far1) = layer((x_far,), (g_far,), first, second, (64, 64), (s_lft1, s_rgt0))
-    rgt0, lft1 = middle(rgt0, lft1, right(far0), left(far1), (xz_far, xz_lft))
+    arrived = right(far0), left(far1)
+    hidden_az, dhidden_az, (far0, far1) = layer((xz_far,), (gz_far,), first, second, (64, 64), (gz_rgt, xz_lft))
+    rgt0, lft1 = middle(rgt0, lft1, *arrived, (hidden_az,))
     summands = p_own, right(rgt0), s_lft1, s_rgt0, left(lft1)
-
-    hidden_az, dhidden_az, (far0, far1) = layer((xz_far,), (gz_far,), first, second, (64, 64), (rgt0, gz_rgt))
     hidden_bz, dhidden_bz, partials_z = layer(
         (xz_own, xz_lft, xz_rgt), (gz_own, gz_lft, gz_rgt), first, second, (128, 64, 64, 64, 64), (dhidden_az,)
     )

time: 143 us -> 140 us (0.979)
  starting transfers between devices: 38.5 us -> 36.8 us
  transfers between devices with their start and end apart: 27 -> 27, of which waited for: 6 -> 8; matrix products, arithmetic and copies ran while one was open for 0% -> 0% of each run, Pallas kernels for 25% -> 25%
where the time goes in v4:
time: 140 us
  waiting for transfers between devices  39.9 us (28%)
  Pallas kernels  37.7 us (27%)
  starting transfers between devices  36.8 us (26%)
  blocking collectives  21.9 us (16%)
  local copies, waits for them, and re-layouts  2 us (1%)
    ppermute x26, waiting for transfers between devices, move(): return lax.ppermute(blocks, axis, pairs).reshape(value.shape)  39.9 us
    ppermute x26, starting transfers between devices, move(): return lax.ppermute(blocks, axis, pairs).reshape(value.shape)  27.9 us
    all_to_all x1, blocking collectives, exchange(): lax.all_to_all(blocks, axes, split_axis=0, concat_axis=0, tiled=True)  21.9 us
    pallas_call x2, Pallas kernels, weights(): pl.pallas_call(weights_kernel, out_shape=pltpu.HBM((width, units), BF), i...  19.5 us
    pallas_call x7, Pallas kernels, call(): pl.pallas_call(ordered, out_shape=tuple((jax.ShapeDtypeStruct(s, d) for s...  15.3 us
    all_to_all x1, starting transfers between devices, exchange(): lax.all_to_all(blocks, axes, split_axis=0, concat_axis=0, tiled=True)  8.97 us
  transfers between devices with their start and end apart: 27, of which 8 were waited for; matrix products, arithmetic and copies ran while one was open for 0% of the time, Pallas kernels for 25%

profile of v4, /device:TPU:1, one launch (start us, length us, event | category | flops | bytes accessed | tf_op | source)
XLA Modules:
  0.0 139.5 jit_solution(95463277392690546)
XLA Ops:
  0.6 2.1 %collective-permute-start = (bf16[2,64,2080]{2,1,0:T(8,128)(2,1)}, bf16[2,64,2080]{2,1,0:T(8,128)(2,1)S(1)}, u32[]{:S(2)}, u32[]{:S(2)}) collective-permute-start(bf16[2,64,2080]{2,1,0:T(8,128)(2,1)} %bitcast.118), channel_id=1, source_target_pairs={{0,2},{2,4},{4,6},{6,0},{1,3},{3,5},{5,7},{7,1},{8,10},{10,12},{12... | collective-permute-start | bytes 1597448 | tf_op jit(solution)/shard_map/ppermute | solution.py:237
  2.7 1.4 collective-permute-start.1
  4.1 1.6 %collective-permute-start.2 = (bf16[2,64,2080]{2,1,0:T(8,128)(2,1)}, bf16[2,64,2080]{2,1,0:T(8,128)(2,1)S(1)}, u32[]{:S(2)}, u32[]{:S(2)}) collective-permute-start(bf16[2,64,2080]{2,1,0:T(8,128)(2,1)} %bitcast.120), channel_id=1, source_target_pairs={{0,4},{2,6},{4,0},{6,2},{1,5},{3,7},{5,1},{7,3},{8,12},{10,14},{12... | collective-permute-start | bytes 1597448 | tf_op jit(solution)/shard_map/ppermute | solution.py:237
  5.7 1.6 %collective-permute-start.3 = (bf16[2,64,2080]{2,1,0:T(8,128)(2,1)}, bf16[2,64,2080]{2,1,0:T(8,128)(2,1)S(1)}, u32[]{:S(2)}, u32[]{:S(2)}) collective-permute-start(bf16[2,64,2080]{2,1,0:T(8,128)(2,1)} %bitcast.121), channel_id=1, source_target_pairs={{0,1},{1,0},{2,3},{3,2},{4,5},{5,4},{6,7},{7,6},{8,9},{9,8},{10,11... | collective-permute-start | bytes 1597448 | tf_op jit(solution)/shard_map/ppermute | solution.py:237
  7.4 1.5 %prepare.1 = bf16[128,2080]{1,0:T(8,128)(2,1)S(1)} custom-call(bf16[2080,128]{1,0:T(8,128)(2,1)} %bitcast.152, s32[1,128]{1,0:T(1,128)} %bitcast.138, s32[1,128]{1,0:T(1,128)} %bitcast.140, f32[1,128]{1,0:T(1,128)} %bitcast.154), custom_call_target="tpu_custom_call" | custom-call | flops 68157440 | bytes 2129920 | tf_op jit(solution)/shard_map/prepare/pallas_call | solution.py:70
  8.9 0.0 copy-start
  8.9 0.0 copy-start.1
  8.9 21.9 %all_to_all.10 = bf16[16,8,2080]{2,1,0:T(8,128)(2,1)S(1)} all-to-all(bf16[16,8,2080]{2,1,0:T(8,128)(2,1)S(1)} %bitcast.107), channel_id=1, replica_groups=mesh['y'=4,'zh'=2,'core'=2,'x'=4,'zl'=2] {'y','zh','core'}, dimensions={0} | all-to-all | bytes 1064960 | tf_op jit(solution)/shard_map/all_to_all | solution.py:258
  30.8 0.0 collective-permute-done
  30.8 0.0 collective-permute-done.1
  30.9 0.0 collective-permute-done.3
  30.9 0.9 collective-permute-start.5
  31.8 0.6 collective-permute-start.4
  32.4 0.1 collective-permute-start.12
  32.6 12.2 %collective-permute-done.5 = bf16[2,64,2080]{2,1,0:T(8,128)(2,1)S(1)} collective-permute-done((bf16[2,64,2080]{2,1,0:T(8,128)(2,1)S(1)}, bf16[2,64,2080]{2,1,0:T(8,128)(2,1)S(1)}, u32[]{:S(2)}, u32[]{:S(2)}) %collective-permute-start.5) | collective-permute-done | bytes 532512 | tf_op jit(solution)/shard_map/ppermute | solution.py:237
  44.8 1.6 %collective-permute-start.6 = (bf16[2,64,2080]{2,1,0:T(8,128)(2,1)S(1)}, bf16[2,64,2080]{2,1,0:T(8,128)(2,1)S(1)}, u32[]{:S(2)}, u32[]{:S(2)}) collective-permute-start(bf16[2,64,2080]{2,1,0:T(8,128)(2,1)S(1)} %collective-permute-done.5), channel_id=1, source_target_pairs={{0,6},{2,0},{4,2},{6,4},{1,7},{3,1},{5,3},{7,5},{8,14},{10,8},{12,... | collective-permute-start | bytes 1597448 | tf_op jit(solution)/shard_map/ppermute | solution.py:237
  46.4 0.1 collective-permute-start.13
  46.5 4.4 %layer.4 = (bf16[384,768]{1,0:T(8,128)(2,1)S(1)}, bf16[384,768]{1,0:T(8,128)(2,1)S(1)}, bf16[128,2080]{1,0:T(8,128)(2,1)S(1)}, bf16[64,2080]{1,0:T(8,128)(2,1)S(...) custom-call(bf16[128,2080]{1,0:T(8,128)(2,1)S(1)} %bitcast.123, ...), custom_call_target="tpu_custom_call" | custom-call | tf_op jit(solution)/shard_map/layer/pallas_call | solution.py:34
  51.0 0.0 copy-start.17
  51.0 0.0 copy-start.27
  51.0 0.3 collective-permute-start.7
  51.3 0.0 collective-permute-start.11
  51.3 1.5 %collective-permute-start.16 = (bf16[2,64,2080]{2,1,0:T(8,128)(2,1)S(1)}, bf16[2,64,2080]{2,1,0:T(8,128)(2,1)S(1)}, u32[]{:S(2)}, u32[]{:S(2)}) collective-permute-start(bf16[2,64,2080]{2,1,0:T(8,128)(2,1)S(1)} %collective-permute-done), channel_id=1, source_target_pairs={{0,1},{1,0},{2,3},{3,2},{4,5},{5,4},{6,7},{7,6},{8,9},{9,8},{10,11... | collective-permute-start | bytes 1597448 | tf_op jit(solution)/shard_map/ppermute | solution.py:237
  52.7 4.9 %collective-permute-done.6 = bf16[2,64,2080]{2,1,0:T(8,128)(2,1)S(1)} collective-permute-done((bf16[2,64,2080]{2,1,0:T(8,128)(2,1)S(1)}, bf16[2,64,2080]{2,1,0:T(8,128)(2,1)S(1)}, u32[]{:S(2)}, u32[]{:S(2)}) %collective-permute-start.6) | collective-permute-done | bytes 532512 | tf_op jit(solution)/shard_map/ppermute | solution.py:237
  57.7 2.4 %collective-permute-start.8 = (bf16[1,64,2080]{2,1,0:T(8,128)(2,1)S(1)}, bf16[1,64,2080]{2,1,0:T(8,128)(2,1)S(1)}, u32[]{:S(2)}, u32[]{:S(2)}) collective-permute-start(bf16[1,64,2080]{2,1,0:T(8,128)(2,1)S(1)} %bitcast.145), channel_id=1, source_target_pairs={{0,6},{2,0},{4,2},{6,4},{1,7},{3,1},{5,3},{7,5},{8,14},{10,8},{12,... | collective-permute-start | bytes 798728 | tf_op jit(solution)/shard_map/ppermute | solution.py:237
  60.1 0.0 collective-permute-done.13
  60.1 0.1 collective-permute-start.14
  60.2 5.7 %collective-permute-done.7 = bf16[1,64,2080]{2,1,0:T(8,128)(2,1)S(1)} collective-permute-done((bf16[1,64,2080]{2,1,0:T(8,128)(2,1)S(1)}, bf16[1,64,2080]{2,1,0:T(8,128)(2,1)S(1)}, u32[]{:S(2)}, u32[]{:S(2)}) %collective-permute-start.7) | collective-permute-done | bytes 266272 | tf_op jit(solution)/shard_map/ppermute | solution.py:237
  65.8 0.0 collective-permute-start.15
  65.8 0.0 collective-permute-done.8
  65.8 2.1 %layer.5 = (bf16[128,768]{1,0:T(8,128)(2,1)S(1)}, bf16[128,768]{1,0:T(8,128)(2,1)S(1)}, bf16[64,2080]{1,0:T(8,128)(2,1)S(1)}, bf16[64,2080]{1,0:T(8,128)(2,1)S(1)}) custom-call(bf16[128,2080]{1,0:T(8,128)(2,1)S(1)} %bitcast.109, bf16[128,2080]{1,0:T(8,128)(2,1)S(1)} %bitcast.112, bf16[2080,768]{1,0:T(8,128)(2,1)S(1)} %bitcast.63, ...), custom_call_target="tpu_custom_call" | custom-call | tf_op jit(solution)/shard_map/layer/pallas_call | solution.py:34
  68.1 1.5 %collective-permute-start.9 = (bf16[1,64,2080]{2,1,0:T(8,128)(2,1)S(1)}, bf16[1,64,2080]{2,1,0:T(8,128)(2,1)S(1)}, u32[]{:S(2)}, u32[]{:S(2)}) collective-permute-start(bf16[1,64,2080]{2,1,0:T(8,128)(2,1)S(1)} %bitcast.149), channel_id=1, source_target_pairs={{0,2},{2,4},{4,6},{6,0},{1,3},{3,5},{5,7},{7,1},{8,10},{10,12},{12... | collective-permute-start | bytes 798728 | tf_op jit(solution)/shard_map/ppermute | solution.py:237
  69.6 0.0 collective-permute-done.11
  69.6 1.2 collective-permute-start.10
  70.8 4.1 %collective-permute-done.16 = bf16[2,64,2080]{2,1,0:T(8,128)(2,1)S(1)} collective-permute-done((bf16[2,64,2080]{2,1,0:T(8,128)(2,1)S(1)}, bf16[2,64,2080]{2,1,0:T(8,128)(2,1)S(1)}, u32[]{:S(2)}, u32[]{:S(2)}) %collective-permute-start.16) | collective-permute-done | bytes 532512 | tf_op jit(solution)/shard_map/ppermute | solution.py:237
  74.9 0.0 collective-permute-start.19
  74.9 2.9 %collective-permute-done.14 = bf16[2,64,2080]{2,1,0:T(8,128)(2,1)S(1)} collective-permute-done((bf16[2,64,2080]{2,1,0:T(8,128)(2,1)S(1)}, bf16[2,64,2080]{2,1,0:T(8,128)(2,1)S(1)}, u32[]{:S(2)}, u32[]{:S(2)}) %collective-permute-start.14) | collective-permute-done | bytes 532512 | tf_op jit(solution)/shard_map/ppermute | solution.py:237
  77.8 0.0 collective-permute-done.15
  77.8 2.1 %layer.6 = (bf16[128,768]{1,0:T(8,128)(2,1)S(1)}, bf16[128,768]{1,0:T(8,128)(2,1)S(1)}, bf16[64,2080]{1,0:T(8,128)(2,1)S(1)}, bf16[64,2080]{1,0:T(8,128)(2,1)S(1)}) custom-call(bf16[128,2080]{1,0:T(8,128)(2,1)S(1)} %bitcast.124, bf16[128,2080]{1,0:T(8,128)(2,1)S(1)} %bitcast.126, bf16[2080,768]{1,0:T(8,128)(2,1)S(1)} %bitcast.64, ...), custom_call_target="tpu_custom_call" | custom-call | tf_op jit(solution)/shard_map/layer/pallas_call | solution.py:34
  80.0 3.7 %collective-permute-done.9 = bf16[1,64,2080]{2,1,0:T(8,128)(2,1)S(1)} collective-permute-done((bf16[1,64,2080]{2,1,0:T(8,128)(2,1)S(1)}, bf16[1,64,2080]{2,1,0:T(8,128)(2,1)S(1)}, u32[]{:S(2)}, u32[]{:S(2)}) %collective-permute-start.9) | collective-permute-done | bytes 266272 | tf_op jit(solution)/shard_map/ppermute | solution.py:237
  83.7 0.0 collective-permute-done.10
  83.7 0.1 middle.2
  83.9 0.1 collective-permute-start.17
  84.0 2.7 %collective-permute-start.18 = (bf16[1,64,2080]{2,1,0:T(8,128)(2,1)S(1)}, bf16[1,64,2080]{2,1,0:T(8,128)(2,1)S(1)}, u32[]{:S(2)}, u32[]{:S(2)}) collective-permute-start(bf16[1,64,2080]{2,1,0:T(8,128)(2,1)S(1)} %bitcast.144), channel_id=1, source_target_pairs={{0,6},{2,0},{4,2},{6,4},{1,7},{3,1},{5,3},{7,5},{8,14},{10,8},{12,... | collective-permute-start | bytes 798728 | tf_op jit(solution)/shard_map/ppermute | solution.py:237
  86.6 0.0 collective-permute-start.20
  86.6 2.7 %collective-permute-start.21 = (bf16[1,64,2080]{2,1,0:T(8,128)(2,1)S(1)}, bf16[1,64,2080]{2,1,0:T(8,128)(2,1)S(1)}, u32[]{:S(2)}, u32[]{:S(2)}) collective-permute-start(bf16[1,64,2080]{2,1,0:T(8,128)(2,1)S(1)} %bitcast.142), channel_id=1, source_target_pairs={{0,6},{2,0},{4,2},{6,4},{1,7},{3,1},{5,3},{7,5},{8,14},{10,8},{12,... | collective-permute-start | bytes 798728 | tf_op jit(solution)/shard_map/ppermute | solution.py:237
  89.3 0.0 collective-permute-done.19
  89.3 0.0 copy-start.18
  89.4 5.2 %layer.7 = (bf16[384,768]{1,0:T(8,128)(2,1)S(1)}, bf16[384,768]{1,0:T(8,128)(2,1)S(1)}, bf16[128,2080]{1,0:T(8,128)(2,1)S(1)}, bf16[64,2080]{1,0:T(8,128)(2,1)},...) custom-call(bf16[128,2080]{1,0:T(8,128)(2,1)S(1)} %bitcast.93, ...), custom_call_target="tpu_custom_call" | custom-call | tf_op jit(solution)/shard_map/layer/pallas_call | solution.py:34
  94.6 0.8 copy-done.20
  95.4 2.7 %collective-permute-start.24 = (bf16[1,64,2080]{2,1,0:T(8,128)(2,1)}, bf16[1,64,2080]{2,1,0:T(8,128)(2,1)S(1)}, u32[]{:S(2)}, u32[]{:S(2)}) collective-permute-start(bf16[1,64,2080]{2,1,0:T(8,128)(2,1)} %bitcast.51), channel_id=1, source_target_pairs={{0,6},{2,0},{4,2},{6,4},{1,7},{3,1},{5,3},{7,5},{8,14},{10,8},{12,... | collective-permute-start | bytes 798728 | tf_op jit(solution)/shard_map/ppermute | solution.py:237
  98.1 0.1 middle.3
  98.2 0.1 collective-permute-start.22
  98.3 2.6 %collective-permute-start.25 = (bf16[1,64,2080]{2,1,0:T(8,128)(2,1)S(1)}, bf16[1,64,2080]{2,1,0:T(8,128)(2,1)S(1)}, u32[]{:S(2)}, u32[]{:S(2)}) collective-permute-start(bf16[1,64,2080]{2,1,0:T(8,128)(2,1)S(1)} %bitcast.150), channel_id=1, source_target_pairs={{0,6},{2,0},{4,2},{6,4},{1,7},{3,1},{5,3},{7,5},{8,14},{10,8},{12,... | collective-permute-start | bytes 798728 | tf_op jit(solution)/shard_map/ppermute | solution.py:237
  101.0 1.5 %collective-permute-done.23 = bf16[1,64,2080]{2,1,0:T(8,128)(2,1)S(1)} collective-permute-done((bf16[1,64,2080]{2,1,0:T(8,128)(2,1)}, bf16[1,64,2080]{2,1,0:T(8,128)(2,1)S(1)}, u32[]{:S(2)}, u32[]{:S(2)}) %collective-permute-start.23) | collective-permute-done | bytes 266272 | tf_op jit(solution)/shard_map/ppermute | solution.py:237
  102.5 4.8 %collective-permute-done.22 = bf16[1,64,2080]{2,1,0:T(8,128)(2,1)S(1)} collective-permute-done((bf16[1,64,2080]{2,1,0:T(8,128)(2,1)S(1)}, bf16[1,64,2080]{2,1,0:T(8,128)(2,1)S(1)}, u32[]{:S(2)}, u32[]{:S(2)}) %collective-permute-start.22) | collective-permute-done | bytes 266272 | tf_op jit(solution)/shard_map/ppermute | solution.py:237
  107.3 1.1 copy-done.21
  108.4 1.4 %total.1 = bf16[256,2080]{1,0:T(8,128)(2,1)} custom-call(s32[1]{0:T(128)} %bitcast.z_ref, bf16[128,2080]{1,0:T(8,128)(2,1)S(1)} %copy-done.18, bf16[64,2080]{1,0:T(8,128)(2,1)S(1)} %bitcast.115, bf16[64,2080]{1,0:T(8,128)(2,1)S(1)} %bitcast.82, bf16[64,2080]{1,0:T(8,128)(2,1)S(1)} %bitcast.85, bf16[64,2080]{1,0:T(8,128)(2,1)S(1)} %bitcast.117, ...), custom_call_target="tpu_custom_call" | custom-call | tf_op jit(solution)/shard_map/total/pallas_call | solution.py:153
  109.8 9.0 %all-to-all-start.1 = ((bf16[32,8,2080]{2,1,0:T(8,128)(2,1)}), bf16[32,8,2080]{2,1,0:T(8,128)(2,1)S(1)}, u32[]{:S(2)}, u32[]{:S(2)}) async-start(bf16[32,8,2080]{2,1,0:T(8,128)(2,1)} %bitcast.55), calls=%async_computation.1 | async-start | bytes 2228224 | tf_op jit(solution)/shard_map/all_to_all | solution.py:258
  118.8 9.8 %weights.2 = bf16[2080,768]{1,0:T(8,128)(2,1)} custom-call(bf16[128,2080]{1,0:T(8,128)(2,1)} %bitcast.122, bf16[128,2080]{1,0:T(8,128)(2,1)} %bitcast.88, bf16[128,2080]{1,0:T(8,128)(2,1)} %bitcast.91, bf16[128,2080]{1,0:T(8,128)(2,1)} %bitcast.110, bf16[128,2080]{1,0:T(8,128)(2,1)} %bitcast.94, bf16[128,2080]{1,0:T(8,128)(2,1)} %bitcast.97, ...), custom_call_target="tpu_custom_call" | custom-call | flops 3271557120 | bytes 10485760 | tf_op jit(solution)/shard_map/weights/pallas_call | solution.py:214
  128.6 0.0 copy-start.24
  128.6 0.0 copy-start.25
  128.6 9.8 %weights.3 = bf16[2080,768]{1,0:T(8,128)(2,1)} custom-call(bf16[128,2080]{1,0:T(8,128)(2,1)} %copy-done.2, bf16[128,2080]{1,0:T(8,128)(2,1)} %bitcast.106, bf16[128,2080]{1,0:T(8,128)(2,1)} %bitcast.103, bf16[128,2080]{1,0:T(8,128)(2,1)} %bitcast.113, bf16[128,2080]{1,0:T(8,128)(2,1)} %copy-done.4, bf16[128,2080]{1,0:T(8,128)(2,1)} %copy-done.3, ...), custom_call_target="tpu_custom_call" | custom-call | flops 3271557120 | bytes 10485760 | tf_op jit(solution)/shard_map/weights/pallas_call | solution.py:214
  138.4 1.1 finish.1
  (70 shorter events, 0.1 us)
Async XLA Ops:
  0.6 30.2 %collective-permute-start = (bf16[2,64,2080]{2,1,0:T(8,128)(2,1)}, bf16[2,64,2080]{2,1,0:T(8,128)(2,1)S(1)}, u32[]{:S(2)}, u32[]{:S(2)}) collective-permute-start(bf16[2,64,2080]{2,1,0:T(8,128)(2,1)} %bitcast.118), channel_id=1, source_target_pairs={{0,2},{2,4},{4,6},{6,0},{1,3},{3,5},{5,7},{7,1},{8,10},{10,12},{12... | collective-permute-start | bytes 1597448 | tf_op jit(solution)/shard_map/ppermute | solution.py:237
  2.7 28.1 %collective-permute-start.1 = (bf16[2,64,2080]{2,1,0:T(8,128)(2,1)}, bf16[2,64,2080]{2,1,0:T(8,128)(2,1)S(1)}, u32[]{:S(2)}, u32[]{:S(2)}) collective-permute-start(bf16[2,64,2080]{2,1,0:T(8,128)(2,1)} %bitcast.119), channel_id=1, source_target_pairs={{0,6},{2,0},{4,2},{6,4},{1,7},{3,1},{5,3},{7,5},{8,14},{10,8},{12,... | collective-permute-start | bytes 1597448 | tf_op jit(solution)/shard_map/ppermute | solution.py:237
  4.1 26.7 %collective-permute-start.2 = (bf16[2,64,2080]{2,1,0:T(8,128)(2,1)}, bf16[2,64,2080]{2,1,0:T(8,128)(2,1)S(1)}, u32[]{:S(2)}, u32[]{:S(2)}) collective-permute-start(bf16[2,64,2080]{2,1,0:T(8,128)(2,1)} %bitcast.120), channel_id=1, source_target_pairs={{0,4},{2,6},{4,0},{6,2},{1,5},{3,7},{5,1},{7,3},{8,12},{10,14},{12... | collective-permute-start | bytes 1597448 | tf_op jit(solution)/shard_map/ppermute | solution.py:237
  5.7 25.1 %collective-permute-start.3 = (bf16[2,64,2080]{2,1,0:T(8,128)(2,1)}, bf16[2,64,2080]{2,1,0:T(8,128)(2,1)S(1)}, u32[]{:S(2)}, u32[]{:S(2)}) collective-permute-start(bf16[2,64,2080]{2,1,0:T(8,128)(2,1)} %bitcast.121), channel_id=1, source_target_pairs={{0,1},{1,0},{2,3},{3,2},{4,5},{5,4},{6,7},{7,6},{8,9},{9,8},{10,11... | collective-permute-start | bytes 1597448 | tf_op jit(solution)/shard_map/ppermute | solution.py:237
  7.4 39.1 %copy-start.14 = (bf16[1,16,8,2080]{3,2,1,0:T(8,128)(2,1)S(1)}, bf16[1,16,8,2080]{3,2,1,0:T(8,128)(2,1)}, u32[]{:S(2)}) copy-start(bf16[1,16,8,2080]{3,2,1,0:T(8,128)(2,1)} %param.11) | copy-start | bytes 1597444
  8.9 37.7 %copy-start = (bf16[1,2080,768]{2,1,0:T(8,128)(2,1)S(1)}, bf16[1,2080,768]{2,1,0:T(8,128)(2,1)}, u32[]{:S(2)}) copy-start(bf16[1,2080,768]{2,1,0:T(8,128)(2,1)} %param.12) | copy-start | bytes 9584644
  8.9 37.7 %copy-start.1 = (bf16[1,768,2080]{1,2,0:T(8,128)(2,1)S(1)}, bf16[1,768,2080]{1,2,0:T(8,128)(2,1)}, u32[]{:S(2)}) copy-start(bf16[1,768,2080]{1,2,0:T(8,128)(2,1)} %param.13) | copy-start | bytes 9584644
  30.8 20.5 %copy-start.5 = (bf16[2,64,2080]{2,1,0:T(8,128)(2,1)}, bf16[2,64,2080]{2,1,0:T(8,128)(2,1)S(1)}, u32[]{:S(2)}) copy-start(bf16[2,64,2080]{2,1,0:T(8,128)(2,1)S(1)} %collective-permute-done) | copy-start | bytes 1597444
  30.8 44.1 %copy-start.6 = (bf16[2,64,2080]{2,1,0:T(8,128)(2,1)}, bf16[2,64,2080]{2,1,0:T(8,128)(2,1)S(1)}, u32[]{:S(2)}) copy-start(bf16[2,64,2080]{2,1,0:T(8,128)(2,1)S(1)} %collective-permute-done.1) | copy-start | bytes 1597444
  30.8 35.0 %copy-start.12 = (bf16[2,64,2080]{2,1,0:T(8,128)(2,1)}, bf16[2,64,2080]{2,1,0:T(8,128)(2,1)S(1)}, u32[]{:S(2)}) copy-start(bf16[2,64,2080]{2,1,0:T(8,128)(2,1)S(1)} %collective-permute-done.2) | copy-start | bytes 1597444
  30.9 58.5 %copy-start.7 = (bf16[2,64,2080]{2,1,0:T(8,128)(2,1)}, bf16[2,64,2080]{2,1,0:T(8,128)(2,1)S(1)}, u32[]{:S(2)}) copy-start(bf16[2,64,2080]{2,1,0:T(8,128)(2,1)S(1)} %collective-permute-done.3) | copy-start | bytes 1597444
  30.9 20.1 %copy-start.2 = (bf16[128,2080]{1,0:T(8,128)(2,1)}, bf16[128,2080]{1,0:T(8,128)(2,1)S(1)}, u32[]{:S(2)}) copy-start(bf16[128,2080]{1,0:T(8,128)(2,1)S(1)} %after.4.refs_3_.refs_0_) | copy-start | bytes 1597444
  30.9 13.9 %collective-permute-start.5 = (bf16[2,64,2080]{2,1,0:T(8,128)(2,1)S(1)}, bf16[2,64,2080]{2,1,0:T(8,128)(2,1)S(1)}, u32[]{:S(2)}, u32[]{:S(2)}) collective-permute-start(bf16[2,64,2080]{2,1,0:T(8,128)(2,1)S(1)} %bitcast.71), channel_id=1, source_target_pairs={{0,6},{2,0},{4,2},{6,4},{1,7},{3,1},{5,3},{7,5},{8,14},{10,8},{12,... | collective-permute-start | bytes 1597448 | tf_op jit(solution)/shard_map/ppermute | solution.py:237
  31.8 14.6 %collective-permute-start.4 = (bf16[2,64,2080]{2,1,0:T(8,128)(2,1)S(1)}, bf16[2,64,2080]{2,1,0:T(8,128)(2,1)S(1)}, u32[]{:S(2)}, u32[]{:S(2)}) collective-permute-start(bf16[2,64,2080]{2,1,0:T(8,128)(2,1)S(1)} %bitcast.72), channel_id=1, source_target_pairs={{0,2},{2,4},{4,6},{6,0},{1,3},{3,5},{5,7},{7,1},{8,10},{10,12},{12... | collective-permute-start | bytes 1597448 | tf_op jit(solution)/shard_map/ppermute | solution.py:237
  32.4 14.0 %collective-permute-start.12 = (bf16[2,64,2080]{2,1,0:T(8,128)(2,1)S(1)}, bf16[2,64,2080]{2,1,0:T(8,128)(2,1)S(1)}, u32[]{:S(2)}, u32[]{:S(2)}) collective-permute-start(bf16[2,64,2080]{2,1,0:T(8,128)(2,1)S(1)} %bitcast.73), channel_id=1, source_target_pairs={{0,1},{1,0},{2,3},{3,2},{4,5},{5,4},{6,7},{7,6},{8,9},{9,8},{10,11... | collective-permute-start | bytes 1597448 | tf_op jit(solution)/shard_map/ppermute | solution.py:237
  44.8 6.2 %copy-start.10 = (bf16[2,64,2080]{2,1,0:T(8,128)(2,1)}, bf16[2,64,2080]{2,1,0:T(8,128)(2,1)S(1)}, u32[]{:S(2)}) copy-start(bf16[2,64,2080]{2,1,0:T(8,128)(2,1)S(1)} %collective-permute-done.5) | copy-start | bytes 1597444
  44.8 12.9 %collective-permute-start.6 = (bf16[2,64,2080]{2,1,0:T(8,128)(2,1)S(1)}, bf16[2,64,2080]{2,1,0:T(8,128)(2,1)S(1)}, u32[]{:S(2)}, u32[]{:S(2)}) collective-permute-start(bf16[2,64,2080]{2,1,0:T(8,128)(2,1)S(1)} %collective-permute-done.5), channel_id=1, source_target_pairs={{0,6},{2,0},{4,2},{6,4},{1,7},{3,1},{5,3},{7,5},{8,14},{10,8},{12,... | collective-permute-start | bytes 1597448 | tf_op jit(solution)/shard_map/ppermute | solution.py:237
  46.4 4.6 %copy-start.11 = (bf16[2,64,2080]{2,1,0:T(8,128)(2,1)}, bf16[2,64,2080]{2,1,0:T(8,128)(2,1)S(1)}, u32[]{:S(2)}) copy-start(bf16[2,64,2080]{2,1,0:T(8,128)(2,1)S(1)} %collective-permute-done.4) | copy-start | bytes 1597444
  46.4 13.6 %collective-permute-start.13 = (bf16[2,64,2080]{2,1,0:T(8,128)(2,1)S(1)}, bf16[2,64,2080]{2,1,0:T(8,128)(2,1)S(1)}, u32[]{:S(2)}, u32[]{:S(2)}) collective-permute-start(bf16[2,64,2080]{2,1,0:T(8,128)(2,1)S(1)} %bitcast.77), channel_id=1, source_target_pairs={{0,2},{2,4},{4,6},{6,0},{1,3},{3,5},{5,7},{7,1},{8,10},{10,12},{12... | collective-permute-start | bytes 1597448 | tf_op jit(solution)/shard_map/ppermute | solution.py:237
  51.0 17.0 %copy-start.17 = (bf16[128,2080]{1,0:T(8,128)(2,1)}, bf16[128,2080]{1,0:T(8,128)(2,1)S(1)}, u32[]{:S(2)}) copy-start(bf16[128,2080]{1,0:T(8,128)(2,1)S(1)} %get-tuple-element.29.refs_0_) | copy-start | bytes 1597444
  51.0 17.0 %copy-start.26 = (bf16[384,768]{1,0:T(8,128)(2,1)}, bf16[384,768]{1,0:T(8,128)(2,1)S(1)}, u32[]{:S(2)}) copy-start(bf16[384,768]{1,0:T(8,128)(2,1)S(1)} %get-tuple-element.52.refs_8_) | copy-start | bytes 1769476
  51.0 17.0 %copy-start.27 = (bf16[384,768]{1,0:T(8,128)(2,1)}, bf16[384,768]{1,0:T(8,128)(2,1)S(1)}, u32[]{:S(2)}) copy-start(bf16[384,768]{1,0:T(8,128)(2,1)S(1)} %get-tuple-element.49.refs_8_) | copy-start | bytes 1769476
  51.0 14.8 %collective-permute-start.7 = (bf16[1,64,2080]{2,1,0:T(8,128)(2,1)S(1)}, bf16[1,64,2080]{2,1,0:T(8,128)(2,1)S(1)}, u32[]{:S(2)}, u32[]{:S(2)}) collective-permute-start(bf16[1,64,2080]{2,1,0:T(8,128)(2,1)S(1)} %bitcast.147), channel_id=1, source_target_pairs={{0,2},{2,4},{4,6},{6,0},{1,3},{3,5},{5,7},{7,1},{8,10},{10,12},{12... | collective-permute-start | bytes 798728 | tf_op jit(solution)/shard_map/ppermute | solution.py:237
  51.3 18.3 %collective-permute-start.11 = (bf16[2,64,2080]{2,1,0:T(8,128)(2,1)S(1)}, bf16[2,64,2080]{2,1,0:T(8,128)(2,1)S(1)}, u32[]{:S(2)}, u32[]{:S(2)}) collective-permute-start(bf16[2,64,2080]{2,1,0:T(8,128)(2,1)S(1)} %collective-permute-done.2), channel_id=1, source_target_pairs={{0,1},{1,0},{2,3},{3,2},{4,5},{5,4},{6,7},{7,6},{8,9},{9,8},{10,11... | collective-permute-start | bytes 1597448 | tf_op jit(solution)/shard_map/ppermute | solution.py:237
  51.3 23.6 %collective-permute-start.16 = (bf16[2,64,2080]{2,1,0:T(8,128)(2,1)S(1)}, bf16[2,64,2080]{2,1,0:T(8,128)(2,1)S(1)}, u32[]{:S(2)}, u32[]{:S(2)}) collective-permute-start(bf16[2,64,2080]{2,1,0:T(8,128)(2,1)S(1)} %collective-permute-done), channel_id=1, source_target_pairs={{0,1},{1,0},{2,3},{3,2},{4,5},{5,4},{6,7},{7,6},{8,9},{9,8},{10,11... | collective-permute-start | bytes 1597448 | tf_op jit(solution)/shard_map/ppermute | solution.py:237
  57.7 10.4 %copy-start.13 = (bf16[2,64,2080]{2,1,0:T(8,128)(2,1)}, bf16[2,64,2080]{2,1,0:T(8,128)(2,1)S(1)}, u32[]{:S(2)}) copy-start(bf16[2,64,2080]{2,1,0:T(8,128)(2,1)S(1)} %collective-permute-done.6) | copy-start | bytes 1597444
  57.7 8.2 %collective-permute-start.8 = (bf16[1,64,2080]{2,1,0:T(8,128)(2,1)S(1)}, bf16[1,64,2080]{2,1,0:T(8,128)(2,1)S(1)}, u32[]{:S(2)}, u32[]{:S(2)}) collective-permute-start(bf16[1,64,2080]{2,1,0:T(8,128)(2,1)S(1)} %bitcast.145), channel_id=1, source_target_pairs={{0,6},{2,0},{4,2},{6,4},{1,7},{3,1},{5,3},{7,5},{8,14},{10,8},{12,... | collective-permute-start | bytes 798728 | tf_op jit(solution)/shard_map/ppermute | solution.py:237
  60.1 29.3 %copy-start.3 = (bf16[128,2080]{1,0:T(8,128)(2,1)}, bf16[128,2080]{1,0:T(8,128)(2,1)S(1)}, u32[]{:S(2)}) copy-start(bf16[128,2080]{1,0:T(8,128)(2,1)S(1)} %after.6.refs_1_.refs_4_.refs_5_) | copy-start | bytes 1597444
  60.1 29.3 %copy-start.4 = (bf16[128,2080]{1,0:T(8,128)(2,1)}, bf16[128,2080]{1,0:T(8,128)(2,1)S(1)}, u32[]{:S(2)}) copy-start(bf16[128,2080]{1,0:T(8,128)(2,1)S(1)} %after.7.refs_3_.refs_4_) | copy-start | bytes 1597444
  60.1 17.7 %collective-permute-start.14 = (bf16[2,64,2080]{2,1,0:T(8,128)(2,1)S(1)}, bf16[2,64,2080]{2,1,0:T(8,128)(2,1)S(1)}, u32[]{:S(2)}, u32[]{:S(2)}) collective-permute-start(bf16[2,64,2080]{2,1,0:T(8,128)(2,1)S(1)} %bitcast.75), channel_id=1, source_target_pairs={{0,2},{2,4},{4,6},{6,0},{1,3},{3,5},{5,7},{7,1},{8,10},{10,12},{12... | collective-permute-start | bytes 1597448 | tf_op jit(solution)/shard_map/ppermute | solution.py:237
  65.8 11.9 %collective-permute-start.15 = (bf16[2,64,2080]{2,1,0:T(8,128)(2,1)S(1)}, bf16[2,64,2080]{2,1,0:T(8,128)(2,1)S(1)}, u32[]{:S(2)}, u32[]{:S(2)}) collective-permute-start(bf16[2,64,2080]{2,1,0:T(8,128)(2,1)S(1)} %bitcast.78), channel_id=1, source_target_pairs={{0,6},{2,0},{4,2},{6,4},{1,7},{3,1},{5,3},{7,5},{8,14},{10,8},{12,... | collective-permute-start | bytes 1597448 | tf_op jit(solution)/shard_map/ppermute | solution.py:237
  68.0 11.9 %copy-start.30 = (bf16[128,768]{1,0:T(8,128)(2,1)}, bf16[128,768]{1,0:T(8,128)(2,1)S(1)}, u32[]{:S(2)}) copy-start(bf16[128,768]{1,0:T(8,128)(2,1)S(1)} %get-tuple-element.53.refs_9_) | copy-start | bytes 589828
  68.1 11.9 %copy-start.31 = (bf16[128,768]{1,0:T(8,128)(2,1)}, bf16[128,768]{1,0:T(8,128)(2,1)S(1)}, u32[]{:S(2)}) copy-start(bf16[128,768]{1,0:T(8,128)(2,1)S(1)} %get-tuple-element.50.refs_9_) | copy-start | bytes 589828
  68.1 15.7 %collective-permute-start.9 = (bf16[1,64,2080]{2,1,0:T(8,128)(2,1)S(1)}, bf16[1,64,2080]{2,1,0:T(8,128)(2,1)S(1)}, u32[]{:S(2)}, u32[]{:S(2)}) collective-permute-start(bf16[1,64,2080]{2,1,0:T(8,128)(2,1)S(1)} %bitcast.149), channel_id=1, source_target_pairs={{0,2},{2,4},{4,6},{6,0},{1,3},{3,5},{5,7},{7,1},{8,10},{10,12},{12... | collective-permute-start | bytes 798728 | tf_op jit(solution)/shard_map/ppermute | solution.py:237
  69.6 10.4 %copy-start.15 = (bf16[2,64,2080]{2,1,0:T(8,128)(2,1)}, bf16[2,64,2080]{2,1,0:T(8,128)(2,1)S(1)}, u32[]{:S(2)}) copy-start(bf16[2,64,2080]{2,1,0:T(8,128)(2,1)S(1)} %collective-permute-done.11) | copy-start | bytes 1597444
  69.6 14.1 %collective-permute-start.10 = (bf16[1,64,2080]{2,1,0:T(8,128)(2,1)S(1)}, bf16[1,64,2080]{2,1,0:T(8,128)(2,1)S(1)}, u32[]{:S(2)}, u32[]{:S(2)}) collective-permute-start(bf16[1,64,2080]{2,1,0:T(8,128)(2,1)S(1)} %bitcast.148), channel_id=1, source_target_pairs={{0,6},{2,0},{4,2},{6,4},{1,7},{3,1},{5,3},{7,5},{8,14},{10,8},{12,... | collective-permute-start | bytes 798728 | tf_op jit(solution)/shard_map/ppermute | solution.py:237
  74.9 14.4 %copy-start.8 = (bf16[2,64,2080]{2,1,0:T(8,128)(2,1)}, bf16[2,64,2080]{2,1,0:T(8,128)(2,1)S(1)}, u32[]{:S(2)}) copy-start(bf16[2,64,2080]{2,1,0:T(8,128)(2,1)S(1)} %collective-permute-done.16) | copy-start | bytes 1597444
  74.9 14.4 %collective-permute-start.19 = (bf16[2,64,2080]{2,1,0:T(8,128)(2,1)S(1)}, bf16[2,64,2080]{2,1,0:T(8,128)(2,1)S(1)}, u32[]{:S(2)}, u32[]{:S(2)}) collective-permute-start(bf16[2,64,2080]{2,1,0:T(8,128)(2,1)S(1)} %collective-permute-done.1), channel_id=1, source_target_pairs={{0,1},{1,0},{2,3},{3,2},{4,5},{5,4},{6,7},{7,6},{8,9},{9,8},{10,11... | collective-permute-start | bytes 1597448 | tf_op jit(solution)/shard_map/ppermute | solution.py:237
  77.8 2.2 %copy-start.16 = (bf16[2,64,2080]{2,1,0:T(8,128)(2,1)}, bf16[2,64,2080]{2,1,0:T(8,128)(2,1)S(1)}, u32[]{:S(2)}) copy-start(bf16[2,64,2080]{2,1,0:T(8,128)(2,1)S(1)} %collective-permute-done.14) | copy-start | bytes 1597444
  77.8 11.6 %copy-start.9 = (bf16[2,64,2080]{2,1,0:T(8,128)(2,1)}, bf16[2,64,2080]{2,1,0:T(8,128)(2,1)S(1)}, u32[]{:S(2)}) copy-start(bf16[2,64,2080]{2,1,0:T(8,128)(2,1)S(1)} %collective-permute-done.15) | copy-start | bytes 1597444
  80.0 14.6 %copy-start.22 = (bf16[128,768]{1,0:T(8,128)(2,1)}, bf16[128,768]{1,0:T(8,128)(2,1)S(1)}, u32[]{:S(2)}) copy-start(bf16[128,768]{1,0:T(8,128)(2,1)S(1)} %get-tuple-element.36.refs_4_.refs_11_) | copy-start | bytes 589828
  80.0 14.5 %copy-start.23 = (bf16[128,768]{1,0:T(8,128)(2,1)}, bf16[128,768]{1,0:T(8,128)(2,1)S(1)}, u32[]{:S(2)}) copy-start(bf16[128,768]{1,0:T(8,128)(2,1)S(1)} %get-tuple-element.39.refs_8_.refs_11_) | copy-start | bytes 589828
  83.9 11.5 %collective-permute-start.17 = (bf16[1,64,2080]{2,1,0:T(8,128)(2,1)S(1)}, bf16[1,64,2080]{2,1,0:T(8,128)(2,1)S(1)}, u32[]{:S(2)}, u32[]{:S(2)}) collective-permute-start(bf16[1,64,2080]{2,1,0:T(8,128)(2,1)S(1)} %bitcast.146), channel_id=1, source_target_pairs={{0,2},{2,4},{4,6},{6,0},{1,3},{3,5},{5,7},{7,1},{8,10},{10,12},{12... | collective-permute-start | bytes 798728 | tf_op jit(solution)/shard_map/ppermute | solution.py:237
  84.0 14.1 %collective-permute-start.18 = (bf16[1,64,2080]{2,1,0:T(8,128)(2,1)S(1)}, bf16[1,64,2080]{2,1,0:T(8,128)(2,1)S(1)}, u32[]{:S(2)}, u32[]{:S(2)}) collective-permute-start(bf16[1,64,2080]{2,1,0:T(8,128)(2,1)S(1)} %bitcast.144), channel_id=1, source_target_pairs={{0,6},{2,0},{4,2},{6,4},{1,7},{3,1},{5,3},{7,5},{8,14},{10,8},{12,... | collective-permute-start | bytes 798728 | tf_op jit(solution)/shard_map/ppermute | solution.py:237
  86.6 11.4 %collective-permute-start.20 = (bf16[1,64,2080]{2,1,0:T(8,128)(2,1)S(1)}, bf16[1,64,2080]{2,1,0:T(8,128)(2,1)S(1)}, u32[]{:S(2)}, u32[]{:S(2)}) collective-permute-start(bf16[1,64,2080]{2,1,0:T(8,128)(2,1)S(1)} %bitcast.143), channel_id=1, source_target_pairs={{0,2},{2,4},{4,6},{6,0},{1,3},{3,5},{5,7},{7,1},{8,10},{10,12},{12... | collective-permute-start | bytes 798728 | tf_op jit(solution)/shard_map/ppermute | solution.py:237
  86.6 11.4 %collective-permute-start.21 = (bf16[1,64,2080]{2,1,0:T(8,128)(2,1)S(1)}, bf16[1,64,2080]{2,1,0:T(8,128)(2,1)S(1)}, u32[]{:S(2)}, u32[]{:S(2)}) collective-permute-start(bf16[1,64,2080]{2,1,0:T(8,128)(2,1)S(1)} %bitcast.142), channel_id=1, source_target_pairs={{0,6},{2,0},{4,2},{6,4},{1,7},{3,1},{5,3},{7,5},{8,14},{10,8},{12,... | collective-permute-start | bytes 798728 | tf_op jit(solution)/shard_map/ppermute | solution.py:237
  89.3 5.2 %copy-start.19 = (bf16[2,64,2080]{2,1,0:T(8,128)(2,1)}, bf16[2,64,2080]{2,1,0:T(8,128)(2,1)S(1)}, u32[]{:S(2)}) copy-start(bf16[2,64,2080]{2,1,0:T(8,128)(2,1)S(1)} %collective-permute-done.19) | copy-start | bytes 1597444
  89.3 18.0 %copy-start.18 = (bf16[128,2080]{1,0:T(8,128)(2,1)S(1)}, bf16[128,2080]{1,0:T(8,128)(2,1)}, u32[]{:S(2)}) copy-start(bf16[128,2080]{1,0:T(8,128)(2,1)} %copy-done.17) | copy-start | bytes 1597444
  94.5 0.8 copy-start.20
  95.4 2.9 %copy-start.28 = (bf16[384,768]{1,0:T(8,128)(2,1)}, bf16[384,768]{1,0:T(8,128)(2,1)S(1)}, u32[]{:S(2)}) copy-start(bf16[384,768]{1,0:T(8,128)(2,1)S(1)} %get-tuple-element.54.refs_10_) | copy-start | bytes 1769476
  95.4 2.9 %copy-start.29 = (bf16[384,768]{1,0:T(8,128)(2,1)}, bf16[384,768]{1,0:T(8,128)(2,1)S(1)}, u32[]{:S(2)}) copy-start(bf16[384,768]{1,0:T(8,128)(2,1)S(1)} %get-tuple-element.51.refs_10_) | copy-start | bytes 1769476
  95.4 7.1 %collective-permute-start.23 = (bf16[1,64,2080]{2,1,0:T(8,128)(2,1)}, bf16[1,64,2080]{2,1,0:T(8,128)(2,1)S(1)}, u32[]{:S(2)}, u32[]{:S(2)}) collective-permute-start(bf16[1,64,2080]{2,1,0:T(8,128)(2,1)} %bitcast.49), channel_id=1, source_target_pairs={{0,2},{2,4},{4,6},{6,0},{1,3},{3,5},{5,7},{7,1},{8,10},{10,12},{12... | collective-permute-start | bytes 798728 | tf_op jit(solution)/shard_map/ppermute | solution.py:237
  95.4 7.1 %collective-permute-start.24 = (bf16[1,64,2080]{2,1,0:T(8,128)(2,1)}, bf16[1,64,2080]{2,1,0:T(8,128)(2,1)S(1)}, u32[]{:S(2)}, u32[]{:S(2)}) collective-permute-start(bf16[1,64,2080]{2,1,0:T(8,128)(2,1)} %bitcast.51), channel_id=1, source_target_pairs={{0,6},{2,0},{4,2},{6,4},{1,7},{3,1},{5,3},{7,5},{8,14},{10,8},{12,... | collective-permute-start | bytes 798728 | tf_op jit(solution)/shard_map/ppermute | solution.py:237
  98.2 9.1 %collective-permute-start.22 = (bf16[1,64,2080]{2,1,0:T(8,128)(2,1)S(1)}, bf16[1,64,2080]{2,1,0:T(8,128)(2,1)S(1)}, u32[]{:S(2)}, u32[]{:S(2)}) collective-permute-start(bf16[1,64,2080]{2,1,0:T(8,128)(2,1)S(1)} %bitcast.151), channel_id=1, source_target_pairs={{0,2},{2,4},{4,6},{6,0},{1,3},{3,5},{5,7},{7,1},{8,10},{10,12},{12... | collective-permute-start | bytes 798728 | tf_op jit(solution)/shard_map/ppermute | solution.py:237
  98.3 9.0 %collective-permute-start.25 = (bf16[1,64,2080]{2,1,0:T(8,128)(2,1)S(1)}, bf16[1,64,2080]{2,1,0:T(8,128)(2,1)S(1)}, u32[]{:S(2)}, u32[]{:S(2)}) collective-permute-start(bf16[1,64,2080]{2,1,0:T(8,128)(2,1)S(1)} %bitcast.150), channel_id=1, source_target_pairs={{0,6},{2,0},{4,2},{6,4},{1,7},{3,1},{5,3},{7,5},{8,14},{10,8},{12,... | collective-permute-start | bytes 798728 | tf_op jit(solution)/shard_map/ppermute | solution.py:237
  107.3 1.1 copy-start.21
  109.8 28.5 %all-to-all-start.1 = ((bf16[32,8,2080]{2,1,0:T(8,128)(2,1)}), bf16[32,8,2080]{2,1,0:T(8,128)(2,1)S(1)}, u32[]{:S(2)}, u32[]{:S(2)}) async-start(bf16[32,8,2080]{2,1,0:T(8,128)(2,1)} %bitcast.55), calls=%async_computation.1 | async-start | bytes 2228224 | tf_op jit(solution)/shard_map/all_to_all | solution.py:258
  128.6 9.8 %copy-start.24 = (s32[128]{0:T(128)S(1)}, s32[128]{0:T(128)}, u32[]{:S(2)}) copy-start(s32[128]{0:T(128)} %param.8) | copy-start | bytes 1540
  128.6 9.8 %copy-start.25 = (s32[128]{0:T(128)S(1)}, s32[128]{0:T(128)}, u32[]{:S(2)}) copy-start(s32[128]{0:T(128)} %param.9) | copy-start | bytes 1540

commit v5 on v4

--- a/solution.py
+++ b/solution.py
@@ -37,7 +37,7 @@
         in_specs=[VMEM] * len(args) + [ANY] * len(after),
         out_specs=(VMEM,) * len(outs),
         compiler_params=PARAMS,
-        cost_estimate=pl.CostEstimate(flops=0, bytes_accessed=0, transcendentals=0),
+        cost_estimate=pl.CostEstimate(flops=0, bytes_accessed=4 << 20, transcendentals=0),
         name=name,
     )(*args, *after)
 
@@ -111,6 +111,52 @@
     return hidden, dhidden, partials
 
 
+def forward_kernel(own, lft, far, wi_ref, hidden_ref, hidden_far_ref, slope_ref, slope_far_ref):
+    value, slope = gelu_parts(dot(stacked((own, lft, far)), wi_ref[...], 1, 0))
+    hidden_ref[...] = value[:256].astype(BF)
+    hidden_far_ref[...] = value[256:].astype(BF)
+    slope_ref[...] = slope[:256]
+    slope_far_ref[...] = slope[256:]
+
+
+def forward(own, lft, far, w_in):
+    units = w_in.shape[1]
+    outs = tuple(((rows, units), dtype) for dtype in (BF, F32) for rows in (256, 128))
+    return call(forward_kernel, outs, (own, lft, far, w_in), "forward")
+
+
+def far_kernel(g, slope_ref, wi_ref, wo_ref, dhidden_ref, out0, out1):
+    dhidden = (dot(g[...], wo_ref[...], 1, 0) * slope_ref[...]).astype(BF)
+    dhidden_ref[...] = dhidden
+    partial_value = dot(dhidden, wi_ref[...], 1, 1).astype(BF)
+    out0[...] = partial_value[:64]
+    out1[...] = partial_value[64:]
+
+
+def far_layer(g, slope, w_in, w_out_t, before):
+    width, units = w_in.shape
+    outs = (((128, units), BF),) + (((64, width), BF),) * 2
+    return call(far_kernel, outs, (g, slope, w_in, w_out_t), "far_layer", before)
+
+
+def rest_kernel(x, own, lft, rgt, slope_ref, wi_ref, wo_ref, hidden_ref, dhidden_ref, *outs):
+    value, slope = gelu_parts(dot(x[...], wi_ref[...], 1, 0))
+    hidden_ref[...] = value.astype(BF)
+    slope = jnp.concatenate([slope_ref[...], slope], axis=0)
+    dhidden = (dot(stacked((own, lft, rgt)), wo_ref[...], 1, 0) * slope).astype(BF)
+    dhidden_ref[...] = dhidden
+    partial_value = dot(dhidden, wi_ref[...], 1, 1).astype(BF)
+    outs[0][...] = partial_value[:128]
+    for i, out in enumerate(outs[1:]):
+        out[...] = partial_value[128 + 64 * i : 192 + 64 * i]
+
+
+def rest_layer(x, g, slope, w_in, w_out_t, before):
+    width, units = w_in.shape
+    outs = (((128, units), BF), ((384, units), BF), ((128, width), BF)) + (((64, width), BF),) * 4
+    return call(rest_kernel, outs, (x, *g, slope, w_in, w_out_t), "rest_layer", before)
+
+
 def middle_kernel(rgt, lft, far0, far1, rgt_out, lft_out):
     rgt_out[...] = (rgt[...].astype(F32) + far0[...].astype(F32)).astype(BF)
     lft_out[...] = (lft[...].astype(F32) + far1[...].astype(F32)).astype(BF)
@@ -173,8 +219,8 @@
 
 
 def weights_kernel(*refs):
-    pieces, factors = refs[:8], refs[8:12]
-    out, rows, b, blocks, sems, b_sems, out_sems = refs[12:]
+    pieces, factors = refs[:8], refs[8:-7]
+    out, rows, b, blocks, sems, b_sems, out_sems = refs[-7:]
     width = out.shape[0]
     cut = 1024
     loads = []
@@ -185,10 +231,11 @@
                 for i, piece in enumerate(pieces)
             ]
         )
-    loads[0] += [
-        pltpu.make_async_copy(factor, b.at[pl.ds(start, factor.shape[0]), :], b_sems.at[i])
-        for i, (factor, start) in enumerate(zip(factors, (0, 384, 512, 896)))
-    ]
+    start = 0
+    for i, factor in enumerate(factors):
+        size = factor.shape[0]
+        loads[0].append(pltpu.make_async_copy(factor, b.at[pl.ds(start, size), :], b_sems.at[i]))
+        start += size
     for part in loads:
         for copy in part:
             copy.start()
@@ -214,14 +261,14 @@
     return pl.pallas_call(
         weights_kernel,
         out_shape=pltpu.HBM((width, units), BF),
-        in_specs=[pl.BlockSpec(memory_space=pltpu.HBM)] * 12,
+        in_specs=[pl.BlockSpec(memory_space=pltpu.HBM)] * len(args),
         out_specs=pl.BlockSpec(memory_space=pltpu.HBM),
         scratch_shapes=[
             pltpu.VMEM((1024, width), BF),
             pltpu.VMEM((1024, units), BF),
             pltpu.VMEM((2, 256, units), BF),
             pltpu.SemaphoreType.DMA((16,)),
-            pltpu.SemaphoreType.DMA((4,)),
+            pltpu.SemaphoreType.DMA((len(factors),)),
             pltpu.SemaphoreType.DMA((2,)),
         ],
         compiler_params=PARAMS,
@@ -274,7 +321,7 @@
     g_lft, g_rgt, gz_own = right(g_own), left(g_own), other_z(g_own)
     xz_lft = other_z(x_lft)
 
-    gz_own = after(gz_own, g_lft, g_rgt)
+    gz_own = after(gz_own, g_lft)
     gz_lft, g_far, xz_far = right(gz_own), left(g_rgt), other_z(x_far)
     hidden_b, dhidden_b, partials = layer(
         (x_own, x_lft, x_rgt), (g_own, g_lft, g_rgt), first, second, (128, 64, 64, 64, 64)
@@ -285,21 +332,21 @@
     gz_far, gz_rgt, xz_rgt = right(gz_lft), left(gz_own), other_z(x_rgt)
     p_own, lft0, lft1, rgt0, rgt1 = partials
     s_lft1, s_rgt0 = right(rgt1), left(lft0)
-    hidden_a, dhidden_a, (far0, far1) = layer((x_far,), (g_far,), first, second, (64, 64), (s_lft1, s_rgt0))
+    hidden_a, dhidden_a, (far0, far1) = layer((x_far,), (g_far,), first, second, (64, 64), (s_lft1, s_rgt0, ))
     arrived = right(far0), left(far1)
-    hidden_az, dhidden_az, (far0, far1) = layer((xz_far,), (gz_far,), first, second, (64, 64), (gz_rgt, xz_lft))
-    rgt0, lft1 = middle(rgt0, lft1, *arrived, (hidden_az,))
+    hidden_bz, hidden_az, slope, slope_far = forward(xz_own, xz_lft, xz_far, first)
+    dhidden_az, far0, far1 = far_layer(gz_far, slope_far, first, second, (gz_rgt,))
+    rgt0, lft1 = middle(rgt0, lft1, *arrived, (dhidden_az,))
     summands = p_own, right(rgt0), s_lft1, s_rgt0, left(lft1)
-    hidden_bz, dhidden_bz, partials_z = layer(
-        (xz_own, xz_lft, xz_rgt), (gz_own, gz_lft, gz_rgt), first, second, (128, 64, 64, 64, 64), (dhidden_az,)
+    hidden_cz, dhidden_bz, pz_own, lft0, lft1, rgt0, rgt1 = rest_layer(
+        xz_rgt, (gz_own, gz_lft, gz_rgt), slope, first, second, (dhidden_az,)
     )
-    pz_own, lft0, lft1, rgt0, rgt1 = partials_z
-    s_lft1, s_rgt0 = right(rgt1), left(lft0)
-    rgt0, lft1 = middle(rgt0, lft1, right(far0), left(far1), summands[1:])
-    summands_z = pz_own, right(rgt0), s_lft1, s_rgt0, left(lft1)
+    sz_lft1, sz_rgt0 = right(rgt1), left(lft0)
+    rgt0, lft1 = middle(rgt0, lft1, right(far0), left(far1), (*summands[1:], ))
+    summands_z = pz_own, right(rgt0), sz_lft1, sz_rgt0, left(lft1)
     g_all = (g_own, g_lft, g_rgt, g_far, gz_own, gz_lft, gz_rgt, gz_far)
     x_all = (x_own, x_lft, x_rgt, x_far, xz_own, xz_lft, xz_rgt, xz_far)
-    grad_out_w = weights(g_all, (hidden_b, hidden_a, hidden_bz, hidden_az))
+    grad_out_w = weights(g_all, (hidden_b, hidden_a, hidden_bz, hidden_cz, hidden_az))
     grad_in = weights(x_all, (dhidden_b, dhidden_a, dhidden_bz, dhidden_az))
     came_back = exchange(total(z, summands, summands_z), WIDE_AND_Z)
     tokens = finish(came_back, expert, place)

time: 140 us -> 139 us (level)
  Pallas kernels: 37.7 us -> 39.7 us
    pallas_call x7 -> x8, Pallas kernels: 15.3 us -> 17.1 us  [call(): pl.pallas_call(ordered, out_shape=tuple((jax.ShapeDtypeStruct(s, d) for s...]
  transfers between devices with their start and end apart: 27 -> 27, of which waited for: 8 -> 8; matrix products, arithmetic and copies ran while one was open for 0% -> 0% of each run, Pallas kernels for 25% -> 27%
where the time goes in v5:
time: 139 us; the launch traced here: 138 us
  Pallas kernels  39.7 us (29%)
  waiting for transfers between devices  39.4 us (28%)
  starting transfers between devices  35.5 us (26%)
  blocking collectives  21.9 us (16%)
    ppermute x26, waiting for transfers between devices, move(): return lax.ppermute(blocks, axis, pairs).reshape(value.shape)  39.4 us
    ppermute x26, starting transfers between devices, move(): return lax.ppermute(blocks, axis, pairs).reshape(value.shape)  27.9 us
    all_to_all x1, blocking collectives, exchange(): lax.all_to_all(blocks, axes, split_axis=0, concat_axis=0, tiled=True)  21.9 us
    pallas_call x2, Pallas kernels, weights(): pl.pallas_call(weights_kernel, out_shape=pltpu.HBM((width, units), BF), i...  19.5 us
    pallas_call x8, Pallas kernels, call(): pl.pallas_call(ordered, out_shape=tuple((jax.ShapeDtypeStruct(s, d) for s...  17.1 us
    all_to_all x1, starting transfers between devices, exchange(): lax.all_to_all(blocks, axes, split_axis=0, concat_axis=0, tiled=True)  7.6 us
  transfers between devices with their start and end apart: 27, of which 8 were waited for; matrix products, arithmetic and copies ran while one was open for 0% of the time, Pallas kernels for 27%

profile of v5, /device:TPU:1, one launch (start us, length us, event | category | flops | bytes accessed | tf_op | source)
XLA Modules:
  0.0 138.5 jit_solution(14390503694092236598)
XLA Ops:
  0.6 2.1 %collective-permute-start = (bf16[2,64,2080]{2,1,0:T(8,128)(2,1)}, bf16[2,64,2080]{2,1,0:T(8,128)(2,1)S(1)}, u32[]{:S(2)}, u32[]{:S(2)}) collective-permute-start(bf16[2,64,2080]{2,1,0:T(8,128)(2,1)} %bitcast.113), channel_id=1, source_target_pairs={{0,2},{2,4},{4,6},{6,0},{1,3},{3,5},{5,7},{7,1},{8,10},{10,12},{12... | collective-permute-start | bytes 1597448 | tf_op jit(solution)/shard_map/ppermute | solution.py:284
  2.7 1.4 collective-permute-start.1
  4.1 1.6 %collective-permute-start.2 = (bf16[2,64,2080]{2,1,0:T(8,128)(2,1)}, bf16[2,64,2080]{2,1,0:T(8,128)(2,1)S(1)}, u32[]{:S(2)}, u32[]{:S(2)}) collective-permute-start(bf16[2,64,2080]{2,1,0:T(8,128)(2,1)} %bitcast.115), channel_id=1, source_target_pairs={{0,4},{2,6},{4,0},{6,2},{1,5},{3,7},{5,1},{7,3},{8,12},{10,14},{12... | collective-permute-start | bytes 1597448 | tf_op jit(solution)/shard_map/ppermute | solution.py:284
  5.7 1.6 %collective-permute-start.3 = (bf16[2,64,2080]{2,1,0:T(8,128)(2,1)}, bf16[2,64,2080]{2,1,0:T(8,128)(2,1)S(1)}, u32[]{:S(2)}, u32[]{:S(2)}) collective-permute-start(bf16[2,64,2080]{2,1,0:T(8,128)(2,1)} %bitcast.116), channel_id=1, source_target_pairs={{0,1},{1,0},{2,3},{3,2},{4,5},{5,4},{6,7},{7,6},{8,9},{9,8},{10,11... | collective-permute-start | bytes 1597448 | tf_op jit(solution)/shard_map/ppermute | solution.py:284
  7.4 1.6 %prepare.1 = bf16[128,2080]{1,0:T(8,128)(2,1)S(1)} custom-call(bf16[2080,128]{1,0:T(8,128)(2,1)} %bitcast.149, s32[1,128]{1,0:T(1,128)} %bitcast.137, s32[1,128]{1,0:T(1,128)} %bitcast.139, f32[1,128]{1,0:T(1,128)} %bitcast.151), custom_call_target="tpu_custom_call" | custom-call | flops 68157440 | bytes 2129920 | tf_op jit(solution)/shard_map/prepare/pallas_call | solution.py:70
  8.9 0.0 copy-start
  9.0 0.0 copy-start.13
  9.0 21.9 %all_to_all.10 = bf16[16,8,2080]{2,1,0:T(8,128)(2,1)S(1)} all-to-all(bf16[16,8,2080]{2,1,0:T(8,128)(2,1)S(1)} %bitcast.99), channel_id=1, replica_groups=mesh['y'=4,'zh'=2,'core'=2,'x'=4,'zl'=2] {'y','zh','core'}, dimensions={0} | all-to-all | bytes 1064960 | tf_op jit(solution)/shard_map/all_to_all | solution.py:305
  30.9 0.0 collective-permute-done
  30.9 0.0 collective-permute-done.1
  30.9 0.0 collective-permute-done.2
  31.0 0.9 collective-permute-start.5
  31.9 0.6 collective-permute-start.4
  32.5 0.0 collective-permute-start.11
  32.6 12.3 %collective-permute-done.5 = bf16[2,64,2080]{2,1,0:T(8,128)(2,1)S(1)} collective-permute-done((bf16[2,64,2080]{2,1,0:T(8,128)(2,1)S(1)}, bf16[2,64,2080]{2,1,0:T(8,128)(2,1)S(1)}, u32[]{:S(2)}, u32[]{:S(2)}) %collective-permute-start.5) | collective-permute-done | bytes 532512 | tf_op jit(solution)/shard_map/ppermute | solution.py:284
  44.9 1.7 %collective-permute-start.6 = (bf16[2,64,2080]{2,1,0:T(8,128)(2,1)S(1)}, bf16[2,64,2080]{2,1,0:T(8,128)(2,1)S(1)}, u32[]{:S(2)}, u32[]{:S(2)}) collective-permute-start(bf16[2,64,2080]{2,1,0:T(8,128)(2,1)S(1)} %collective-permute-done.5), channel_id=1, source_target_pairs={{0,6},{2,0},{4,2},{6,4},{1,7},{3,1},{5,3},{7,5},{8,14},{10,8},{12,... | collective-permute-start | bytes 1597448 | tf_op jit(solution)/shard_map/ppermute | solution.py:284
  46.6 0.0 collective-permute-done.4
  46.6 0.1 collective-permute-start.12
  46.7 4.4 %layer.2 = (bf16[384,768]{1,0:T(8,128)(2,1)S(1)}, bf16[384,768]{1,0:T(8,128)(2,1)S(1)}, bf16[128,2080]{1,0:T(8,128)(2,1)S(1)}, bf16[64,2080]{1,0:T(8,128)(2,1)S(...) custom-call(bf16[128,2080]{1,0:T(8,128)(2,1)S(1)} %bitcast.118, ...), custom_call_target="tpu_custom_call" | custom-call | bytes 4194304 | tf_op jit(solution)/shard_map/layer/pallas_call | solution.py:34
  51.2 0.0 copy-start.24
  51.2 0.0 copy-start.17
  51.2 0.2 collective-permute-start.7
  51.4 0.0 collective-permute-start.14
  51.4 1.5 %collective-permute-start.15 = (bf16[2,64,2080]{2,1,0:T(8,128)(2,1)S(1)}, bf16[2,64,2080]{2,1,0:T(8,128)(2,1)S(1)}, u32[]{:S(2)}, u32[]{:S(2)}) collective-permute-start(bf16[2,64,2080]{2,1,0:T(8,128)(2,1)S(1)} %collective-permute-done.2), channel_id=1, source_target_pairs={{0,1},{1,0},{2,3},{3,2},{4,5},{5,4},{6,7},{7,6},{8,9},{9,8},{10,11... | collective-permute-start | bytes 1597448 | tf_op jit(solution)/shard_map/ppermute | solution.py:284
  52.9 4.9 %collective-permute-done.6 = bf16[2,64,2080]{2,1,0:T(8,128)(2,1)S(1)} collective-permute-done((bf16[2,64,2080]{2,1,0:T(8,128)(2,1)S(1)}, bf16[2,64,2080]{2,1,0:T(8,128)(2,1)S(1)}, u32[]{:S(2)}, u32[]{:S(2)}) %collective-permute-start.6) | collective-permute-done | bytes 532512 | tf_op jit(solution)/shard_map/ppermute | solution.py:284
  57.8 2.6 %collective-permute-start.8 = (bf16[1,64,2080]{2,1,0:T(8,128)(2,1)S(1)}, bf16[1,64,2080]{2,1,0:T(8,128)(2,1)S(1)}, u32[]{:S(2)}, u32[]{:S(2)}) collective-permute-start(bf16[1,64,2080]{2,1,0:T(8,128)(2,1)S(1)} %bitcast.144), channel_id=1, source_target_pairs={{0,6},{2,0},{4,2},{6,4},{1,7},{3,1},{5,3},{7,5},{8,14},{10,8},{12,... | collective-permute-start | bytes 798728 | tf_op jit(solution)/shard_map/ppermute | solution.py:284
  60.4 0.1 collective-permute-start.13
  60.5 5.7 %collective-permute-done.7 = bf16[1,64,2080]{2,1,0:T(8,128)(2,1)S(1)} collective-permute-done((bf16[1,64,2080]{2,1,0:T(8,128)(2,1)S(1)}, bf16[1,64,2080]{2,1,0:T(8,128)(2,1)S(1)}, u32[]{:S(2)}, u32[]{:S(2)}) %collective-permute-start.7) | collective-permute-done | bytes 266272 | tf_op jit(solution)/shard_map/ppermute | solution.py:284
  66.2 2.2 %layer.3 = (bf16[128,768]{1,0:T(8,128)(2,1)S(1)}, bf16[128,768]{1,0:T(8,128)(2,1)S(1)}, bf16[64,2080]{1,0:T(8,128)(2,1)S(1)}, bf16[64,2080]{1,0:T(8,128)(2,1)S(1)}) custom-call(bf16[128,2080]{1,0:T(8,128)(2,1)S(1)} %bitcast.101, bf16[128,2080]{1,0:T(8,128)(2,1)S(1)} %bitcast.107, bf16[2080,768]{1,0:T(8,128)(2,1)S(1)} %bitcast.63, ...), custom_call_target="tpu_custom_call" | custom-call | bytes 4194304 | tf_op jit(solution)/shard_map/layer/pallas_call | solution.py:34
  68.4 0.7 copy-done.28
  69.0 1.5 %collective-permute-start.9 = (bf16[1,64,2080]{2,1,0:T(8,128)(2,1)S(1)}, bf16[1,64,2080]{2,1,0:T(8,128)(2,1)S(1)}, u32[]{:S(2)}, u32[]{:S(2)}) collective-permute-start(bf16[1,64,2080]{2,1,0:T(8,128)(2,1)S(1)} %bitcast.147), channel_id=1, source_target_pairs={{0,2},{2,4},{4,6},{6,0},{1,3},{3,5},{5,7},{7,1},{8,10},{10,12},{12... | collective-permute-start | bytes 798728 | tf_op jit(solution)/shard_map/ppermute | solution.py:284
  70.5 0.0 collective-permute-done.14
  70.5 1.2 collective-permute-start.10
  71.7 3.3 %collective-permute-done.15 = bf16[2,64,2080]{2,1,0:T(8,128)(2,1)S(1)} collective-permute-done((bf16[2,64,2080]{2,1,0:T(8,128)(2,1)S(1)}, bf16[2,64,2080]{2,1,0:T(8,128)(2,1)S(1)}, u32[]{:S(2)}, u32[]{:S(2)}) %collective-permute-start.15) | collective-permute-done | bytes 532512 | tf_op jit(solution)/shard_map/ppermute | solution.py:284
  75.0 0.0 collective-permute-start.19
  75.1 1.8 %forward.1 = (bf16[256,768]{1,0:T(8,128)(2,1)S(1)}, bf16[128,768]{1,0:T(8,128)(2,1)S(1)}, f32[256,768]{1,0:T(8,128)S(1)}, f32[128,768]{1,0:T(8,128)S(1)}) custom-call(bf16[128,2080]{1,0:T(8,128)(2,1)S(1)} %bitcast.94, bf16[128,2080]{1,0:T(8,128)(2,1)S(1)} %bitcast.121, bf16[128,2080]{1,0:T(8,128)(2,1)S(1)} %bitcast.123, bf16[2080,768]{1,0:T(8,128)(2,1)S(1)} %bitcast.64), custom_call_target="tpu_custom_call" | custom-call | bytes 4194304 | tf_op jit(solution)/shard_map/forward/pallas_call | solution.py:34
  76.8 0.0 copy-start.26
  76.9 1.2 collective-permute-done.13
  78.1 1.8 %far_layer.1 = (bf16[128,768]{1,0:T(8,128)(2,1)S(1)}, bf16[64,2080]{1,0:T(8,128)(2,1)S(1)}, bf16[64,2080]{1,0:T(8,128)(2,1)S(1)}) custom-call(bf16[128,2080]{1,0:T(8,128)(2,1)S(1)} %bitcast.127, f32[128,768]{1,0:T(8,128)S(1)} %get-tuple-element.39.refs_1_, bf16[2080,768]{1,0:T(8,128)(2,1)S(1)} %bitcast.65, bf16[2080,768]{1,0:T(8,128)(2,1)S(1)} %bitcast.69, ...), custom_call_target="tpu_custom_call" | custom-call | bytes 4194304 | tf_op jit(solution)/shard_map/far_layer/pallas_call | solution.py:34
  79.9 4.1 %collective-permute-done.9 = bf16[1,64,2080]{2,1,0:T(8,128)(2,1)S(1)} collective-permute-done((bf16[1,64,2080]{2,1,0:T(8,128)(2,1)S(1)}, bf16[1,64,2080]{2,1,0:T(8,128)(2,1)S(1)}, u32[]{:S(2)}, u32[]{:S(2)}) %collective-permute-start.9) | collective-permute-done | bytes 266272 | tf_op jit(solution)/shard_map/ppermute | solution.py:284
  84.0 0.1 middle.2
  84.2 0.1 collective-permute-start.17
  84.3 2.7 %collective-permute-start.18 = (bf16[1,64,2080]{2,1,0:T(8,128)(2,1)S(1)}, bf16[1,64,2080]{2,1,0:T(8,128)(2,1)S(1)}, u32[]{:S(2)}, u32[]{:S(2)}) collective-permute-start(bf16[1,64,2080]{2,1,0:T(8,128)(2,1)S(1)} %bitcast.143), channel_id=1, source_target_pairs={{0,6},{2,0},{4,2},{6,4},{1,7},{3,1},{5,3},{7,5},{8,14},{10,8},{12,... | collective-permute-start | bytes 798728 | tf_op jit(solution)/shard_map/ppermute | solution.py:284
  86.9 0.0 collective-permute-start.20
  86.9 2.7 %collective-permute-start.21 = (bf16[1,64,2080]{2,1,0:T(8,128)(2,1)S(1)}, bf16[1,64,2080]{2,1,0:T(8,128)(2,1)S(1)}, u32[]{:S(2)}, u32[]{:S(2)}) collective-permute-start(bf16[1,64,2080]{2,1,0:T(8,128)(2,1)S(1)} %bitcast.141), channel_id=1, source_target_pairs={{0,6},{2,0},{4,2},{6,4},{1,7},{3,1},{5,3},{7,5},{8,14},{10,8},{12,... | collective-permute-start | bytes 798728 | tf_op jit(solution)/shard_map/ppermute | solution.py:284
  89.6 0.0 copy-start.18
  89.6 4.9 %rest_layer.1 = (bf16[128,768]{1,0:T(8,128)(2,1)S(1)}, bf16[384,768]{1,0:T(8,128)(2,1)S(1)}, bf16[128,2080]{1,0:T(8,128)(2,1)S(1)}, bf16[64,2080]{1,0:T(8,128)(2...) custom-call(bf16[128,2080]{1,0:T(8,128)(2,1)S(1)} %bitcast.125, ...), custom_call_target="tpu_custom_call" | custom-call | bytes 4194304 | tf_op jit(solution)/shard_map/rest_layer/pallas_call | solution.py:34
  94.5 0.1 collective-permute-start.23
  94.6 0.0 collective-permute-done.17
  94.6 2.7 %collective-permute-start.24 = (bf16[1,64,2080]{2,1,0:T(8,128)(2,1)}, bf16[1,64,2080]{2,1,0:T(8,128)(2,1)S(1)}, u32[]{:S(2)}, u32[]{:S(2)}) collective-permute-start(bf16[1,64,2080]{2,1,0:T(8,128)(2,1)} %bitcast.51), channel_id=1, source_target_pairs={{0,6},{2,0},{4,2},{6,4},{1,7},{3,1},{5,3},{7,5},{8,14},{10,8},{12,... | collective-permute-start | bytes 798728 | tf_op jit(solution)/shard_map/ppermute | solution.py:284
  97.3 0.0 collective-permute-done.18
  97.3 0.9 middle.3
  98.2 0.0 collective-permute-start.22
  98.2 2.7 %collective-permute-start.25 = (bf16[1,64,2080]{2,1,0:T(8,128)(2,1)}, bf16[1,64,2080]{2,1,0:T(8,128)(2,1)S(1)}, u32[]{:S(2)}, u32[]{:S(2)}) collective-permute-start(bf16[1,64,2080]{2,1,0:T(8,128)(2,1)} %bitcast.53), channel_id=1, source_target_pairs={{0,6},{2,0},{4,2},{6,4},{1,7},{3,1},{5,3},{7,5},{8,14},{10,8},{12,... | collective-permute-start | bytes 798728 | tf_op jit(solution)/shard_map/ppermute | solution.py:284
  100.8 1.9 %collective-permute-done.23 = bf16[1,64,2080]{2,1,0:T(8,128)(2,1)S(1)} collective-permute-done((bf16[1,64,2080]{2,1,0:T(8,128)(2,1)}, bf16[1,64,2080]{2,1,0:T(8,128)(2,1)S(1)}, u32[]{:S(2)}, u32[]{:S(2)}) %collective-permute-start.23) | collective-permute-done | bytes 266272 | tf_op jit(solution)/shard_map/ppermute | solution.py:284
  102.8 0.0 collective-permute-done.24
  102.8 5.9 %collective-permute-done.22 = bf16[1,64,2080]{2,1,0:T(8,128)(2,1)S(1)} collective-permute-done((bf16[1,64,2080]{2,1,0:T(8,128)(2,1)}, bf16[1,64,2080]{2,1,0:T(8,128)(2,1)S(1)}, u32[]{:S(2)}, u32[]{:S(2)}) %collective-permute-start.22) | collective-permute-done | bytes 266272 | tf_op jit(solution)/shard_map/ppermute | solution.py:284
  108.7 1.4 %total.1 = bf16[256,2080]{1,0:T(8,128)(2,1)} custom-call(s32[1]{0:T(128)} %bitcast.z_ref, bf16[128,2080]{1,0:T(8,128)(2,1)S(1)} %copy-done.18, bf16[64,2080]{1,0:T(8,128)(2,1)S(1)} %bitcast.110, bf16[64,2080]{1,0:T(8,128)(2,1)S(1)} %bitcast.83, bf16[64,2080]{1,0:T(8,128)(2,1)S(1)} %bitcast.86, bf16[64,2080]{1,0:T(8,128)(2,1)S(1)} %bitcast.112, ...), custom_call_target="tpu_custom_call" | custom-call | tf_op jit(solution)/shard_map/total/pallas_call | solution.py:199
  110.1 7.6 %all-to-all-start.1 = ((bf16[32,8,2080]{2,1,0:T(8,128)(2,1)}), bf16[32,8,2080]{2,1,0:T(8,128)(2,1)S(1)}, u32[]{:S(2)}, u32[]{:S(2)}) async-start(bf16[32,8,2080]{2,1,0:T(8,128)(2,1)} %bitcast.55), calls=%async_computation.1 | async-start | bytes 2228224 | tf_op jit(solution)/shard_map/all_to_all | solution.py:305
  117.7 9.8 %weights.2 = bf16[2080,768]{1,0:T(8,128)(2,1)} custom-call(bf16[128,2080]{1,0:T(8,128)(2,1)} %bitcast.117, bf16[128,2080]{1,0:T(8,128)(2,1)} %bitcast.89, bf16[128,2080]{1,0:T(8,128)(2,1)} %bitcast.92, bf16[128,2080]{1,0:T(8,128)(2,1)} %bitcast.102, bf16[128,2080]{1,0:T(8,128)(2,1)} %bitcast.95, bf16[128,2080]{1,0:T(8,128)(2,1)} %bitcast.122, ...), custom_call_target="tpu_custom_call" | custom-call | flops 3271557120 | bytes 10485760 | tf_op jit(solution)/shard_map/weights/pallas_call | solution.py:261
  127.5 0.0 copy-start.21
  127.5 0.0 copy-start.22
  127.5 9.8 %weights.3 = bf16[2080,768]{1,0:T(8,128)(2,1)} custom-call(bf16[128,2080]{1,0:T(8,128)(2,1)} %copy-done.2, bf16[128,2080]{1,0:T(8,128)(2,1)} %bitcast.98, bf16[128,2080]{1,0:T(8,128)(2,1)} %bitcast.120, bf16[128,2080]{1,0:T(8,128)(2,1)} %bitcast.108, bf16[128,2080]{1,0:T(8,128)(2,1)} %copy-done.4, bf16[128,2080]{1,0:T(8,128)(2,1)} %copy-done.3, ...), custom_call_target="tpu_custom_call" | custom-call | flops 3271557120 | bytes 10485760 | tf_op jit(solution)/shard_map/weights/pallas_call | solution.py:261
  137.3 1.2 finish.1
  (69 shorter events, 0.1 us)
Async XLA Ops:
  0.6 30.3 %collective-permute-start = (bf16[2,64,2080]{2,1,0:T(8,128)(2,1)}, bf16[2,64,2080]{2,1,0:T(8,128)(2,1)S(1)}, u32[]{:S(2)}, u32[]{:S(2)}) collective-permute-start(bf16[2,64,2080]{2,1,0:T(8,128)(2,1)} %bitcast.113), channel_id=1, source_target_pairs={{0,2},{2,4},{4,6},{6,0},{1,3},{3,5},{5,7},{7,1},{8,10},{10,12},{12... | collective-permute-start | bytes 1597448 | tf_op jit(solution)/shard_map/ppermute | solution.py:284
  2.7 28.2 %collective-permute-start.1 = (bf16[2,64,2080]{2,1,0:T(8,128)(2,1)}, bf16[2,64,2080]{2,1,0:T(8,128)(2,1)S(1)}, u32[]{:S(2)}, u32[]{:S(2)}) collective-permute-start(bf16[2,64,2080]{2,1,0:T(8,128)(2,1)} %bitcast.114), channel_id=1, source_target_pairs={{0,6},{2,0},{4,2},{6,4},{1,7},{3,1},{5,3},{7,5},{8,14},{10,8},{12,... | collective-permute-start | bytes 1597448 | tf_op jit(solution)/shard_map/ppermute | solution.py:284
  4.1 26.8 %collective-permute-start.2 = (bf16[2,64,2080]{2,1,0:T(8,128)(2,1)}, bf16[2,64,2080]{2,1,0:T(8,128)(2,1)S(1)}, u32[]{:S(2)}, u32[]{:S(2)}) collective-permute-start(bf16[2,64,2080]{2,1,0:T(8,128)(2,1)} %bitcast.115), channel_id=1, source_target_pairs={{0,4},{2,6},{4,0},{6,2},{1,5},{3,7},{5,1},{7,3},{8,12},{10,14},{12... | collective-permute-start | bytes 1597448 | tf_op jit(solution)/shard_map/ppermute | solution.py:284
  5.7 25.2 %collective-permute-start.3 = (bf16[2,64,2080]{2,1,0:T(8,128)(2,1)}, bf16[2,64,2080]{2,1,0:T(8,128)(2,1)S(1)}, u32[]{:S(2)}, u32[]{:S(2)}) collective-permute-start(bf16[2,64,2080]{2,1,0:T(8,128)(2,1)} %bitcast.116), channel_id=1, source_target_pairs={{0,1},{1,0},{2,3},{3,2},{4,5},{5,4},{6,7},{7,6},{8,9},{9,8},{10,11... | collective-permute-start | bytes 1597448 | tf_op jit(solution)/shard_map/ppermute | solution.py:284
  7.4 39.3 %copy-start.1 = (bf16[1,768,2080]{1,2,0:T(8,128)(2,1)S(1)}, bf16[1,768,2080]{1,2,0:T(8,128)(2,1)}, u32[]{:S(2)}) copy-start(bf16[1,768,2080]{1,2,0:T(8,128)(2,1)} %param.13) | copy-start | bytes 9584644
  8.9 37.8 %copy-start = (bf16[1,2080,768]{2,1,0:T(8,128)(2,1)S(1)}, bf16[1,2080,768]{2,1,0:T(8,128)(2,1)}, u32[]{:S(2)}) copy-start(bf16[1,2080,768]{2,1,0:T(8,128)(2,1)} %param.12) | copy-start | bytes 9584644
  9.0 37.8 %copy-start.13 = (bf16[1,16,8,2080]{3,2,1,0:T(8,128)(2,1)S(1)}, bf16[1,16,8,2080]{3,2,1,0:T(8,128)(2,1)}, u32[]{:S(2)}) copy-start(bf16[1,16,8,2080]{3,2,1,0:T(8,128)(2,1)} %param.11) | copy-start | bytes 1597444
  30.9 20.5 %copy-start.5 = (bf16[2,64,2080]{2,1,0:T(8,128)(2,1)}, bf16[2,64,2080]{2,1,0:T(8,128)(2,1)S(1)}, u32[]{:S(2)}) copy-start(bf16[2,64,2080]{2,1,0:T(8,128)(2,1)S(1)} %collective-permute-done) | copy-start | bytes 1597444
  30.9 44.1 %copy-start.6 = (bf16[2,64,2080]{2,1,0:T(8,128)(2,1)}, bf16[2,64,2080]{2,1,0:T(8,128)(2,1)S(1)}, u32[]{:S(2)}) copy-start(bf16[2,64,2080]{2,1,0:T(8,128)(2,1)S(1)} %collective-permute-done.1) | copy-start | bytes 1597444
  30.9 35.2 %copy-start.9 = (bf16[2,64,2080]{2,1,0:T(8,128)(2,1)}, bf16[2,64,2080]{2,1,0:T(8,128)(2,1)S(1)}, u32[]{:S(2)}) copy-start(bf16[2,64,2080]{2,1,0:T(8,128)(2,1)S(1)} %collective-permute-done.2) | copy-start | bytes 1597444
  31.0 44.1 %copy-start.7 = (bf16[2,64,2080]{2,1,0:T(8,128)(2,1)}, bf16[2,64,2080]{2,1,0:T(8,128)(2,1)S(1)}, u32[]{:S(2)}) copy-start(bf16[2,64,2080]{2,1,0:T(8,128)(2,1)S(1)} %collective-permute-done.3) | copy-start | bytes 1597444
  31.0 20.2 %copy-start.2 = (bf16[128,2080]{1,0:T(8,128)(2,1)}, bf16[128,2080]{1,0:T(8,128)(2,1)S(1)}, u32[]{:S(2)}) copy-start(bf16[128,2080]{1,0:T(8,128)(2,1)S(1)} %after.4.refs_3_.refs_0_) | copy-start | bytes 1597444
  31.0 13.9 %collective-permute-start.5 = (bf16[2,64,2080]{2,1,0:T(8,128)(2,1)S(1)}, bf16[2,64,2080]{2,1,0:T(8,128)(2,1)S(1)}, u32[]{:S(2)}, u32[]{:S(2)}) collective-permute-start(bf16[2,64,2080]{2,1,0:T(8,128)(2,1)S(1)} %bitcast.72), channel_id=1, source_target_pairs={{0,6},{2,0},{4,2},{6,4},{1,7},{3,1},{5,3},{7,5},{8,14},{10,8},{12,... | collective-permute-start | bytes 1597448 | tf_op jit(solution)/shard_map/ppermute | solution.py:284
  31.9 14.7 %collective-permute-start.4 = (bf16[2,64,2080]{2,1,0:T(8,128)(2,1)S(1)}, bf16[2,64,2080]{2,1,0:T(8,128)(2,1)S(1)}, u32[]{:S(2)}, u32[]{:S(2)}) collective-permute-start(bf16[2,64,2080]{2,1,0:T(8,128)(2,1)S(1)} %bitcast.73), channel_id=1, source_target_pairs={{0,2},{2,4},{4,6},{6,0},{1,3},{3,5},{5,7},{7,1},{8,10},{10,12},{12... | collective-permute-start | bytes 1597448 | tf_op jit(solution)/shard_map/ppermute | solution.py:284
  32.5 14.1 %collective-permute-start.11 = (bf16[2,64,2080]{2,1,0:T(8,128)(2,1)S(1)}, bf16[2,64,2080]{2,1,0:T(8,128)(2,1)S(1)}, u32[]{:S(2)}, u32[]{:S(2)}) collective-permute-start(bf16[2,64,2080]{2,1,0:T(8,128)(2,1)S(1)} %bitcast.74), channel_id=1, source_target_pairs={{0,1},{1,0},{2,3},{3,2},{4,5},{5,4},{6,7},{7,6},{8,9},{9,8},{10,11... | collective-permute-start | bytes 1597448 | tf_op jit(solution)/shard_map/ppermute | solution.py:284
  44.9 6.3 %copy-start.14 = (bf16[2,64,2080]{2,1,0:T(8,128)(2,1)}, bf16[2,64,2080]{2,1,0:T(8,128)(2,1)S(1)}, u32[]{:S(2)}) copy-start(bf16[2,64,2080]{2,1,0:T(8,128)(2,1)S(1)} %collective-permute-done.5) | copy-start | bytes 1597444
  44.9 12.9 %collective-permute-start.6 = (bf16[2,64,2080]{2,1,0:T(8,128)(2,1)S(1)}, bf16[2,64,2080]{2,1,0:T(8,128)(2,1)S(1)}, u32[]{:S(2)}, u32[]{:S(2)}) collective-permute-start(bf16[2,64,2080]{2,1,0:T(8,128)(2,1)S(1)} %collective-permute-done.5), channel_id=1, source_target_pairs={{0,6},{2,0},{4,2},{6,4},{1,7},{3,1},{5,3},{7,5},{8,14},{10,8},{12,... | collective-permute-start | bytes 1597448 | tf_op jit(solution)/shard_map/ppermute | solution.py:284
  46.6 4.6 %copy-start.8 = (bf16[2,64,2080]{2,1,0:T(8,128)(2,1)}, bf16[2,64,2080]{2,1,0:T(8,128)(2,1)S(1)}, u32[]{:S(2)}) copy-start(bf16[2,64,2080]{2,1,0:T(8,128)(2,1)S(1)} %collective-permute-done.4) | copy-start | bytes 1597444
  46.6 13.7 %collective-permute-start.12 = (bf16[2,64,2080]{2,1,0:T(8,128)(2,1)S(1)}, bf16[2,64,2080]{2,1,0:T(8,128)(2,1)S(1)}, u32[]{:S(2)}, u32[]{:S(2)}) collective-permute-start(bf16[2,64,2080]{2,1,0:T(8,128)(2,1)S(1)} %bitcast.78), channel_id=1, source_target_pairs={{0,2},{2,4},{4,6},{6,0},{1,3},{3,5},{5,7},{7,1},{8,10},{10,12},{12... | collective-permute-start | bytes 1597448 | tf_op jit(solution)/shard_map/ppermute | solution.py:284
  51.2 15.0 %copy-start.23 = (bf16[384,768]{1,0:T(8,128)(2,1)}, bf16[384,768]{1,0:T(8,128)(2,1)S(1)}, u32[]{:S(2)}) copy-start(bf16[384,768]{1,0:T(8,128)(2,1)S(1)} %get-tuple-element.56.refs_8_) | copy-start | bytes 1769476
  51.2 15.0 %copy-start.24 = (bf16[384,768]{1,0:T(8,128)(2,1)}, bf16[384,768]{1,0:T(8,128)(2,1)S(1)}, u32[]{:S(2)}) copy-start(bf16[384,768]{1,0:T(8,128)(2,1)S(1)} %get-tuple-element.53.refs_8_) | copy-start | bytes 1769476
  51.2 17.1 %copy-start.17 = (bf16[128,2080]{1,0:T(8,128)(2,1)}, bf16[128,2080]{1,0:T(8,128)(2,1)S(1)}, u32[]{:S(2)}) copy-start(bf16[128,2080]{1,0:T(8,128)(2,1)S(1)} %get-tuple-element.32.refs_0_) | copy-start | bytes 1597444
  51.2 14.9 %collective-permute-start.7 = (bf16[1,64,2080]{2,1,0:T(8,128)(2,1)S(1)}, bf16[1,64,2080]{2,1,0:T(8,128)(2,1)S(1)}, u32[]{:S(2)}, u32[]{:S(2)}) collective-permute-start(bf16[1,64,2080]{2,1,0:T(8,128)(2,1)S(1)} %bitcast.148), channel_id=1, source_target_pairs={{0,2},{2,4},{4,6},{6,0},{1,3},{3,5},{5,7},{7,1},{8,10},{10,12},{12... | collective-permute-start | bytes 798728 | tf_op jit(solution)/shard_map/ppermute | solution.py:284
  51.4 19.1 %collective-permute-start.14 = (bf16[2,64,2080]{2,1,0:T(8,128)(2,1)S(1)}, bf16[2,64,2080]{2,1,0:T(8,128)(2,1)S(1)}, u32[]{:S(2)}, u32[]{:S(2)}) collective-permute-start(bf16[2,64,2080]{2,1,0:T(8,128)(2,1)S(1)} %collective-permute-done), channel_id=1, source_target_pairs={{0,1},{1,0},{2,3},{3,2},{4,5},{5,4},{6,7},{7,6},{8,9},{9,8},{10,11... | collective-permute-start | bytes 1597448 | tf_op jit(solution)/shard_map/ppermute | solution.py:284
  51.4 23.6 %collective-permute-start.15 = (bf16[2,64,2080]{2,1,0:T(8,128)(2,1)S(1)}, bf16[2,64,2080]{2,1,0:T(8,128)(2,1)S(1)}, u32[]{:S(2)}, u32[]{:S(2)}) collective-permute-start(bf16[2,64,2080]{2,1,0:T(8,128)(2,1)S(1)} %collective-permute-done.2), channel_id=1, source_target_pairs={{0,1},{1,0},{2,3},{3,2},{4,5},{5,4},{6,7},{7,6},{8,9},{9,8},{10,11... | collective-permute-start | bytes 1597448 | tf_op jit(solution)/shard_map/ppermute | solution.py:284
  57.8 10.6 %copy-start.11 = (bf16[2,64,2080]{2,1,0:T(8,128)(2,1)}, bf16[2,64,2080]{2,1,0:T(8,128)(2,1)S(1)}, u32[]{:S(2)}) copy-start(bf16[2,64,2080]{2,1,0:T(8,128)(2,1)S(1)} %collective-permute-done.6) | copy-start | bytes 1597444
  57.8 8.4 %collective-permute-start.8 = (bf16[1,64,2080]{2,1,0:T(8,128)(2,1)S(1)}, bf16[1,64,2080]{2,1,0:T(8,128)(2,1)S(1)}, u32[]{:S(2)}, u32[]{:S(2)}) collective-permute-start(bf16[1,64,2080]{2,1,0:T(8,128)(2,1)S(1)} %bitcast.144), channel_id=1, source_target_pairs={{0,6},{2,0},{4,2},{6,4},{1,7},{3,1},{5,3},{7,5},{8,14},{10,8},{12,... | collective-permute-start | bytes 798728 | tf_op jit(solution)/shard_map/ppermute | solution.py:284
  60.4 29.2 %copy-start.3 = (bf16[128,2080]{1,0:T(8,128)(2,1)}, bf16[128,2080]{1,0:T(8,128)(2,1)S(1)}, u32[]{:S(2)}) copy-start(bf16[128,2080]{1,0:T(8,128)(2,1)S(1)} %after.6.refs_1_.refs_2_.refs_5_) | copy-start | bytes 1597444
  60.4 29.2 %copy-start.4 = (bf16[128,2080]{1,0:T(8,128)(2,1)}, bf16[128,2080]{1,0:T(8,128)(2,1)S(1)}, u32[]{:S(2)}) copy-start(bf16[128,2080]{1,0:T(8,128)(2,1)S(1)} %after.7.refs_1_.refs_4_) | copy-start | bytes 1597444
  60.4 17.7 %collective-permute-start.13 = (bf16[2,64,2080]{2,1,0:T(8,128)(2,1)S(1)}, bf16[2,64,2080]{2,1,0:T(8,128)(2,1)S(1)}, u32[]{:S(2)}, u32[]{:S(2)}) collective-permute-start(bf16[2,64,2080]{2,1,0:T(8,128)(2,1)S(1)} %bitcast.76), channel_id=1, source_target_pairs={{0,2},{2,4},{4,6},{6,0},{1,3},{3,5},{5,7},{7,1},{8,10},{10,12},{12... | collective-permute-start | bytes 1597448 | tf_op jit(solution)/shard_map/ppermute | solution.py:284
  66.1 11.9 %collective-permute-start.16 = (bf16[2,64,2080]{2,1,0:T(8,128)(2,1)S(1)}, bf16[2,64,2080]{2,1,0:T(8,128)(2,1)S(1)}, u32[]{:S(2)}, u32[]{:S(2)}) collective-permute-start(bf16[2,64,2080]{2,1,0:T(8,128)(2,1)S(1)} %bitcast.79), channel_id=1, source_target_pairs={{0,6},{2,0},{4,2},{6,4},{1,7},{3,1},{5,3},{7,5},{8,14},{10,8},{12,... | collective-permute-start | bytes 1597448 | tf_op jit(solution)/shard_map/ppermute | solution.py:284
  68.3 0.7 copy-start.28
  69.0 10.8 %copy-start.27 = (bf16[128,768]{1,0:T(8,128)(2,1)}, bf16[128,768]{1,0:T(8,128)(2,1)S(1)}, u32[]{:S(2)}) copy-start(bf16[128,768]{1,0:T(8,128)(2,1)S(1)} %get-tuple-element.57.refs_9_) | copy-start | bytes 589828
  69.0 15.0 %collective-permute-start.9 = (bf16[1,64,2080]{2,1,0:T(8,128)(2,1)S(1)}, bf16[1,64,2080]{2,1,0:T(8,128)(2,1)S(1)}, u32[]{:S(2)}, u32[]{:S(2)}) collective-permute-start(bf16[1,64,2080]{2,1,0:T(8,128)(2,1)S(1)} %bitcast.147), channel_id=1, source_target_pairs={{0,2},{2,4},{4,6},{6,0},{1,3},{3,5},{5,7},{7,1},{8,10},{10,12},{12... | collective-permute-start | bytes 798728 | tf_op jit(solution)/shard_map/ppermute | solution.py:284
  70.5 7.6 %copy-start.15 = (bf16[2,64,2080]{2,1,0:T(8,128)(2,1)}, bf16[2,64,2080]{2,1,0:T(8,128)(2,1)S(1)}, u32[]{:S(2)}) copy-start(bf16[2,64,2080]{2,1,0:T(8,128)(2,1)S(1)} %collective-permute-done.14) | copy-start | bytes 1597444
  70.5 13.6 %collective-permute-start.10 = (bf16[1,64,2080]{2,1,0:T(8,128)(2,1)S(1)}, bf16[1,64,2080]{2,1,0:T(8,128)(2,1)S(1)}, u32[]{:S(2)}, u32[]{:S(2)}) collective-permute-start(bf16[1,64,2080]{2,1,0:T(8,128)(2,1)S(1)} %bitcast.145), channel_id=1, source_target_pairs={{0,6},{2,0},{4,2},{6,4},{1,7},{3,1},{5,3},{7,5},{8,14},{10,8},{12,... | collective-permute-start | bytes 798728 | tf_op jit(solution)/shard_map/ppermute | solution.py:284
  75.0 4.8 %copy-start.16 = (bf16[2,64,2080]{2,1,0:T(8,128)(2,1)}, bf16[2,64,2080]{2,1,0:T(8,128)(2,1)S(1)}, u32[]{:S(2)}) copy-start(bf16[2,64,2080]{2,1,0:T(8,128)(2,1)S(1)} %collective-permute-done.15) | copy-start | bytes 1597444
  75.0 14.6 %collective-permute-start.19 = (bf16[2,64,2080]{2,1,0:T(8,128)(2,1)S(1)}, bf16[2,64,2080]{2,1,0:T(8,128)(2,1)S(1)}, u32[]{:S(2)}, u32[]{:S(2)}) collective-permute-start(bf16[2,64,2080]{2,1,0:T(8,128)(2,1)S(1)} %collective-permute-done.1), channel_id=1, source_target_pairs={{0,1},{1,0},{2,3},{3,2},{4,5},{5,4},{6,7},{7,6},{8,9},{9,8},{10,11... | collective-permute-start | bytes 1597448 | tf_op jit(solution)/shard_map/ppermute | solution.py:284
  76.8 3.0 %copy-start.26 = (bf16[256,768]{1,0:T(8,128)(2,1)}, bf16[256,768]{1,0:T(8,128)(2,1)S(1)}, u32[]{:S(2)}) copy-start(bf16[256,768]{1,0:T(8,128)(2,1)S(1)} %get-tuple-element.58.refs_10_) | copy-start | bytes 1179652
  76.8 3.0 %copy-start.29 = (bf16[128,768]{1,0:T(8,128)(2,1)}, bf16[128,768]{1,0:T(8,128)(2,1)S(1)}, u32[]{:S(2)}) copy-start(bf16[128,768]{1,0:T(8,128)(2,1)S(1)} %get-tuple-element.60.refs_12_) | copy-start | bytes 589828
  78.1 1.8 %copy-start.20 = (bf16[2,64,2080]{2,1,0:T(8,128)(2,1)}, bf16[2,64,2080]{2,1,0:T(8,128)(2,1)S(1)}, u32[]{:S(2)}) copy-start(bf16[2,64,2080]{2,1,0:T(8,128)(2,1)S(1)} %collective-permute-done.13) | copy-start | bytes 1597444
  78.1 11.5 %copy-start.10 = (bf16[2,64,2080]{2,1,0:T(8,128)(2,1)}, bf16[2,64,2080]{2,1,0:T(8,128)(2,1)S(1)}, u32[]{:S(2)}) copy-start(bf16[2,64,2080]{2,1,0:T(8,128)(2,1)S(1)} %collective-permute-done.16) | copy-start | bytes 1597444
  79.9 14.6 %copy-start.12 = (bf16[128,768]{1,0:T(8,128)(2,1)}, bf16[128,768]{1,0:T(8,128)(2,1)S(1)}, u32[]{:S(2)}) copy-start(bf16[128,768]{1,0:T(8,128)(2,1)S(1)} %get-tuple-element.40.refs_4_.refs_7_.refs_11_) | copy-start | bytes 589828
  84.2 10.4 %collective-permute-start.17 = (bf16[1,64,2080]{2,1,0:T(8,128)(2,1)S(1)}, bf16[1,64,2080]{2,1,0:T(8,128)(2,1)S(1)}, u32[]{:S(2)}, u32[]{:S(2)}) collective-permute-start(bf16[1,64,2080]{2,1,0:T(8,128)(2,1)S(1)} %bitcast.146), channel_id=1, source_target_pairs={{0,2},{2,4},{4,6},{6,0},{1,3},{3,5},{5,7},{7,1},{8,10},{10,12},{12... | collective-permute-start | bytes 798728 | tf_op jit(solution)/shard_map/ppermute | solution.py:284
  84.3 13.0 %collective-permute-start.18 = (bf16[1,64,2080]{2,1,0:T(8,128)(2,1)S(1)}, bf16[1,64,2080]{2,1,0:T(8,128)(2,1)S(1)}, u32[]{:S(2)}, u32[]{:S(2)}) collective-permute-start(bf16[1,64,2080]{2,1,0:T(8,128)(2,1)S(1)} %bitcast.143), channel_id=1, source_target_pairs={{0,6},{2,0},{4,2},{6,4},{1,7},{3,1},{5,3},{7,5},{8,14},{10,8},{12,... | collective-permute-start | bytes 798728 | tf_op jit(solution)/shard_map/ppermute | solution.py:284
  86.9 10.4 %collective-permute-start.20 = (bf16[1,64,2080]{2,1,0:T(8,128)(2,1)S(1)}, bf16[1,64,2080]{2,1,0:T(8,128)(2,1)S(1)}, u32[]{:S(2)}, u32[]{:S(2)}) collective-permute-start(bf16[1,64,2080]{2,1,0:T(8,128)(2,1)S(1)} %bitcast.142), channel_id=1, source_target_pairs={{0,2},{2,4},{4,6},{6,0},{1,3},{3,5},{5,7},{7,1},{8,10},{10,12},{12... | collective-permute-start | bytes 798728 | tf_op jit(solution)/shard_map/ppermute | solution.py:284
  86.9 10.4 %collective-permute-start.21 = (bf16[1,64,2080]{2,1,0:T(8,128)(2,1)S(1)}, bf16[1,64,2080]{2,1,0:T(8,128)(2,1)S(1)}, u32[]{:S(2)}, u32[]{:S(2)}) collective-permute-start(bf16[1,64,2080]{2,1,0:T(8,128)(2,1)S(1)} %bitcast.141), channel_id=1, source_target_pairs={{0,6},{2,0},{4,2},{6,4},{1,7},{3,1},{5,3},{7,5},{8,14},{10,8},{12,... | collective-permute-start | bytes 798728 | tf_op jit(solution)/shard_map/ppermute | solution.py:284
  89.6 4.9 %copy-start.19 = (bf16[2,64,2080]{2,1,0:T(8,128)(2,1)}, bf16[2,64,2080]{2,1,0:T(8,128)(2,1)S(1)}, u32[]{:S(2)}) copy-start(bf16[2,64,2080]{2,1,0:T(8,128)(2,1)S(1)} %collective-permute-done.19) | copy-start | bytes 1597444
  89.6 19.1 %copy-start.18 = (bf16[128,2080]{1,0:T(8,128)(2,1)S(1)}, bf16[128,2080]{1,0:T(8,128)(2,1)}, u32[]{:S(2)}) copy-start(bf16[128,2080]{1,0:T(8,128)(2,1)} %copy-done.17) | copy-start | bytes 1597444
  94.5 3.6 %copy-start.25 = (bf16[384,768]{1,0:T(8,128)(2,1)}, bf16[384,768]{1,0:T(8,128)(2,1)S(1)}, u32[]{:S(2)}) copy-start(bf16[384,768]{1,0:T(8,128)(2,1)S(1)} %get-tuple-element.55.refs_10_) | copy-start | bytes 1769476
  94.5 3.6 %copy-start.30 = (bf16[128,768]{1,0:T(8,128)(2,1)}, bf16[128,768]{1,0:T(8,128)(2,1)S(1)}, u32[]{:S(2)}) copy-start(bf16[128,768]{1,0:T(8,128)(2,1)S(1)} %get-tuple-element.59.refs_11_) | copy-start | bytes 589828
  94.5 8.3 %collective-permute-start.23 = (bf16[1,64,2080]{2,1,0:T(8,128)(2,1)}, bf16[1,64,2080]{2,1,0:T(8,128)(2,1)S(1)}, u32[]{:S(2)}, u32[]{:S(2)}) collective-permute-start(bf16[1,64,2080]{2,1,0:T(8,128)(2,1)} %bitcast.49), channel_id=1, source_target_pairs={{0,2},{2,4},{4,6},{6,0},{1,3},{3,5},{5,7},{7,1},{8,10},{10,12},{12... | collective-permute-start | bytes 798728 | tf_op jit(solution)/shard_map/ppermute | solution.py:284
  94.6 8.2 %collective-permute-start.24 = (bf16[1,64,2080]{2,1,0:T(8,128)(2,1)}, bf16[1,64,2080]{2,1,0:T(8,128)(2,1)S(1)}, u32[]{:S(2)}, u32[]{:S(2)}) collective-permute-start(bf16[1,64,2080]{2,1,0:T(8,128)(2,1)} %bitcast.51), channel_id=1, source_target_pairs={{0,6},{2,0},{4,2},{6,4},{1,7},{3,1},{5,3},{7,5},{8,14},{10,8},{12,... | collective-permute-start | bytes 798728 | tf_op jit(solution)/shard_map/ppermute | solution.py:284
  98.2 10.5 %collective-permute-start.22 = (bf16[1,64,2080]{2,1,0:T(8,128)(2,1)}, bf16[1,64,2080]{2,1,0:T(8,128)(2,1)S(1)}, u32[]{:S(2)}, u32[]{:S(2)}) collective-permute-start(bf16[1,64,2080]{2,1,0:T(8,128)(2,1)} %bitcast.47), channel_id=1, source_target_pairs={{0,2},{2,4},{4,6},{6,0},{1,3},{3,5},{5,7},{7,1},{8,10},{10,12},{12... | collective-permute-start | bytes 798728 | tf_op jit(solution)/shard_map/ppermute | solution.py:284
  98.2 10.5 %collective-permute-start.25 = (bf16[1,64,2080]{2,1,0:T(8,128)(2,1)}, bf16[1,64,2080]{2,1,0:T(8,128)(2,1)S(1)}, u32[]{:S(2)}, u32[]{:S(2)}) collective-permute-start(bf16[1,64,2080]{2,1,0:T(8,128)(2,1)} %bitcast.53), channel_id=1, source_target_pairs={{0,6},{2,0},{4,2},{6,4},{1,7},{3,1},{5,3},{7,5},{8,14},{10,8},{12,... | collective-permute-start | bytes 798728 | tf_op jit(solution)/shard_map/ppermute | solution.py:284
  110.1 27.2 %all-to-all-start.1 = ((bf16[32,8,2080]{2,1,0:T(8,128)(2,1)}), bf16[32,8,2080]{2,1,0:T(8,128)(2,1)S(1)}, u32[]{:S(2)}, u32[]{:S(2)}) async-start(bf16[32,8,2080]{2,1,0:T(8,128)(2,1)} %bitcast.55), calls=%async_computation.1 | async-start | bytes 2228224 | tf_op jit(solution)/shard_map/all_to_all | solution.py:305
  127.5 9.8 %copy-start.21 = (s32[128]{0:T(128)S(1)}, s32[128]{0:T(128)}, u32[]{:S(2)}) copy-start(s32[128]{0:T(128)} %param.8) | copy-start | bytes 1540
  127.5 9.8 %copy-start.22 = (s32[128]{0:T(128)S(1)}, s32[128]{0:T(128)}, u32[]{:S(2)}) copy-start(s32[128]{0:T(128)} %param.9) | copy-start | bytes 1540

commit v6 on v5

--- a/solution.py
+++ b/solution.py
@@ -183,28 +183,33 @@
     )(value, *others)
 
 
-def total_kernel(z_ref, *refs):
-    out_ref = refs[-1]
-    for i, start in enumerate((z_ref[0] * 128, (1 - z_ref[0]) * 128)):
-        own, *halves = refs[5 * i : 5 * i + 5]
-        for half in range(2):
-            value = own[pl.ds(half * 64, 64), :].astype(F32)
-            for ref in halves[half::2]:
-                value = value + ref[...].astype(F32)
-            out_ref[pl.ds(pl.multiple_of(start + half * 64, 64), 64), :] = value.astype(BF)
+def sum_kernel(own, lft0, lft1, rgt0, rgt1, out_ref):
+    for half, (lft, rgt) in enumerate(((lft0, rgt0), (lft1, rgt1))):
+        at = pl.ds(half * 64, 64)
+        value = own[at, :].astype(F32) + lft[...].astype(F32) + rgt[...].astype(F32)
+        out_ref[at, :] = value.astype(BF)
+
+
+def total_kernel(z_ref, near, own, lft0, lft1, rgt0, rgt1, out_ref):
+    out_ref[pl.ds(pl.multiple_of(z_ref[0] * 128, 128), 128), :] = near[...]
+    for half, (lft, rgt) in enumerate(((lft0, rgt0), (lft1, rgt1))):
+        value = own[pl.ds(half * 64, 64), :].astype(F32) + lft[...].astype(F32) + rgt[...].astype(F32)
+        start = pl.multiple_of((1 - z_ref[0]) * 128 + half * 64, 64)
+        out_ref[pl.ds(start, 64), :] = value.astype(BF)
 
 
 def total(z, near, far):
     width = near[0].shape[1]
+    near = call(sum_kernel, (((128, width), BF),), near, "near_sum")[0]
     return pl.pallas_call(
         total_kernel,
         out_shape=jax.ShapeDtypeStruct((256, width), BF),
-        in_specs=[SMEM] + [VMEM] * 10,
+        in_specs=[SMEM] + [VMEM] * 6,
         out_specs=VMEM,
         compiler_params=PARAMS,
         cost_estimate=pl.CostEstimate(flops=0, bytes_accessed=0, transcendentals=0),
         name="total",
-    )(z, *near, *far)
+    )(z, near, *far)
 
 
 def finish_kernel(back_ref, expert_ref, slot_ref, out_ref):

time: 139 us -> 139 us (level)
    pallas_call x8 -> x9, Pallas kernels: 17.1 us -> 17.3 us  [call(): pl.pallas_call(ordered, out_shape=tuple((jax.ShapeDtypeStruct(s, d) for s...]
where the time goes in v6:
time: 139 us; the launch traced here: 138 us
  Pallas kernels  39.7 us (29%)
  waiting for transfers between devices  39.2 us (28%)
  starting transfers between devices  35.5 us (26%)
  blocking collectives  21.9 us (16%)
    ppermute x26, waiting for transfers between devices, move(): return lax.ppermute(blocks, axis, pairs).reshape(value.shape)  39.2 us
    ppermute x26, starting transfers between devices, move(): return lax.ppermute(blocks, axis, pairs).reshape(value.shape)  27.9 us
    all_to_all x1, blocking collectives, exchange(): lax.all_to_all(blocks, axes, split_axis=0, concat_axis=0, tiled=True)  21.9 us
    pallas_call x2, Pallas kernels, weights(): pl.pallas_call(weights_kernel, out_shape=pltpu.HBM((width, units), BF), i...  19.5 us
    pallas_call x9, Pallas kernels, call(): pl.pallas_call(ordered, out_shape=tuple((jax.ShapeDtypeStruct(s, d) for s...  17.3 us
    all_to_all x1, starting transfers between devices, exchange(): lax.all_to_all(blocks, axes, split_axis=0, concat_axis=0, tiled=True)  7.6 us
  transfers between devices with their start and end apart: 27, of which 8 were waited for; matrix products, arithmetic and copies ran while one was open for 0% of the time, Pallas kernels for 27%

profile of v6, /device:TPU:1, one launch (start us, length us, event | category | flops | bytes accessed | tf_op | source)
XLA Modules:
  0.0 138.3 jit_solution(3652694047687689885)
XLA Ops:
  0.6 2.1 %collective-permute-start = (bf16[2,64,2080]{2,1,0:T(8,128)(2,1)}, bf16[2,64,2080]{2,1,0:T(8,128)(2,1)S(1)}, u32[]{:S(2)}, u32[]{:S(2)}) collective-permute-start(bf16[2,64,2080]{2,1,0:T(8,128)(2,1)} %bitcast.113), channel_id=1, source_target_pairs={{0,2},{2,4},{4,6},{6,0},{1,3},{3,5},{5,7},{7,1},{8,10},{10,12},{12... | collective-permute-start | bytes 1597448 | tf_op jit(solution)/shard_map/ppermute | solution.py:289
  2.7 1.4 collective-permute-start.1
  4.1 1.6 %collective-permute-start.2 = (bf16[2,64,2080]{2,1,0:T(8,128)(2,1)}, bf16[2,64,2080]{2,1,0:T(8,128)(2,1)S(1)}, u32[]{:S(2)}, u32[]{:S(2)}) collective-permute-start(bf16[2,64,2080]{2,1,0:T(8,128)(2,1)} %bitcast.115), channel_id=1, source_target_pairs={{0,4},{2,6},{4,0},{6,2},{1,5},{3,7},{5,1},{7,3},{8,12},{10,14},{12... | collective-permute-start | bytes 1597448 | tf_op jit(solution)/shard_map/ppermute | solution.py:289
  5.7 1.6 %collective-permute-start.3 = (bf16[2,64,2080]{2,1,0:T(8,128)(2,1)}, bf16[2,64,2080]{2,1,0:T(8,128)(2,1)S(1)}, u32[]{:S(2)}, u32[]{:S(2)}) collective-permute-start(bf16[2,64,2080]{2,1,0:T(8,128)(2,1)} %bitcast.116), channel_id=1, source_target_pairs={{0,1},{1,0},{2,3},{3,2},{4,5},{5,4},{6,7},{7,6},{8,9},{9,8},{10,11... | collective-permute-start | bytes 1597448 | tf_op jit(solution)/shard_map/ppermute | solution.py:289
  7.4 1.6 %prepare.1 = bf16[128,2080]{1,0:T(8,128)(2,1)S(1)} custom-call(bf16[2080,128]{1,0:T(8,128)(2,1)} %bitcast.149, s32[1,128]{1,0:T(1,128)} %bitcast.137, s32[1,128]{1,0:T(1,128)} %bitcast.139, f32[1,128]{1,0:T(1,128)} %bitcast.151), custom_call_target="tpu_custom_call" | custom-call | flops 68157440 | bytes 2129920 | tf_op jit(solution)/shard_map/prepare/pallas_call | solution.py:70
  8.9 0.0 copy-start
  9.0 0.0 copy-start.13
  9.0 21.9 %all_to_all.10 = bf16[16,8,2080]{2,1,0:T(8,128)(2,1)S(1)} all-to-all(bf16[16,8,2080]{2,1,0:T(8,128)(2,1)S(1)} %bitcast.99), channel_id=1, replica_groups=mesh['y'=4,'zh'=2,'core'=2,'x'=4,'zl'=2] {'y','zh','core'}, dimensions={0} | all-to-all | bytes 1064960 | tf_op jit(solution)/shard_map/all_to_all | solution.py:310
  30.9 0.0 collective-permute-done
  30.9 0.0 collective-permute-done.1
  30.9 0.0 collective-permute-done.3
  31.0 0.9 collective-permute-start.5
  31.9 0.6 collective-permute-start.4
  32.5 0.0 collective-permute-start.11
  32.6 12.3 %collective-permute-done.5 = bf16[2,64,2080]{2,1,0:T(8,128)(2,1)S(1)} collective-permute-done((bf16[2,64,2080]{2,1,0:T(8,128)(2,1)S(1)}, bf16[2,64,2080]{2,1,0:T(8,128)(2,1)S(1)}, u32[]{:S(2)}, u32[]{:S(2)}) %collective-permute-start.5) | collective-permute-done | bytes 532512 | tf_op jit(solution)/shard_map/ppermute | solution.py:289
  44.9 1.7 %collective-permute-start.6 = (bf16[2,64,2080]{2,1,0:T(8,128)(2,1)S(1)}, bf16[2,64,2080]{2,1,0:T(8,128)(2,1)S(1)}, u32[]{:S(2)}, u32[]{:S(2)}) collective-permute-start(bf16[2,64,2080]{2,1,0:T(8,128)(2,1)S(1)} %collective-permute-done.5), channel_id=1, source_target_pairs={{0,6},{2,0},{4,2},{6,4},{1,7},{3,1},{5,3},{7,5},{8,14},{10,8},{12,... | collective-permute-start | bytes 1597448 | tf_op jit(solution)/shard_map/ppermute | solution.py:289
  46.6 0.0 collective-permute-done.11
  46.6 0.1 collective-permute-start.12
  46.7 4.4 %layer.2 = (bf16[384,768]{1,0:T(8,128)(2,1)S(1)}, bf16[384,768]{1,0:T(8,128)(2,1)S(1)}, bf16[128,2080]{1,0:T(8,128)(2,1)S(1)}, bf16[64,2080]{1,0:T(8,128)(2,1)S(...) custom-call(bf16[128,2080]{1,0:T(8,128)(2,1)S(1)} %bitcast.118, ...), custom_call_target="tpu_custom_call" | custom-call | bytes 4194304 | tf_op jit(solution)/shard_map/layer/pallas_call | solution.py:34
  51.2 0.0 copy-start.24
  51.2 0.0 copy-start.18
  51.2 0.2 collective-permute-start.7
  51.4 0.0 collective-permute-start.14
  51.4 1.5 %collective-permute-start.15 = (bf16[2,64,2080]{2,1,0:T(8,128)(2,1)S(1)}, bf16[2,64,2080]{2,1,0:T(8,128)(2,1)S(1)}, u32[]{:S(2)}, u32[]{:S(2)}) collective-permute-start(bf16[2,64,2080]{2,1,0:T(8,128)(2,1)S(1)} %collective-permute-done.2), channel_id=1, source_target_pairs={{0,1},{1,0},{2,3},{3,2},{4,5},{5,4},{6,7},{7,6},{8,9},{9,8},{10,11... | collective-permute-start | bytes 1597448 | tf_op jit(solution)/shard_map/ppermute | solution.py:289
  52.9 4.9 %collective-permute-done.6 = bf16[2,64,2080]{2,1,0:T(8,128)(2,1)S(1)} collective-permute-done((bf16[2,64,2080]{2,1,0:T(8,128)(2,1)S(1)}, bf16[2,64,2080]{2,1,0:T(8,128)(2,1)S(1)}, u32[]{:S(2)}, u32[]{:S(2)}) %collective-permute-start.6) | collective-permute-done | bytes 532512 | tf_op jit(solution)/shard_map/ppermute | solution.py:289
  57.8 2.6 %collective-permute-start.8 = (bf16[1,64,2080]{2,1,0:T(8,128)(2,1)S(1)}, bf16[1,64,2080]{2,1,0:T(8,128)(2,1)S(1)}, u32[]{:S(2)}, u32[]{:S(2)}) collective-permute-start(bf16[1,64,2080]{2,1,0:T(8,128)(2,1)S(1)} %bitcast.144), channel_id=1, source_target_pairs={{0,6},{2,0},{4,2},{6,4},{1,7},{3,1},{5,3},{7,5},{8,14},{10,8},{12,... | collective-permute-start | bytes 798728 | tf_op jit(solution)/shard_map/ppermute | solution.py:289
  60.4 0.0 collective-permute-done.12
  60.4 0.1 collective-permute-start.13
  60.5 5.7 %collective-permute-done.7 = bf16[1,64,2080]{2,1,0:T(8,128)(2,1)S(1)} collective-permute-done((bf16[1,64,2080]{2,1,0:T(8,128)(2,1)S(1)}, bf16[1,64,2080]{2,1,0:T(8,128)(2,1)S(1)}, u32[]{:S(2)}, u32[]{:S(2)}) %collective-permute-start.7) | collective-permute-done | bytes 266272 | tf_op jit(solution)/shard_map/ppermute | solution.py:289
  66.1 0.0 collective-permute-start.16
  66.1 0.0 collective-permute-done.8
  66.2 2.2 %layer.3 = (bf16[128,768]{1,0:T(8,128)(2,1)S(1)}, bf16[128,768]{1,0:T(8,128)(2,1)S(1)}, bf16[64,2080]{1,0:T(8,128)(2,1)S(1)}, bf16[64,2080]{1,0:T(8,128)(2,1)S(1)}) custom-call(bf16[128,2080]{1,0:T(8,128)(2,1)S(1)} %bitcast.101, bf16[128,2080]{1,0:T(8,128)(2,1)S(1)} %bitcast.107, bf16[2080,768]{1,0:T(8,128)(2,1)S(1)} %bitcast.63, ...), custom_call_target="tpu_custom_call" | custom-call | bytes 4194304 | tf_op jit(solution)/shard_map/layer/pallas_call | solution.py:34
  68.4 0.7 copy-done.28
  69.0 1.5 %collective-permute-start.9 = (bf16[1,64,2080]{2,1,0:T(8,128)(2,1)S(1)}, bf16[1,64,2080]{2,1,0:T(8,128)(2,1)S(1)}, u32[]{:S(2)}, u32[]{:S(2)}) collective-permute-start(bf16[1,64,2080]{2,1,0:T(8,128)(2,1)S(1)} %bitcast.147), channel_id=1, source_target_pairs={{0,2},{2,4},{4,6},{6,0},{1,3},{3,5},{5,7},{7,1},{8,10},{10,12},{12... | collective-permute-start | bytes 798728 | tf_op jit(solution)/shard_map/ppermute | solution.py:289
  70.5 1.2 collective-permute-start.10
  71.7 3.3 %collective-permute-done.15 = bf16[2,64,2080]{2,1,0:T(8,128)(2,1)S(1)} collective-permute-done((bf16[2,64,2080]{2,1,0:T(8,128)(2,1)S(1)}, bf16[2,64,2080]{2,1,0:T(8,128)(2,1)S(1)}, u32[]{:S(2)}, u32[]{:S(2)}) %collective-permute-start.15) | collective-permute-done | bytes 532512 | tf_op jit(solution)/shard_map/ppermute | solution.py:289
  75.0 0.0 collective-permute-start.19
  75.1 1.8 %forward.1 = (bf16[256,768]{1,0:T(8,128)(2,1)S(1)}, bf16[128,768]{1,0:T(8,128)(2,1)S(1)}, f32[256,768]{1,0:T(8,128)S(1)}, f32[128,768]{1,0:T(8,128)S(1)}) custom-call(bf16[128,2080]{1,0:T(8,128)(2,1)S(1)} %bitcast.94, bf16[128,2080]{1,0:T(8,128)(2,1)S(1)} %bitcast.121, bf16[128,2080]{1,0:T(8,128)(2,1)S(1)} %bitcast.123, bf16[2080,768]{1,0:T(8,128)(2,1)S(1)} %bitcast.64), custom_call_target="tpu_custom_call" | custom-call | bytes 4194304 | tf_op jit(solution)/shard_map/forward/pallas_call | solution.py:34
  76.8 0.0 copy-start.26
  76.9 1.2 collective-permute-done.13
  78.1 0.0 collective-permute-done.16
  78.1 1.8 %far_layer.1 = (bf16[128,768]{1,0:T(8,128)(2,1)S(1)}, bf16[64,2080]{1,0:T(8,128)(2,1)S(1)}, bf16[64,2080]{1,0:T(8,128)(2,1)S(1)}) custom-call(bf16[128,2080]{1,0:T(8,128)(2,1)S(1)} %bitcast.127, f32[128,768]{1,0:T(8,128)S(1)} %get-tuple-element.39.refs_1_, bf16[2080,768]{1,0:T(8,128)(2,1)S(1)} %bitcast.65, bf16[2080,768]{1,0:T(8,128)(2,1)S(1)} %bitcast.69, ...), custom_call_target="tpu_custom_call" | custom-call | bytes 4194304 | tf_op jit(solution)/shard_map/far_layer/pallas_call | solution.py:34
  79.9 4.1 %collective-permute-done.9 = bf16[1,64,2080]{2,1,0:T(8,128)(2,1)S(1)} collective-permute-done((bf16[1,64,2080]{2,1,0:T(8,128)(2,1)S(1)}, bf16[1,64,2080]{2,1,0:T(8,128)(2,1)S(1)}, u32[]{:S(2)}, u32[]{:S(2)}) %collective-permute-start.9) | collective-permute-done | bytes 266272 | tf_op jit(solution)/shard_map/ppermute | solution.py:289
  84.0 0.0 collective-permute-done.10
  84.0 0.1 middle.2
  84.2 0.1 collective-permute-start.17
  84.3 2.7 %collective-permute-start.18 = (bf16[1,64,2080]{2,1,0:T(8,128)(2,1)S(1)}, bf16[1,64,2080]{2,1,0:T(8,128)(2,1)S(1)}, u32[]{:S(2)}, u32[]{:S(2)}) collective-permute-start(bf16[1,64,2080]{2,1,0:T(8,128)(2,1)S(1)} %bitcast.143), channel_id=1, source_target_pairs={{0,6},{2,0},{4,2},{6,4},{1,7},{3,1},{5,3},{7,5},{8,14},{10,8},{12,... | collective-permute-start | bytes 798728 | tf_op jit(solution)/shard_map/ppermute | solution.py:289
  86.9 2.7 %collective-permute-start.21 = (bf16[1,64,2080]{2,1,0:T(8,128)(2,1)S(1)}, bf16[1,64,2080]{2,1,0:T(8,128)(2,1)S(1)}, u32[]{:S(2)}, u32[]{:S(2)}) collective-permute-start(bf16[1,64,2080]{2,1,0:T(8,128)(2,1)S(1)} %bitcast.141), channel_id=1, source_target_pairs={{0,6},{2,0},{4,2},{6,4},{1,7},{3,1},{5,3},{7,5},{8,14},{10,8},{12,... | collective-permute-start | bytes 798728 | tf_op jit(solution)/shard_map/ppermute | solution.py:289
  89.6 0.0 copy-start.19
  89.6 4.9 %rest_layer.1 = (bf16[128,768]{1,0:T(8,128)(2,1)S(1)}, bf16[384,768]{1,0:T(8,128)(2,1)S(1)}, bf16[128,2080]{1,0:T(8,128)(2,1)S(1)}, bf16[64,2080]{1,0:T(8,128)(2...) custom-call(bf16[128,2080]{1,0:T(8,128)(2,1)S(1)} %bitcast.125, ...), custom_call_target="tpu_custom_call" | custom-call | bytes 4194304 | tf_op jit(solution)/shard_map/rest_layer/pallas_call | solution.py:34
  94.5 0.1 collective-permute-start.23
  94.6 2.7 %collective-permute-start.24 = (bf16[1,64,2080]{2,1,0:T(8,128)(2,1)}, bf16[1,64,2080]{2,1,0:T(8,128)(2,1)S(1)}, u32[]{:S(2)}, u32[]{:S(2)}) collective-permute-start(bf16[1,64,2080]{2,1,0:T(8,128)(2,1)} %bitcast.51), channel_id=1, source_target_pairs={{0,6},{2,0},{4,2},{6,4},{1,7},{3,1},{5,3},{7,5},{8,14},{10,8},{12,... | collective-permute-start | bytes 798728 | tf_op jit(solution)/shard_map/ppermute | solution.py:289
  97.3 0.9 middle.3
  98.2 2.7 %collective-permute-start.25 = (bf16[1,64,2080]{2,1,0:T(8,128)(2,1)}, bf16[1,64,2080]{2,1,0:T(8,128)(2,1)S(1)}, u32[]{:S(2)}, u32[]{:S(2)}) collective-permute-start(bf16[1,64,2080]{2,1,0:T(8,128)(2,1)} %bitcast.53), channel_id=1, source_target_pairs={{0,6},{2,0},{4,2},{6,4},{1,7},{3,1},{5,3},{7,5},{8,14},{10,8},{12,... | collective-permute-start | bytes 798728 | tf_op jit(solution)/shard_map/ppermute | solution.py:289
  100.9 0.2 near_sum.1.near
  101.1 1.7 %collective-permute-done.23 = bf16[1,64,2080]{2,1,0:T(8,128)(2,1)S(1)} collective-permute-done((bf16[1,64,2080]{2,1,0:T(8,128)(2,1)}, bf16[1,64,2080]{2,1,0:T(8,128)(2,1)S(1)}, u32[]{:S(2)}, u32[]{:S(2)}) %collective-permute-start.23) | collective-permute-done | bytes 266272 | tf_op jit(solution)/shard_map/ppermute | solution.py:289
  102.8 5.9 %collective-permute-done.22 = bf16[1,64,2080]{2,1,0:T(8,128)(2,1)S(1)} collective-permute-done((bf16[1,64,2080]{2,1,0:T(8,128)(2,1)}, bf16[1,64,2080]{2,1,0:T(8,128)(2,1)S(1)}, u32[]{:S(2)}, u32[]{:S(2)}) %collective-permute-start.22) | collective-permute-done | bytes 266272 | tf_op jit(solution)/shard_map/ppermute | solution.py:289
  108.7 1.3 total.1
  110.0 7.6 %all-to-all-start.1 = ((bf16[32,8,2080]{2,1,0:T(8,128)(2,1)}), bf16[32,8,2080]{2,1,0:T(8,128)(2,1)S(1)}, u32[]{:S(2)}, u32[]{:S(2)}) async-start(bf16[32,8,2080]{2,1,0:T(8,128)(2,1)} %bitcast.55), calls=%async_computation.1 | async-start | bytes 2228224 | tf_op jit(solution)/shard_map/all_to_all | solution.py:310
  117.6 9.8 %weights.2 = bf16[2080,768]{1,0:T(8,128)(2,1)} custom-call(bf16[128,2080]{1,0:T(8,128)(2,1)} %bitcast.117, bf16[128,2080]{1,0:T(8,128)(2,1)} %bitcast.89, bf16[128,2080]{1,0:T(8,128)(2,1)} %bitcast.92, bf16[128,2080]{1,0:T(8,128)(2,1)} %bitcast.102, bf16[128,2080]{1,0:T(8,128)(2,1)} %bitcast.95, bf16[128,2080]{1,0:T(8,128)(2,1)} %bitcast.122, ...), custom_call_target="tpu_custom_call" | custom-call | flops 3271557120 | bytes 10485760 | tf_op jit(solution)/shard_map/weights/pallas_call | solution.py:266
  127.3 0.0 copy-start.21
  127.4 0.0 copy-start.22
  127.4 9.8 %weights.3 = bf16[2080,768]{1,0:T(8,128)(2,1)} custom-call(bf16[128,2080]{1,0:T(8,128)(2,1)} %copy-done.2, bf16[128,2080]{1,0:T(8,128)(2,1)} %bitcast.98, bf16[128,2080]{1,0:T(8,128)(2,1)} %bitcast.120, bf16[128,2080]{1,0:T(8,128)(2,1)} %bitcast.108, bf16[128,2080]{1,0:T(8,128)(2,1)} %copy-done.4, bf16[128,2080]{1,0:T(8,128)(2,1)} %copy-done.3, ...), custom_call_target="tpu_custom_call" | custom-call | flops 3271557120 | bytes 10485760 | tf_op jit(solution)/shard_map/weights/pallas_call | solution.py:266
  137.2 1.2 finish.1
  (70 shorter events, 0.1 us)
Async XLA Ops:
  0.6 30.3 %collective-permute-start = (bf16[2,64,2080]{2,1,0:T(8,128)(2,1)}, bf16[2,64,2080]{2,1,0:T(8,128)(2,1)S(1)}, u32[]{:S(2)}, u32[]{:S(2)}) collective-permute-start(bf16[2,64,2080]{2,1,0:T(8,128)(2,1)} %bitcast.113), channel_id=1, source_target_pairs={{0,2},{2,4},{4,6},{6,0},{1,3},{3,5},{5,7},{7,1},{8,10},{10,12},{12... | collective-permute-start | bytes 1597448 | tf_op jit(solution)/shard_map/ppermute | solution.py:289
  2.7 28.2 %collective-permute-start.1 = (bf16[2,64,2080]{2,1,0:T(8,128)(2,1)}, bf16[2,64,2080]{2,1,0:T(8,128)(2,1)S(1)}, u32[]{:S(2)}, u32[]{:S(2)}) collective-permute-start(bf16[2,64,2080]{2,1,0:T(8,128)(2,1)} %bitcast.114), channel_id=1, source_target_pairs={{0,6},{2,0},{4,2},{6,4},{1,7},{3,1},{5,3},{7,5},{8,14},{10,8},{12,... | collective-permute-start | bytes 1597448 | tf_op jit(solution)/shard_map/ppermute | solution.py:289
  4.1 26.8 %collective-permute-start.2 = (bf16[2,64,2080]{2,1,0:T(8,128)(2,1)}, bf16[2,64,2080]{2,1,0:T(8,128)(2,1)S(1)}, u32[]{:S(2)}, u32[]{:S(2)}) collective-permute-start(bf16[2,64,2080]{2,1,0:T(8,128)(2,1)} %bitcast.115), channel_id=1, source_target_pairs={{0,4},{2,6},{4,0},{6,2},{1,5},{3,7},{5,1},{7,3},{8,12},{10,14},{12... | collective-permute-start | bytes 1597448 | tf_op jit(solution)/shard_map/ppermute | solution.py:289
  5.7 25.2 %collective-permute-start.3 = (bf16[2,64,2080]{2,1,0:T(8,128)(2,1)}, bf16[2,64,2080]{2,1,0:T(8,128)(2,1)S(1)}, u32[]{:S(2)}, u32[]{:S(2)}) collective-permute-start(bf16[2,64,2080]{2,1,0:T(8,128)(2,1)} %bitcast.116), channel_id=1, source_target_pairs={{0,1},{1,0},{2,3},{3,2},{4,5},{5,4},{6,7},{7,6},{8,9},{9,8},{10,11... | collective-permute-start | bytes 1597448 | tf_op jit(solution)/shard_map/ppermute | solution.py:289
  7.4 39.3 %copy-start.1 = (bf16[1,768,2080]{1,2,0:T(8,128)(2,1)S(1)}, bf16[1,768,2080]{1,2,0:T(8,128)(2,1)}, u32[]{:S(2)}) copy-start(bf16[1,768,2080]{1,2,0:T(8,128)(2,1)} %param.13) | copy-start | bytes 9584644
  8.9 37.8 %copy-start = (bf16[1,2080,768]{2,1,0:T(8,128)(2,1)S(1)}, bf16[1,2080,768]{2,1,0:T(8,128)(2,1)}, u32[]{:S(2)}) copy-start(bf16[1,2080,768]{2,1,0:T(8,128)(2,1)} %param.12) | copy-start | bytes 9584644
  9.0 37.8 %copy-start.13 = (bf16[1,16,8,2080]{3,2,1,0:T(8,128)(2,1)S(1)}, bf16[1,16,8,2080]{3,2,1,0:T(8,128)(2,1)}, u32[]{:S(2)}) copy-start(bf16[1,16,8,2080]{3,2,1,0:T(8,128)(2,1)} %param.11) | copy-start | bytes 1597444
  30.9 20.5 %copy-start.5 = (bf16[2,64,2080]{2,1,0:T(8,128)(2,1)}, bf16[2,64,2080]{2,1,0:T(8,128)(2,1)S(1)}, u32[]{:S(2)}) copy-start(bf16[2,64,2080]{2,1,0:T(8,128)(2,1)S(1)} %collective-permute-done) | copy-start | bytes 1597444
  30.9 44.1 %copy-start.6 = (bf16[2,64,2080]{2,1,0:T(8,128)(2,1)}, bf16[2,64,2080]{2,1,0:T(8,128)(2,1)S(1)}, u32[]{:S(2)}) copy-start(bf16[2,64,2080]{2,1,0:T(8,128)(2,1)S(1)} %collective-permute-done.1) | copy-start | bytes 1597444
  30.9 35.2 %copy-start.9 = (bf16[2,64,2080]{2,1,0:T(8,128)(2,1)}, bf16[2,64,2080]{2,1,0:T(8,128)(2,1)S(1)}, u32[]{:S(2)}) copy-start(bf16[2,64,2080]{2,1,0:T(8,128)(2,1)S(1)} %collective-permute-done.2) | copy-start | bytes 1597444
  31.0 44.1 %copy-start.7 = (bf16[2,64,2080]{2,1,0:T(8,128)(2,1)}, bf16[2,64,2080]{2,1,0:T(8,128)(2,1)S(1)}, u32[]{:S(2)}) copy-start(bf16[2,64,2080]{2,1,0:T(8,128)(2,1)S(1)} %collective-permute-done.3) | copy-start | bytes 1597444
  31.0 20.2 %copy-start.2 = (bf16[128,2080]{1,0:T(8,128)(2,1)}, bf16[128,2080]{1,0:T(8,128)(2,1)S(1)}, u32[]{:S(2)}) copy-start(bf16[128,2080]{1,0:T(8,128)(2,1)S(1)} %after.4.refs_3_.refs_0_) | copy-start | bytes 1597444
  31.0 13.9 %collective-permute-start.5 = (bf16[2,64,2080]{2,1,0:T(8,128)(2,1)S(1)}, bf16[2,64,2080]{2,1,0:T(8,128)(2,1)S(1)}, u32[]{:S(2)}, u32[]{:S(2)}) collective-permute-start(bf16[2,64,2080]{2,1,0:T(8,128)(2,1)S(1)} %bitcast.72), channel_id=1, source_target_pairs={{0,6},{2,0},{4,2},{6,4},{1,7},{3,1},{5,3},{7,5},{8,14},{10,8},{12,... | collective-permute-start | bytes 1597448 | tf_op jit(solution)/shard_map/ppermute | solution.py:289
  31.9 14.7 %collective-permute-start.4 = (bf16[2,64,2080]{2,1,0:T(8,128)(2,1)S(1)}, bf16[2,64,2080]{2,1,0:T(8,128)(2,1)S(1)}, u32[]{:S(2)}, u32[]{:S(2)}) collective-permute-start(bf16[2,64,2080]{2,1,0:T(8,128)(2,1)S(1)} %bitcast.73), channel_id=1, source_target_pairs={{0,2},{2,4},{4,6},{6,0},{1,3},{3,5},{5,7},{7,1},{8,10},{10,12},{12... | collective-permute-start | bytes 1597448 | tf_op jit(solution)/shard_map/ppermute | solution.py:289
  32.5 14.1 %collective-permute-start.11 = (bf16[2,64,2080]{2,1,0:T(8,128)(2,1)S(1)}, bf16[2,64,2080]{2,1,0:T(8,128)(2,1)S(1)}, u32[]{:S(2)}, u32[]{:S(2)}) collective-permute-start(bf16[2,64,2080]{2,1,0:T(8,128)(2,1)S(1)} %bitcast.74), channel_id=1, source_target_pairs={{0,1},{1,0},{2,3},{3,2},{4,5},{5,4},{6,7},{7,6},{8,9},{9,8},{10,11... | collective-permute-start | bytes 1597448 | tf_op jit(solution)/shard_map/ppermute | solution.py:289
  44.9 6.3 %copy-start.14 = (bf16[2,64,2080]{2,1,0:T(8,128)(2,1)}, bf16[2,64,2080]{2,1,0:T(8,128)(2,1)S(1)}, u32[]{:S(2)}) copy-start(bf16[2,64,2080]{2,1,0:T(8,128)(2,1)S(1)} %collective-permute-done.5) | copy-start | bytes 1597444
  44.9 12.9 %collective-permute-start.6 = (bf16[2,64,2080]{2,1,0:T(8,128)(2,1)S(1)}, bf16[2,64,2080]{2,1,0:T(8,128)(2,1)S(1)}, u32[]{:S(2)}, u32[]{:S(2)}) collective-permute-start(bf16[2,64,2080]{2,1,0:T(8,128)(2,1)S(1)} %collective-permute-done.5), channel_id=1, source_target_pairs={{0,6},{2,0},{4,2},{6,4},{1,7},{3,1},{5,3},{7,5},{8,14},{10,8},{12,... | collective-permute-start | bytes 1597448 | tf_op jit(solution)/shard_map/ppermute | solution.py:289
  46.6 4.6 %copy-start.8 = (bf16[2,64,2080]{2,1,0:T(8,128)(2,1)}, bf16[2,64,2080]{2,1,0:T(8,128)(2,1)S(1)}, u32[]{:S(2)}) copy-start(bf16[2,64,2080]{2,1,0:T(8,128)(2,1)S(1)} %collective-permute-done.4) | copy-start | bytes 1597444
  46.6 13.7 %collective-permute-start.12 = (bf16[2,64,2080]{2,1,0:T(8,128)(2,1)S(1)}, bf16[2,64,2080]{2,1,0:T(8,128)(2,1)S(1)}, u32[]{:S(2)}, u32[]{:S(2)}) collective-permute-start(bf16[2,64,2080]{2,1,0:T(8,128)(2,1)S(1)} %bitcast.78), channel_id=1, source_target_pairs={{0,2},{2,4},{4,6},{6,0},{1,3},{3,5},{5,7},{7,1},{8,10},{10,12},{12... | collective-permute-start | bytes 1597448 | tf_op jit(solution)/shard_map/ppermute | solution.py:289
  51.2 15.0 %copy-start.23 = (bf16[384,768]{1,0:T(8,128)(2,1)}, bf16[384,768]{1,0:T(8,128)(2,1)S(1)}, u32[]{:S(2)}) copy-start(bf16[384,768]{1,0:T(8,128)(2,1)S(1)} %get-tuple-element.56.refs_8_) | copy-start | bytes 1769476
  51.2 15.0 %copy-start.24 = (bf16[384,768]{1,0:T(8,128)(2,1)}, bf16[384,768]{1,0:T(8,128)(2,1)S(1)}, u32[]{:S(2)}) copy-start(bf16[384,768]{1,0:T(8,128)(2,1)S(1)} %get-tuple-element.53.refs_8_) | copy-start | bytes 1769476
  51.2 17.1 %copy-start.18 = (bf16[128,2080]{1,0:T(8,128)(2,1)}, bf16[128,2080]{1,0:T(8,128)(2,1)S(1)}, u32[]{:S(2)}) copy-start(bf16[128,2080]{1,0:T(8,128)(2,1)S(1)} %get-tuple-element.32.refs_0_) | copy-start | bytes 1597444
  51.2 14.9 %collective-permute-start.7 = (bf16[1,64,2080]{2,1,0:T(8,128)(2,1)S(1)}, bf16[1,64,2080]{2,1,0:T(8,128)(2,1)S(1)}, u32[]{:S(2)}, u32[]{:S(2)}) collective-permute-start(bf16[1,64,2080]{2,1,0:T(8,128)(2,1)S(1)} %bitcast.148), channel_id=1, source_target_pairs={{0,2},{2,4},{4,6},{6,0},{1,3},{3,5},{5,7},{7,1},{8,10},{10,12},{12... | collective-permute-start | bytes 798728 | tf_op jit(solution)/shard_map/ppermute | solution.py:289
  51.4 19.1 %collective-permute-start.14 = (bf16[2,64,2080]{2,1,0:T(8,128)(2,1)S(1)}, bf16[2,64,2080]{2,1,0:T(8,128)(2,1)S(1)}, u32[]{:S(2)}, u32[]{:S(2)}) collective-permute-start(bf16[2,64,2080]{2,1,0:T(8,128)(2,1)S(1)} %collective-permute-done), channel_id=1, source_target_pairs={{0,1},{1,0},{2,3},{3,2},{4,5},{5,4},{6,7},{7,6},{8,9},{9,8},{10,11... | collective-permute-start | bytes 1597448 | tf_op jit(solution)/shard_map/ppermute | solution.py:289
  51.4 23.6 %collective-permute-start.15 = (bf16[2,64,2080]{2,1,0:T(8,128)(2,1)S(1)}, bf16[2,64,2080]{2,1,0:T(8,128)(2,1)S(1)}, u32[]{:S(2)}, u32[]{:S(2)}) collective-permute-start(bf16[2,64,2080]{2,1,0:T(8,128)(2,1)S(1)} %collective-permute-done.2), channel_id=1, source_target_pairs={{0,1},{1,0},{2,3},{3,2},{4,5},{5,4},{6,7},{7,6},{8,9},{9,8},{10,11... | collective-permute-start | bytes 1597448 | tf_op jit(solution)/shard_map/ppermute | solution.py:289
  57.8 10.6 %copy-start.11 = (bf16[2,64,2080]{2,1,0:T(8,128)(2,1)}, bf16[2,64,2080]{2,1,0:T(8,128)(2,1)S(1)}, u32[]{:S(2)}) copy-start(bf16[2,64,2080]{2,1,0:T(8,128)(2,1)S(1)} %collective-permute-done.6) | copy-start | bytes 1597444
  57.8 8.4 %collective-permute-start.8 = (bf16[1,64,2080]{2,1,0:T(8,128)(2,1)S(1)}, bf16[1,64,2080]{2,1,0:T(8,128)(2,1)S(1)}, u32[]{:S(2)}, u32[]{:S(2)}) collective-permute-start(bf16[1,64,2080]{2,1,0:T(8,128)(2,1)S(1)} %bitcast.144), channel_id=1, source_target_pairs={{0,6},{2,0},{4,2},{6,4},{1,7},{3,1},{5,3},{7,5},{8,14},{10,8},{12,... | collective-permute-start | bytes 798728 | tf_op jit(solution)/shard_map/ppermute | solution.py:289
  60.4 29.2 %copy-start.3 = (bf16[128,2080]{1,0:T(8,128)(2,1)}, bf16[128,2080]{1,0:T(8,128)(2,1)S(1)}, u32[]{:S(2)}) copy-start(bf16[128,2080]{1,0:T(8,128)(2,1)S(1)} %after.6.refs_1_.refs_2_.refs_5_) | copy-start | bytes 1597444
  60.4 29.2 %copy-start.4 = (bf16[128,2080]{1,0:T(8,128)(2,1)}, bf16[128,2080]{1,0:T(8,128)(2,1)S(1)}, u32[]{:S(2)}) copy-start(bf16[128,2080]{1,0:T(8,128)(2,1)S(1)} %after.7.refs_1_.refs_4_) | copy-start | bytes 1597444
  60.4 17.7 %collective-permute-start.13 = (bf16[2,64,2080]{2,1,0:T(8,128)(2,1)S(1)}, bf16[2,64,2080]{2,1,0:T(8,128)(2,1)S(1)}, u32[]{:S(2)}, u32[]{:S(2)}) collective-permute-start(bf16[2,64,2080]{2,1,0:T(8,128)(2,1)S(1)} %bitcast.76), channel_id=1, source_target_pairs={{0,2},{2,4},{4,6},{6,0},{1,3},{3,5},{5,7},{7,1},{8,10},{10,12},{12... | collective-permute-start | bytes 1597448 | tf_op jit(solution)/shard_map/ppermute | solution.py:289
  66.1 11.9 %collective-permute-start.16 = (bf16[2,64,2080]{2,1,0:T(8,128)(2,1)S(1)}, bf16[2,64,2080]{2,1,0:T(8,128)(2,1)S(1)}, u32[]{:S(2)}, u32[]{:S(2)}) collective-permute-start(bf16[2,64,2080]{2,1,0:T(8,128)(2,1)S(1)} %bitcast.79), channel_id=1, source_target_pairs={{0,6},{2,0},{4,2},{6,4},{1,7},{3,1},{5,3},{7,5},{8,14},{10,8},{12,... | collective-permute-start | bytes 1597448 | tf_op jit(solution)/shard_map/ppermute | solution.py:289
  68.3 0.7 copy-start.28
  69.0 10.8 %copy-start.27 = (bf16[128,768]{1,0:T(8,128)(2,1)}, bf16[128,768]{1,0:T(8,128)(2,1)S(1)}, u32[]{:S(2)}) copy-start(bf16[128,768]{1,0:T(8,128)(2,1)S(1)} %get-tuple-element.57.refs_9_) | copy-start | bytes 589828
  69.0 15.0 %collective-permute-start.9 = (bf16[1,64,2080]{2,1,0:T(8,128)(2,1)S(1)}, bf16[1,64,2080]{2,1,0:T(8,128)(2,1)S(1)}, u32[]{:S(2)}, u32[]{:S(2)}) collective-permute-start(bf16[1,64,2080]{2,1,0:T(8,128)(2,1)S(1)} %bitcast.147), channel_id=1, source_target_pairs={{0,2},{2,4},{4,6},{6,0},{1,3},{3,5},{5,7},{7,1},{8,10},{10,12},{12... | collective-permute-start | bytes 798728 | tf_op jit(solution)/shard_map/ppermute | solution.py:289
  70.5 7.6 %copy-start.15 = (bf16[2,64,2080]{2,1,0:T(8,128)(2,1)}, bf16[2,64,2080]{2,1,0:T(8,128)(2,1)S(1)}, u32[]{:S(2)}) copy-start(bf16[2,64,2080]{2,1,0:T(8,128)(2,1)S(1)} %collective-permute-done.14) | copy-start | bytes 1597444
  70.5 13.6 %collective-permute-start.10 = (bf16[1,64,2080]{2,1,0:T(8,128)(2,1)S(1)}, bf16[1,64,2080]{2,1,0:T(8,128)(2,1)S(1)}, u32[]{:S(2)}, u32[]{:S(2)}) collective-permute-start(bf16[1,64,2080]{2,1,0:T(8,128)(2,1)S(1)} %bitcast.145), channel_id=1, source_target_pairs={{0,6},{2,0},{4,2},{6,4},{1,7},{3,1},{5,3},{7,5},{8,14},{10,8},{12,... | collective-permute-start | bytes 798728 | tf_op jit(solution)/shard_map/ppermute | solution.py:289
  75.0 4.8 %copy-start.16 = (bf16[2,64,2080]{2,1,0:T(8,128)(2,1)}, bf16[2,64,2080]{2,1,0:T(8,128)(2,1)S(1)}, u32[]{:S(2)}) copy-start(bf16[2,64,2080]{2,1,0:T(8,128)(2,1)S(1)} %collective-permute-done.15) | copy-start | bytes 1597444
  75.0 14.6 %collective-permute-start.19 = (bf16[2,64,2080]{2,1,0:T(8,128)(2,1)S(1)}, bf16[2,64,2080]{2,1,0:T(8,128)(2,1)S(1)}, u32[]{:S(2)}, u32[]{:S(2)}) collective-permute-start(bf16[2,64,2080]{2,1,0:T(8,128)(2,1)S(1)} %collective-permute-done.1), channel_id=1, source_target_pairs={{0,1},{1,0},{2,3},{3,2},{4,5},{5,4},{6,7},{7,6},{8,9},{9,8},{10,11... | collective-permute-start | bytes 1597448 | tf_op jit(solution)/shard_map/ppermute | solution.py:289
  76.8 3.0 %copy-start.26 = (bf16[256,768]{1,0:T(8,128)(2,1)}, bf16[256,768]{1,0:T(8,128)(2,1)S(1)}, u32[]{:S(2)}) copy-start(bf16[256,768]{1,0:T(8,128)(2,1)S(1)} %get-tuple-element.58.refs_10_) | copy-start | bytes 1179652
  76.8 3.0 %copy-start.29 = (bf16[128,768]{1,0:T(8,128)(2,1)}, bf16[128,768]{1,0:T(8,128)(2,1)S(1)}, u32[]{:S(2)}) copy-start(bf16[128,768]{1,0:T(8,128)(2,1)S(1)} %get-tuple-element.60.refs_12_) | copy-start | bytes 589828
  78.1 1.8 %copy-start.20 = (bf16[2,64,2080]{2,1,0:T(8,128)(2,1)}, bf16[2,64,2080]{2,1,0:T(8,128)(2,1)S(1)}, u32[]{:S(2)}) copy-start(bf16[2,64,2080]{2,1,0:T(8,128)(2,1)S(1)} %collective-permute-done.13) | copy-start | bytes 1597444
  78.1 11.5 %copy-start.10 = (bf16[2,64,2080]{2,1,0:T(8,128)(2,1)}, bf16[2,64,2080]{2,1,0:T(8,128)(2,1)S(1)}, u32[]{:S(2)}) copy-start(bf16[2,64,2080]{2,1,0:T(8,128)(2,1)S(1)} %collective-permute-done.16) | copy-start | bytes 1597444
  79.9 14.6 %copy-start.12 = (bf16[128,768]{1,0:T(8,128)(2,1)}, bf16[128,768]{1,0:T(8,128)(2,1)S(1)}, u32[]{:S(2)}) copy-start(bf16[128,768]{1,0:T(8,128)(2,1)S(1)} %get-tuple-element.40.refs_4_.refs_7_.refs_11_) | copy-start | bytes 589828
  84.2 10.4 %collective-permute-start.17 = (bf16[1,64,2080]{2,1,0:T(8,128)(2,1)S(1)}, bf16[1,64,2080]{2,1,0:T(8,128)(2,1)S(1)}, u32[]{:S(2)}, u32[]{:S(2)}) collective-permute-start(bf16[1,64,2080]{2,1,0:T(8,128)(2,1)S(1)} %bitcast.146), channel_id=1, source_target_pairs={{0,2},{2,4},{4,6},{6,0},{1,3},{3,5},{5,7},{7,1},{8,10},{10,12},{12... | collective-permute-start | bytes 798728 | tf_op jit(solution)/shard_map/ppermute | solution.py:289
  84.3 13.0 %collective-permute-start.18 = (bf16[1,64,2080]{2,1,0:T(8,128)(2,1)S(1)}, bf16[1,64,2080]{2,1,0:T(8,128)(2,1)S(1)}, u32[]{:S(2)}, u32[]{:S(2)}) collective-permute-start(bf16[1,64,2080]{2,1,0:T(8,128)(2,1)S(1)} %bitcast.143), channel_id=1, source_target_pairs={{0,6},{2,0},{4,2},{6,4},{1,7},{3,1},{5,3},{7,5},{8,14},{10,8},{12,... | collective-permute-start | bytes 798728 | tf_op jit(solution)/shard_map/ppermute | solution.py:289
  86.9 10.4 %collective-permute-start.20 = (bf16[1,64,2080]{2,1,0:T(8,128)(2,1)S(1)}, bf16[1,64,2080]{2,1,0:T(8,128)(2,1)S(1)}, u32[]{:S(2)}, u32[]{:S(2)}) collective-permute-start(bf16[1,64,2080]{2,1,0:T(8,128)(2,1)S(1)} %bitcast.142), channel_id=1, source_target_pairs={{0,2},{2,4},{4,6},{6,0},{1,3},{3,5},{5,7},{7,1},{8,10},{10,12},{12... | collective-permute-start | bytes 798728 | tf_op jit(solution)/shard_map/ppermute | solution.py:289
  86.9 10.4 %collective-permute-start.21 = (bf16[1,64,2080]{2,1,0:T(8,128)(2,1)S(1)}, bf16[1,64,2080]{2,1,0:T(8,128)(2,1)S(1)}, u32[]{:S(2)}, u32[]{:S(2)}) collective-permute-start(bf16[1,64,2080]{2,1,0:T(8,128)(2,1)S(1)} %bitcast.141), channel_id=1, source_target_pairs={{0,6},{2,0},{4,2},{6,4},{1,7},{3,1},{5,3},{7,5},{8,14},{10,8},{12,... | collective-permute-start | bytes 798728 | tf_op jit(solution)/shard_map/ppermute | solution.py:289
  89.6 4.9 %copy-start.17 = (bf16[2,64,2080]{2,1,0:T(8,128)(2,1)}, bf16[2,64,2080]{2,1,0:T(8,128)(2,1)S(1)}, u32[]{:S(2)}) copy-start(bf16[2,64,2080]{2,1,0:T(8,128)(2,1)S(1)} %collective-permute-done.19) | copy-start | bytes 1597444
  89.6 11.2 %copy-start.19 = (bf16[128,2080]{1,0:T(8,128)(2,1)S(1)}, bf16[128,2080]{1,0:T(8,128)(2,1)}, u32[]{:S(2)}) copy-start(bf16[128,2080]{1,0:T(8,128)(2,1)} %copy-done.18) | copy-start | bytes 1597444
  94.5 3.6 %copy-start.25 = (bf16[384,768]{1,0:T(8,128)(2,1)}, bf16[384,768]{1,0:T(8,128)(2,1)S(1)}, u32[]{:S(2)}) copy-start(bf16[384,768]{1,0:T(8,128)(2,1)S(1)} %get-tuple-element.55.refs_10_) | copy-start | bytes 1769476
  94.5 3.6 %copy-start.30 = (bf16[128,768]{1,0:T(8,128)(2,1)}, bf16[128,768]{1,0:T(8,128)(2,1)S(1)}, u32[]{:S(2)}) copy-start(bf16[128,768]{1,0:T(8,128)(2,1)S(1)} %get-tuple-element.59.refs_11_) | copy-start | bytes 589828
  94.5 8.3 %collective-permute-start.23 = (bf16[1,64,2080]{2,1,0:T(8,128)(2,1)}, bf16[1,64,2080]{2,1,0:T(8,128)(2,1)S(1)}, u32[]{:S(2)}, u32[]{:S(2)}) collective-permute-start(bf16[1,64,2080]{2,1,0:T(8,128)(2,1)} %bitcast.49), channel_id=1, source_target_pairs={{0,2},{2,4},{4,6},{6,0},{1,3},{3,5},{5,7},{7,1},{8,10},{10,12},{12... | collective-permute-start | bytes 798728 | tf_op jit(solution)/shard_map/ppermute | solution.py:289
  94.6 8.2 %collective-permute-start.24 = (bf16[1,64,2080]{2,1,0:T(8,128)(2,1)}, bf16[1,64,2080]{2,1,0:T(8,128)(2,1)S(1)}, u32[]{:S(2)}, u32[]{:S(2)}) collective-permute-start(bf16[1,64,2080]{2,1,0:T(8,128)(2,1)} %bitcast.51), channel_id=1, source_target_pairs={{0,6},{2,0},{4,2},{6,4},{1,7},{3,1},{5,3},{7,5},{8,14},{10,8},{12,... | collective-permute-start | bytes 798728 | tf_op jit(solution)/shard_map/ppermute | solution.py:289
  98.2 10.5 %collective-permute-start.22 = (bf16[1,64,2080]{2,1,0:T(8,128)(2,1)}, bf16[1,64,2080]{2,1,0:T(8,128)(2,1)S(1)}, u32[]{:S(2)}, u32[]{:S(2)}) collective-permute-start(bf16[1,64,2080]{2,1,0:T(8,128)(2,1)} %bitcast.47), channel_id=1, source_target_pairs={{0,2},{2,4},{4,6},{6,0},{1,3},{3,5},{5,7},{7,1},{8,10},{10,12},{12... | collective-permute-start | bytes 798728 | tf_op jit(solution)/shard_map/ppermute | solution.py:289
  98.2 10.5 %collective-permute-start.25 = (bf16[1,64,2080]{2,1,0:T(8,128)(2,1)}, bf16[1,64,2080]{2,1,0:T(8,128)(2,1)S(1)}, u32[]{:S(2)}, u32[]{:S(2)}) collective-permute-start(bf16[1,64,2080]{2,1,0:T(8,128)(2,1)} %bitcast.53), channel_id=1, source_target_pairs={{0,6},{2,0},{4,2},{6,4},{1,7},{3,1},{5,3},{7,5},{8,14},{10,8},{12,... | collective-permute-start | bytes 798728 | tf_op jit(solution)/shard_map/ppermute | solution.py:289
  110.0 27.2 %all-to-all-start.1 = ((bf16[32,8,2080]{2,1,0:T(8,128)(2,1)}), bf16[32,8,2080]{2,1,0:T(8,128)(2,1)S(1)}, u32[]{:S(2)}, u32[]{:S(2)}) async-start(bf16[32,8,2080]{2,1,0:T(8,128)(2,1)} %bitcast.55), calls=%async_computation.1 | async-start | bytes 2228224 | tf_op jit(solution)/shard_map/all_to_all | solution.py:310
  127.3 9.8 %copy-start.21 = (s32[128]{0:T(128)S(1)}, s32[128]{0:T(128)}, u32[]{:S(2)}) copy-start(s32[128]{0:T(128)} %param.8) | copy-start | bytes 1540
  127.4 9.8 %copy-start.22 = (s32[128]{0:T(128)S(1)}, s32[128]{0:T(128)}, u32[]{:S(2)}) copy-start(s32[128]{0:T(128)} %param.9) | copy-start | bytes 1540
